TPU v7x, 32 devices: a whole 2x2x4 slice. The times are simulated.
32 devices in a mesh: dp: 4 (over z), expert: 8 (over y, x, core).
Axes of the slice: x: 2, y: 2, z: 4, core: 2. Of those that a mesh axis runs over, the one named last changes fastest.
Arguments:
- tokens: bfloat16 [4096, 3584], P(('dp', 'expert')), may hold values from -6 to 6
- expert_ids: int32 [4096, 1], P(('dp', 'expert')), may hold values from 0 to 7; in each aligned block of 128 rows (0 to 127, 128 to 255, ...) at most 32 rows name the same one
- gates: bfloat16 [4096], P(('dp', 'expert')), may hold values from 0.19921875 to 1
- cotangent: bfloat16 [4096, 1024], P(('dp', 'expert')), may hold values from -6 to 6
- weights: bfloat16 [8, 3584, 1024], P('expert'), may hold values from -0.09375 to 0.09375
Outputs:
- hidden: bfloat16 [4096, 1024], P(('dp', 'expert'))
- grad: float32 [8, 3584, 1024], P('expert', 'dp')
Inputs may be any that keep to these rules, and one draw needn't show every extreme that they name: `expert_ids`: among the 128 tokens of one device at most 32 name one expert; some device and expert reach 32 in every draw.
All inputs are finite; a program needn't handle non-finite values.
Results may differ from a plain program's by a relative error of at most 0.0029.
Values may be sent and summed in bfloat16 or wider, within the bound.
No kernel may reach another device: no remote copies, remote signals or barrier semaphores. Data moves between devices by JAX's collectives and lax.ppermute only.
A program may use at most 64 MiB of HBM per device.

v0:
```python
import jax
import jax.numpy as jnp
from jax import lax
from jax.sharding import PartitionSpec as P


def on_device(tokens, expert_ids, gates, cotangent, weights):
    experts = lax.axis_size("expert")
    members = lax.axis_size("dp")
    tok_count = tokens.shape[0]
    slots = max(2, 2 * tok_count // experts)
    ids = expert_ids[:, 0]
    onehot = (ids[:, None] == jnp.arange(experts, dtype=jnp.int32)[None, :]).astype(jnp.int32)
    before = jnp.cumsum(onehot, axis=0) - onehot
    rank = jnp.sum(before * onehot, axis=1)
    slot_of = ids * slots + rank
    placing = (jnp.arange(experts * slots, dtype=jnp.int32)[:, None] == slot_of[None, :]).astype(
        jnp.bfloat16
    )
    width = tokens.shape[1]
    inner = cotangent.shape[1]
    x_slots = (
        jnp.dot(placing, tokens, preferred_element_type=jnp.float32)
        .astype(jnp.bfloat16)
        .reshape(experts, slots, width)
    )
    c_slots = (
        jnp.dot(placing, cotangent, preferred_element_type=jnp.float32)
        .astype(jnp.bfloat16)
        .reshape(experts, slots, inner)
    )
    g_slots = (
        jnp.dot(placing, gates[:, None], preferred_element_type=jnp.float32)
        .astype(jnp.bfloat16)
        .reshape(experts, slots)
    )
    rows, cots, gvals = (
        lax.all_to_all(x_slots, "expert", split_axis=0, concat_axis=0, tiled=True),
        lax.all_to_all(c_slots, "expert", split_axis=0, concat_axis=0, tiled=True),
        lax.all_to_all(g_slots, "expert", split_axis=0, concat_axis=0, tiled=True),
    )
    row_count = experts * slots
    rows = rows.reshape(row_count, width)
    cots = cots.reshape(row_count, inner).astype(jnp.float32)
    gate = gvals.reshape(row_count, 1).astype(jnp.float32)
    pre = jnp.dot(rows, weights[0], preferred_element_type=jnp.float32)
    sig = jax.nn.sigmoid(pre)
    hval = (gate * pre * sig).astype(jnp.bfloat16).reshape(experts, slots, inner)
    returned = lax.all_to_all(hval, "expert", split_axis=0, concat_axis=0, tiled=True).reshape(
        row_count, inner
    )
    hidden = lax.dot_general(
        placing, returned, (((0,), (0,)), ((), ())), preferred_element_type=jnp.float32
    ).astype(jnp.bfloat16)
    dpre = (cots * gate * sig * (1.0 + pre * (1.0 - sig))).astype(jnp.bfloat16)
    share = width // members
    sliced = lax.all_to_all(rows, "dp", split_axis=1, concat_axis=0, tiled=True)
    gathered = lax.all_gather(dpre, "dp", axis=0, tiled=True)

    def add_member(member, total):
        left = lax.dynamic_slice_in_dim(sliced, member * row_count, row_count, 0)
        right = lax.dynamic_slice_in_dim(gathered, member * row_count, row_count, 0)
        part = lax.dot_general(
            left, right, (((0,), (0,)), ((), ())), preferred_element_type=jnp.float32
        )
        return total + part

    grad = lax.fori_loop(0, members, add_member, jnp.zeros((share, inner), jnp.float32))
    return (hidden, grad[None])


def solution(mesh):
    return jax.shard_map(
        on_device,
        mesh=mesh,
        in_specs=(
            P(("dp", "expert"), None),
            P(("dp", "expert"), None),
            P(("dp", "expert")),
            P(("dp", "expert"), None),
            P("expert", None, None),
        ),
        out_specs=(P(("dp", "expert"), None), P("expert", "dp", None)),
        check_vma=False,
    )
```

profile of v0, /device:TPU:0, one launch (start us, length us, event | category | flops | bytes accessed | tf_op | source)
XLA Modules:
  0.0 184.5 jit_solution(12494674954646142568)
XLA Ops:
  7.2 0.0 copy-start
  7.2 0.8 fusion.13
  8.0 0.2 reduce_window_sum.11
  8.2 0.8 select_reduce_fusion
  9.0 0.7 multiply_add_fusion
  9.7 0.8 fusion.8
  10.5 0.7 all_to_all.38
  11.2 5.2 %all-to-all-start = ((bf16[8,1,32]{2,1,0:T(2,128)(2,1)}), bf16[8,1,32]{2,1,0:T(2,128)(2,1)S(1)}, u32[]{:S(2)}, u32[]{:S(2)}) async-start(bf16[8,1,32]{2,1,0:T(2,128)(2,1)} %all_to_all.38), calls=%async_computation | async-start | bytes 8192 | tf_op jit(solution)/shard_map/all_to_all | solution.py:40
  16.3 2.0 %convolution_convert_fusion.1 = bf16[256,1024]{1,0:T(8,128)(2,1)} fusion(bf16[128,1024]{1,0:T(8,128)(2,1)} %param.10, s32[128]{0:T(128)S(1)} %multiply_add_fusion), kind=kOutput, calls=%fused_computation.7 | convolution fusion | flops 67403776 | bytes 786944 | tf_op jit(solution)/shard_map/dot_general | solution.py:28
  18.4 2.6 %all-to-all-done = bf16[8,1,32]{2,1,0:T(2,128)(2,1)S(1)} async-done(((bf16[8,1,32]{2,1,0:T(2,128)(2,1)}), bf16[8,1,32]{2,1,0:T(2,128)(2,1)S(1)}, u32[]{:S(2)}, u32[]{:S(2)}) %all-to-all-start) | async-done | bytes 544 | tf_op jit(solution)/shard_map/all_to_all | solution.py:40
  20.9 3.5 %all-to-all-start.4 = ((bf16[8,32,1024]{2,1,0:T(8,128)(2,1)}), bf16[8,32,1024]{2,1,0:T(8,128)(2,1)S(1)}, u32[]{:S(2)}, u32[]{:S(2)}) async-start(bf16[8,32,1024]{2,1,0:T(8,128)(2,1)} %bitcast.10), calls=%async_computation.4 | async-start | bytes 1048576 | tf_op jit(solution)/shard_map/all_to_all | solution.py:39
  24.4 0.0 copy-done
  24.4 1.9 %convolution_convert_fusion = bf16[256,3584]{1,0:T(8,128)(2,1)} fusion(bf16[128,3584]{1,0:T(8,128)(2,1)S(1)} %copy-done, s32[128]{0:T(128)S(1)} %multiply_add_fusion), kind=kOutput, calls=%fused_computation.6 | convolution fusion | flops 235831296 | bytes 2753024 | tf_op jit(solution)/shard_map/dot_general | solution.py:23
  26.3 7.8 %all-to-all-done.4 = bf16[8,32,1024]{2,1,0:T(8,128)(2,1)S(1)} async-done(((bf16[8,32,1024]{2,1,0:T(8,128)(2,1)}), bf16[8,32,1024]{2,1,0:T(8,128)(2,1)S(1)}, u32[]{:S(2)}, u32[]{:S(2)}) %all-to-all-start.4) | async-done | bytes 524320 | tf_op jit(solution)/shard_map/all_to_all | solution.py:39
  34.1 3.6 %all-to-all-start.1 = ((bf16[8,32,3584]{2,1,0:T(8,128)(2,1)}), bf16[8,32,3584]{2,1,0:T(8,128)(2,1)S(1)}, u32[]{:S(2)}, u32[]{:S(2)}) async-start(bf16[8,32,3584]{2,1,0:T(8,128)(2,1)} %bitcast.30), calls=%async_computation.1 | async-start | bytes 3670016 | tf_op jit(solution)/shard_map/all_to_all | solution.py:38
  37.7 0.1 reshape.59
  37.8 23.7 %all-to-all-done.1 = bf16[8,32,3584]{2,1,0:T(8,128)(2,1)S(1)} async-done(((bf16[8,32,3584]{2,1,0:T(8,128)(2,1)}), bf16[8,32,3584]{2,1,0:T(8,128)(2,1)S(1)}, u32[]{:S(2)}, u32[]{:S(2)}) %all-to-all-start.1) | async-done | bytes 1835040 | tf_op jit(solution)/shard_map/all_to_all | solution.py:38
  61.5 6.5 %fusion.7 = (bf16[256,1024]{1,0:T(8,128)(2,1)}, bf16[256,1024]{1,0:T(8,128)(2,1)}) fusion(bf16[8,32,1024]{2,1,0:T(8,128)(2,1)S(1)} %all-to-all-done.4, f32[256]{0:T(256)S(1)} %reshape.59, bf16[256,3584]{1,0:T(8,128)(2,1)S(1)} %bitcast.29, bf16[1,3584,1024]{2,1,0:T(8,128)(2,1)} %param.11), kind=kOutput, calls=%fused_computation.12 | convolution fusion | flops 1882718208 | bytes 10748928 | tf_op jit(solution)/shard_map/dot_general | solution.py:46
  68.0 3.5 %all-to-all-start.2 = ((bf16[8,32,1024]{2,1,0:T(8,128)(2,1)}), bf16[8,32,1024]{2,1,0:T(8,128)(2,1)S(1)}, u32[]{:S(2)}, u32[]{:S(2)}) async-start(bf16[8,32,1024]{2,1,0:T(8,128)(2,1)} %bitcast.32), calls=%async_computation.2 | async-start | bytes 1048576 | tf_op jit(solution)/shard_map/all_to_all | solution.py:49
  71.5 0.0 all-gather.2.cloned.1.call-start
  71.5 0.7 all-gather.2.cloned.1.call-update
  72.2 1.5 all_to_all.33
  73.7 2.9 %copy.10 = bf16[256,4,896]{2,0,1:T(8,128)(2,1)} copy(bf16[256,4,896]{2,1,0:T(4,128)(2,1)} %all_to_all.33) | data formatting | bytes 3670016 | tf_op jit(solution)/shard_map/all_to_all | solution.py:57
  76.6 4.5 %all-to-all-done.2 = bf16[8,32,1024]{2,1,0:T(8,128)(2,1)S(1)} async-done(((bf16[8,32,1024]{2,1,0:T(8,128)(2,1)}), bf16[8,32,1024]{2,1,0:T(8,128)(2,1)S(1)}, u32[]{:S(2)}, u32[]{:S(2)}) %all-to-all-start.2) | async-done | bytes 524320 | tf_op jit(solution)/shard_map/all_to_all | solution.py:49
  81.2 4.9 %all-to-all-start.3 = ((bf16[256,4,896]{2,0,1:T(8,128)(2,1)}), bf16[256,4,896]{2,0,1:T(8,128)(2,1)S(1)}, u32[]{:S(2)}, u32[]{:S(2)}) async-start(bf16[256,4,896]{2,0,1:T(8,128)(2,1)} %copy.10), calls=%async_computation.3 | async-start | bytes 3670016 | tf_op jit(solution)/shard_map/all_to_all | solution.py:57
  86.0 1.0 convolution_convert_fusion.2
  87.0 73.0 %all-to-all-done.3 = bf16[256,4,896]{2,0,1:T(8,128)(2,1)S(1)} async-done(((bf16[256,4,896]{2,0,1:T(8,128)(2,1)}), bf16[256,4,896]{2,0,1:T(8,128)(2,1)S(1)}, u32[]{:S(2)}, u32[]{:S(2)}) %all-to-all-start.3) | async-done | bytes 1835040 | tf_op jit(solution)/shard_map/all_to_all | solution.py:57
  160.0 0.0 all-gather.2.cloned.1.call-done
  160.0 17.7 %while.14 = (s32[]{:T(128)}, f32[896,1024]{1,0:T(8,128)}, bf16[1024,896]{1,0:T(8,128)(2,1)S(1)}, bf16[1024,1024]{1,0:T(8,128)(2,1)}, s32[]{:T(128)}, /*index=5*/s32[]{:T(128)}, s32[]{:T(128)}, s32[]{:T(128)}) while((s32[]{:T(128)}, f32[896,1024]{1,0:T(8,128)}, bf16[1024,896]{1,0:T(8,128)(2,1)S(1)}, bf16[1024,1024]{1,0:T(8,128)(2,1)}, ...), condition=%wide.region_3.4_spmd.clone, body=%wide.region_2.3_spmd.clone.sunk | while | flops 471597056 | bytes 8324756 | solution.py:68
  160.0 3.6 %select_add_fusion.2 = f32[896,1024]{1,0:T(8,128)} fusion(f32[896,1024]{1,0:T(8,128)} %get-tuple-element.141, pred[]{:T(512)S(6)} %compare.3, bf16[1024,1024]{1,0:T(8,128)(2,1)} %get-tuple-element.151, s32[]{:T(128)S(6)} %select_n.10, bf16[1024,896]{1,0:T(8,128)(2,1)S(1)} %get-tuple-element.150), kind=kOutput, calls=%fused_computation.clone.1 | convolution fusion | flops 471597056 | bytes 8324608 | tf_op jit(solution)/shard_map/while/body/eval_jaxpr/dot_general | solution.py:63
  163.5 4.7 %select_add_fusion.2 = f32[896,1024]{1,0:T(8,128)} fusion(f32[896,1024]{1,0:T(8,128)} %get-tuple-element.141, pred[]{:T(512)S(6)} %compare.3, bf16[1024,1024]{1,0:T(8,128)(2,1)} %get-tuple-element.151, s32[]{:T(128)S(6)} %select_n.10, bf16[1024,896]{1,0:T(8,128)(2,1)S(1)} %get-tuple-element.150), kind=kOutput, calls=%fused_computation.clone.1 | convolution fusion | flops 471597056 | bytes 8324608 | tf_op jit(solution)/shard_map/while/body/eval_jaxpr/dot_general | solution.py:63
  168.3 4.7 %select_add_fusion.2 = f32[896,1024]{1,0:T(8,128)} fusion(f32[896,1024]{1,0:T(8,128)} %get-tuple-element.141, pred[]{:T(512)S(6)} %compare.3, bf16[1024,1024]{1,0:T(8,128)(2,1)} %get-tuple-element.151, s32[]{:T(128)S(6)} %select_n.10, bf16[1024,896]{1,0:T(8,128)(2,1)S(1)} %get-tuple-element.150), kind=kOutput, calls=%fused_computation.clone.1 | convolution fusion | flops 471597056 | bytes 8324608 | tf_op jit(solution)/shard_map/while/body/eval_jaxpr/dot_general | solution.py:63
  173.0 4.7 %select_add_fusion.2 = f32[896,1024]{1,0:T(8,128)} fusion(f32[896,1024]{1,0:T(8,128)} %get-tuple-element.141, pred[]{:T(512)S(6)} %compare.3, bf16[1024,1024]{1,0:T(8,128)(2,1)} %get-tuple-element.151, s32[]{:T(128)S(6)} %select_n.10, bf16[1024,896]{1,0:T(8,128)(2,1)S(1)} %get-tuple-element.150), kind=kOutput, calls=%fused_computation.clone.1 | convolution fusion | flops 471597056 | bytes 8324608 | tf_op jit(solution)/shard_map/while/body/eval_jaxpr/dot_general | solution.py:63
  (3 shorter events, 0.0 us)
Async XLA Ops:
  7.2 17.3 %copy-start = (bf16[128,3584]{1,0:T(8,128)(2,1)S(1)}, bf16[128,3584]{1,0:T(8,128)(2,1)}, u32[]{:S(2)}) copy-start(bf16[128,3584]{1,0:T(8,128)(2,1)} %param.7) | copy-start | bytes 2752516
  11.2 9.8 %all-to-all-start = ((bf16[8,1,32]{2,1,0:T(2,128)(2,1)}), bf16[8,1,32]{2,1,0:T(2,128)(2,1)S(1)}, u32[]{:S(2)}, u32[]{:S(2)}) async-start(bf16[8,1,32]{2,1,0:T(2,128)(2,1)} %all_to_all.38), calls=%async_computation | async-start | bytes 8192 | tf_op jit(solution)/shard_map/all_to_all | solution.py:40
  20.9 13.2 %all-to-all-start.4 = ((bf16[8,32,1024]{2,1,0:T(8,128)(2,1)}), bf16[8,32,1024]{2,1,0:T(8,128)(2,1)S(1)}, u32[]{:S(2)}, u32[]{:S(2)}) async-start(bf16[8,32,1024]{2,1,0:T(8,128)(2,1)} %bitcast.10), calls=%async_computation.4 | async-start | bytes 1048576 | tf_op jit(solution)/shard_map/all_to_all | solution.py:39
  34.1 27.4 %all-to-all-start.1 = ((bf16[8,32,3584]{2,1,0:T(8,128)(2,1)}), bf16[8,32,3584]{2,1,0:T(8,128)(2,1)S(1)}, u32[]{:S(2)}, u32[]{:S(2)}) async-start(bf16[8,32,3584]{2,1,0:T(8,128)(2,1)} %bitcast.30), calls=%async_computation.1 | async-start | bytes 3670016 | tf_op jit(solution)/shard_map/all_to_all | solution.py:38
  68.0 13.2 %all-to-all-start.2 = ((bf16[8,32,1024]{2,1,0:T(8,128)(2,1)}), bf16[8,32,1024]{2,1,0:T(8,128)(2,1)S(1)}, u32[]{:S(2)}, u32[]{:S(2)}) async-start(bf16[8,32,1024]{2,1,0:T(8,128)(2,1)} %bitcast.32), calls=%async_computation.2 | async-start | bytes 1048576 | tf_op jit(solution)/shard_map/all_to_all | solution.py:49
  71.5 88.5 %all-gather.2.cloned.1.call-start = ((), (), s32[]{:S(2)}) async-start(), calls=%async_computation.5 | async-start | bytes 2621440 | tf_op jit(solution)/shard_map/all_gather | solution.py:58
  81.2 78.8 %all-to-all-start.3 = ((bf16[256,4,896]{2,0,1:T(8,128)(2,1)}), bf16[256,4,896]{2,0,1:T(8,128)(2,1)S(1)}, u32[]{:S(2)}, u32[]{:S(2)}) async-start(bf16[256,4,896]{2,0,1:T(8,128)(2,1)} %copy.10), calls=%async_computation.3 | async-start | bytes 3670016 | tf_op jit(solution)/shard_map/all_to_all | solution.py:57
Sparse Core Ops, SparseCore 0:
  73.9 83.4 all-gather.1
where the time goes:
time: 185 us
  waiting for transfers between devices  112 us (61%)
  matrix products  29.9 us (16%)
  starting transfers between devices  20.7 us (11%)
  between operations  14.1 us (8%)
  local copies, waits for them, and re-layouts  5.17 us (3%)
  other arithmetic  2.51 us (1%)
    all_to_all x1, waiting for transfers between devices, on_device(): sliced = lax.all_to_all(rows, 'dp', split_axis=1, concat_axis=0, tiled=True)  73 us
    all_to_all x1, waiting for transfers between devices, on_device(): lax.all_to_all(x_slots, 'expert', split_axis=0, concat_axis=0, tiled=True)  23.7 us
    dot_general x4, matrix products, add_member(): lax.dot_general(left, right, (((0,), (0,)), ((), ())), preferred_element_...  17.7 us
    all_to_all x1, waiting for transfers between devices, on_device(): lax.all_to_all(c_slots, 'expert', split_axis=0, concat_axis=0, tiled=True)  7.81 us
    dot_general x1, matrix products, on_device(): pre = jnp.dot(rows, weights[0], preferred_element_type=jnp.float32)  6.53 us
    all_to_all x1, starting transfers between devices, on_device(): lax.all_to_all(g_slots, 'expert', split_axis=0, concat_axis=0, tiled=True)  5.17 us
    all_to_all x1, starting transfers between devices, on_device(): sliced = lax.all_to_all(rows, 'dp', split_axis=1, concat_axis=0, tiled=True)  4.87 us
    all_to_all x1, waiting for transfers between devices, on_device(): lax.all_to_all(hval, 'expert', split_axis=0, concat_axis=0, tiled=True)  4.54 us
  transfers between devices with their start and end apart: 6, of which 5 were waited for; matrix products, arithmetic and copies ran while one was open for 4% of the time, Pallas kernels for 0%

commit v1 on v0

v1 whole, which is shorter than its diff:
```python
import functools

import jax
import jax.numpy as jnp
from jax import lax
from jax.experimental import pallas as pl
from jax.experimental.pallas import tpu as pltpu
from jax.sharding import PartitionSpec as P

LANES = 128


def swap(value, axis, offset):
    count = lax.axis_size(axis)
    return lax.ppermute(value, axis, [(i, i ^ offset) for i in range(count)])


def placing_of(ids, me, experts, slots, parts):
    count = ids.shape[1]
    part = slots // parts
    named = lax.broadcasted_iota(jnp.int32, (experts, count), 0) == ids
    earlier = (
        lax.broadcasted_iota(jnp.int32, (count, count), 0)
        < lax.broadcasted_iota(jnp.int32, (count, count), 1)
    ).astype(jnp.bfloat16)
    before = jnp.dot(named.astype(jnp.bfloat16), earlier, preferred_element_type=jnp.float32)
    rank = jnp.sum(jnp.where(named, before, 0.0), axis=0, keepdims=True).astype(jnp.int32)
    piece = sum(((rank >= part * p).astype(jnp.int32) for p in range(1, parts)), jnp.zeros_like(rank))
    row = (piece * experts + (ids ^ me)) * part + rank - piece * part
    return lax.broadcasted_iota(jnp.int32, (experts * slots, count), 0) == row


def place_kernel(experts, slots, parts, me_ref, ids_ref, gates_ref, tokens_ref, cots_ref, *outs):
    placing = placing_of(ids_ref[...], me_ref[0], experts, slots, parts)
    one_hot = placing.astype(jnp.bfloat16)
    width, inner = tokens_ref.shape[1], cots_ref.shape[1]
    gate = jnp.sum(
        jnp.where(placing, gates_ref[...].astype(jnp.float32), 0.0), axis=1, keepdims=True
    )
    gate = jnp.broadcast_to(gate, (gate.shape[0], LANES)).astype(jnp.bfloat16)
    cots = jnp.dot(one_hot, cots_ref[...], preferred_element_type=jnp.float32).astype(jnp.bfloat16)
    rows = jnp.dot(one_hot, tokens_ref[...], preferred_element_type=jnp.float32).astype(
        jnp.bfloat16
    )
    part = slots // parts
    for i, out in enumerate(outs):
        here = slice(i * part, (i + 1) * part)
        out[:, :width] = rows[here]
        out[:, width : width + inner] = cots[here]
        out[:, width + inner :] = gate[here]


def share_kernel(experts, slots, parts, groups, me_ref, *refs):
    ids, tokens, outs = refs[:groups], refs[groups : 2 * groups], refs[2 * groups :]
    part = slots // parts
    for g in range(groups):
        one_hot = placing_of(ids[g][...], me_ref[0], experts, slots, parts).astype(jnp.bfloat16)
        rows = jnp.dot(one_hot, tokens[g][...], preferred_element_type=jnp.float32).astype(
            jnp.bfloat16
        )
        for p in range(parts):
            for k in range(experts):
                i = p * experts + k
                outs[k][(g * parts + p) * part : (g * parts + p + 1) * part] = rows[
                    i * part : (i + 1) * part
                ]


def vmem(count):
    return [pl.BlockSpec(memory_space=pltpu.VMEM)] * count


def on_device(tokens, expert_ids, gates, cotangent, weights):
    experts = lax.axis_size("expert")
    members = lax.axis_size("dp")
    me = lax.axis_index("expert")
    group = lax.axis_index("dp")
    count, width = tokens.shape
    inner = cotangent.shape[1]
    share = width // members
    slots = max(2, 2 * count // experts)
    parts = 2 if slots % 32 == 0 else 1
    part = slots // parts
    wide = width + inner + LANES
    me_ref = me.reshape(1)
    ids = expert_ids.reshape(1, count)

    everyone = lax.all_gather(ids, "dp", axis=0, tiled=True)
    shares = []
    for k in range(1, members):
        cut = lax.dynamic_slice_in_dim(tokens, (group ^ k) * share, share, 1)
        shares.append(swap(cut, "dp", k))
    others = [lax.dynamic_slice_in_dim(everyone, group ^ k, 1, 0) for k in range(1, members)]

    placed = pl.pallas_call(
        functools.partial(place_kernel, experts, slots, parts),
        out_shape=[jax.ShapeDtypeStruct((part, wide), jnp.bfloat16)] * (parts * experts),
        in_specs=[pl.BlockSpec(memory_space=pltpu.SMEM)] + vmem(4),
        out_specs=vmem(parts * experts),
        compiler_params=pltpu.CompilerParams(vmem_limit_bytes=32 << 20),
        name="place",
    )(me_ref, ids, gates.reshape(1, count), tokens, cotangent)

    received = []
    for p in range(parts):
        blocks = placed[p * experts : (p + 1) * experts]
        got = [blocks[0]] + [None] * (experts - 1)
        for k in reversed(range(1, experts)):
            got[k] = swap(blocks[k], "expert", k)
        received.append(jnp.concatenate(got, axis=0))

    weight = weights[0]
    activation, dpres, own = [], [], []
    for p in range(parts):
        rows = received[p][:, :width]
        cots = received[p][:, width : width + inner].astype(jnp.float32)
        gate = received[p][:, width + inner : width + inner + 1].astype(jnp.float32)
        pre = jnp.dot(rows, weight, preferred_element_type=jnp.float32)
        sig = jax.nn.sigmoid(pre)
        activation.append((gate * pre * sig).astype(jnp.bfloat16))
        dpres.append((cots * gate * sig * (1.0 + pre * (1.0 - sig))).astype(jnp.bfloat16))
        own.append(lax.dynamic_slice_in_dim(rows, group * share, share, 1))

    groups = members - 1
    blocks = pl.pallas_call(
        functools.partial(share_kernel, experts, slots, parts, groups),
        out_shape=[jax.ShapeDtypeStruct((groups * slots, share), jnp.bfloat16)] * experts,
        in_specs=[pl.BlockSpec(memory_space=pltpu.SMEM)] + vmem(2 * groups),
        out_specs=vmem(experts),
        compiler_params=pltpu.CompilerParams(vmem_limit_bytes=32 << 20),
        name="place_shares",
    )(me_ref, *others, *shares)
    lefts = [blocks[0]] + [swap(blocks[k], "expert", k) for k in range(1, experts)]
    lefts = jnp.stack(lefts).reshape(experts, groups, parts, part, share)

    gathered = [[None] * parts for _ in range(groups)]
    for p in range(parts):
        if members == 4:
            mine = dpres[p]
            first = swap(mine, "dp", 1)
            middle = [(1, 2), (2, 1)]
            outward = [(1, 0), (2, 3)]
            across = lax.ppermute(mine, "dp", middle)
            far = lax.ppermute(first, "dp", middle)
            ends = (group == 0) | (group == 3)
            out_near = lax.ppermute(across, "dp", outward)
            out_far = lax.ppermute(far, "dp", outward)
            second = jnp.where(ends, out_near, far)
            third = jnp.where(ends, out_far, across)
            gathered[0][p], gathered[1][p], gathered[2][p] = first, second, third
        else:
            for k in range(1, members):
                gathered[k - 1][p] = swap(dpres[p], "dp", k)

    back = []
    for p in range(parts):
        act = activation[p].reshape(experts, part, inner)
        back += [act[0]] + [swap(act[k], "expert", k) for k in range(1, experts)]
    returned = jnp.concatenate(back, axis=0)
    placing = placing_of(ids, me, experts, slots, parts).astype(jnp.bfloat16)
    hidden = lax.dot_general(
        placing, returned, (((0,), (0,)), ((), ())), preferred_element_type=jnp.float32
    ).astype(jnp.bfloat16)

    left, right = list(own), list(dpres)
    for j in range(groups):
        for p in range(parts):
            left.append(lefts[:, j, p].reshape(experts * part, share))
            right.append(gathered[j][p])
    grad = lax.dot_general(
        jnp.concatenate(left, axis=0),
        jnp.concatenate(right, axis=0),
        (((0,), (0,)), ((), ())),
        preferred_element_type=jnp.float32,
    )
    return (hidden, grad[None])


def solution(mesh):
    return jax.shard_map(
        on_device,
        mesh=mesh,
        in_specs=(
            P(("dp", "expert"), None),
            P(("dp", "expert"), None),
            P(("dp", "expert")),
            P(("dp", "expert"), None),
            P("expert", None, None),
        ),
        out_specs=(P(("dp", "expert"), None), P("expert", "dp", None)),
        check_vma=False,
    )
```

time: 185 us -> 175 us (0.946)
  starting transfers between devices: 20.7 us -> 43.8 us
  matrix products: 29.9 us -> 11.7 us
  waiting for transfers between devices: 112 us -> 94.1 us
  between operations: 14.1 us -> 1.2 us
  blocking collectives: 0 us -> 11.4 us
  local copies, waits for them, and re-layouts: 5.17 us -> 9.3 us
    all_to_all x5 -> x0, waiting for transfers between devices: 112 us -> none  [the longest x1 73 us: on_device(): sliced = lax.all_to_all(rows, 'dp', split_axis=1, concat_axis=0, tiled=True)]
    ppermute x0 -> x48, waiting for transfers between devices: none -> 94.1 us  [the longest x40 72.9 us: swap(): return lax.ppermute(value, axis, [(i, i ^ offset) for i in range(count)])]
    ppermute x0 -> x48, starting transfers between devices: none -> 43.8 us  [the longest x40 35.9 us: swap(): return lax.ppermute(value, axis, [(i, i ^ offset) for i in range(count)])]
    all_to_all x5 -> x0, starting transfers between devices: 20.6 us -> none  [the longest x1 5.17 us: on_device(): lax.all_to_all(g_slots, 'expert', split_axis=0, concat_axis=0, tiled=True)]
    dot_general x8 -> x4, matrix products: 28.9 us -> 10.7 us  [the longest x2 5.87 us: on_device(): pre = jnp.dot(rows, weight, preferred_element_type=jnp.float32)]
    all_gather x0 -> x1, blocking collectives: none -> 11.4 us  [on_device(): everyone = lax.all_gather(ids, 'dp', axis=0, tiled=True)]
    unnamed x2 -> x60, local copies, waits for them, and re-layouts: 0.01 us -> 8.86 us
    all_to_all x3 -> x0, local copies, waits for them, and re-layouts: 5.09 us -> none  [the longest x2 4.39 us: on_device(): sliced = lax.all_to_all(rows, 'dp', split_axis=1, concat_axis=0, tiled=True)]
  transfers between devices with their start and end apart: 6 -> 48, of which waited for: 5 -> 27; matrix products, arithmetic and copies ran while one was open for 4% -> 8% of each run, Pallas kernels for 0% -> 1%
where the time goes in v1:
time: 175 us
  waiting for transfers between devices  94.1 us (54%)
  starting transfers between devices  43.8 us (25%)
  matrix products  11.7 us (7%)
  blocking collectives  11.4 us (7%)
  local copies, waits for them, and re-layouts  9.3 us (5%)
  Pallas kernels  1.81 us (1%)
    ppermute x40, waiting for transfers between devices, swap(): return lax.ppermute(value, axis, [(i, i ^ offset) for i in range(count)])  72.9 us
    ppermute x40, starting transfers between devices, swap(): return lax.ppermute(value, axis, [(i, i ^ offset) for i in range(count)])  35.9 us
    ppermute x2, waiting for transfers between devices, on_device(): out_near = lax.ppermute(across, 'dp', outward)  11.6 us
    all_gather x1, blocking collectives, on_device(): everyone = lax.all_gather(ids, 'dp', axis=0, tiled=True)  11.4 us
    ppermute x2, waiting for transfers between devices, on_device(): out_far = lax.ppermute(far, 'dp', outward)  9.66 us
    unnamed x60, local copies, waits for them, and re-layouts  8.86 us
    dot_general x2, matrix products, on_device(): pre = jnp.dot(rows, weight, preferred_element_type=jnp.float32)  5.87 us
    dot_general x1, matrix products, on_device(): lax.dot_general(jnp.concatenate(left, axis=0), jnp.concatenate(right, axi...  3.97 us
  transfers between devices with their start and end apart: 48, of which 27 were waited for; matrix products, arithmetic and copies ran while one was open for 8% of the time, Pallas kernels for 1%

profile of v1, /device:TPU:0, one launch (start us, length us, event | category | flops | bytes accessed | tf_op | source)
XLA Modules:
  0.0 174.9 jit_solution(12533608893249994700)
XLA Ops:
  0.6 1.2 copy-done
  5.5 2.6 %collective-permute-start.1 = (bf16[16,4736]{1,0:T(8,128)(2,1)S(1)}, bf16[16,4736]{1,0:T(8,128)(2,1)}, u32[]{:S(2)}, u32[]{:S(2)}) collective-permute-start(bf16[16,4736]{1,0:T(8,128)(2,1)S(1)} %get-tuple-element.28), channel_id=1, source_target_pairs={{0,2},{1,3},{2,0},{3,1},{4,6},{5,7},{6,4},{7,5},{8,10},{9,11},{10,... | collective-permute-start | bytes 454664 | tf_op jit(solution)/shard_map/ppermute | solution.py:15
  8.1 1.8 %collective-permute-start.3 = (bf16[16,4736]{1,0:T(8,128)(2,1)S(1)}, bf16[16,4736]{1,0:T(8,128)(2,1)}, u32[]{:S(2)}, u32[]{:S(2)}) collective-permute-start(bf16[16,4736]{1,0:T(8,128)(2,1)S(1)} %get-tuple-element.30), channel_id=1, source_target_pairs={{0,4},{1,5},{2,6},{3,7},{4,0},{5,1},{6,2},{7,3},{8,12},{9,13},{10,... | collective-permute-start | bytes 454664 | tf_op jit(solution)/shard_map/ppermute | solution.py:15
  9.9 11.4 %all-gather = s32[512,1]{0,1:T(1,128)S(1)} all-gather(s32[128,1]{0,1:T(1,128)} %param.6), channel_id=2, replica_groups=mesh['dp'=4,'expert'=8] {'dp'}, dimensions={0}, use_global_device_ids=true | all-gather | bytes 2560 | tf_op jit(solution)/shard_map/all_gather | solution.py:88
  23.8 2.5 %collective-permute-start.5 = (bf16[16,4736]{1,0:T(8,128)(2,1)S(1)}, bf16[16,4736]{1,0:T(8,128)(2,1)S(1)}, u32[]{:S(2)}, u32[]{:S(2)}) collective-permute-start(bf16[16,4736]{1,0:T(8,128)(2,1)S(1)} %get-tuple-element.32), channel_id=1, source_target_pairs={{0,6},{1,7},{2,4},{3,5},{4,2},{5,3},{6,0},{7,1},{8,14},{9,15},{10,... | collective-permute-start | bytes 454664 | tf_op jit(solution)/shard_map/ppermute | solution.py:15
  28.2 1.3 collective-permute-start.14
  32.9 1.1 collective-permute-start.17
  34.0 1.2 collective-permute-start.18
  35.2 1.9 %collective-permute-start.19 = (bf16[16,4736]{1,0:T(8,128)(2,1)S(1)}, bf16[16,4736]{1,0:T(8,128)(2,1)S(1)}, u32[]{:S(2)}, u32[]{:S(2)}) collective-permute-start(bf16[16,4736]{1,0:T(8,128)(2,1)S(1)} %get-tuple-element.40), channel_id=1, source_target_pairs={{0,6},{1,7},{2,4},{3,5},{4,2},{5,3},{6,0},{7,1},{8,14},{9,15},{10,... | collective-permute-start | bytes 454664 | tf_op jit(solution)/shard_map/ppermute | solution.py:15
  37.7 1.4 collective-permute-done.16
  40.0 9.2 %collective-permute-done.18 = bf16[16,4736]{1,0:T(8,128)(2,1)S(1)} collective-permute-done((bf16[16,4736]{1,0:T(8,128)(2,1)S(1)}, bf16[16,4736]{1,0:T(8,128)(2,1)S(1)}, u32[]{:S(2)}, u32[]{:S(2)}) %collective-permute-start.18) | collective-permute-done | bytes 151584 | tf_op jit(solution)/shard_map/ppermute | solution.py:15
  49.6 4.5 %multiply_convert_fusion.3 = (bf16[128,1024]{1,0:T(8,128)(2,1)S(1)}, f32[128,1024]{1,0:T(8,128)S(1)}) fusion(f32[128]{0:T(128)S(1)} %convert_reduce_fusion.1, bf16[1,3584,1024]{2,1,0:T(8,128)(2,1)} %param.9, bf16[128,4736]{1,0:T(8,128)(2,1)S(1)} %constant_dynamic-update-slice_fusion), kind=kOutput, calls=%fused_computation.12 | convolution fusion | flops 940310528 | bytes 9044480 | tf_op jit(solution)/shard_map/dot_general | solution.py:118
  54.8 1.3 multiply_convert_fusion.2
  58.5 3.1 %collective-permute-done.8 = bf16[16,1024]{1,0:T(8,128)(2,1)S(1)} collective-permute-done((bf16[16,1024]{1,0:T(8,128)(2,1)S(1)}, bf16[16,1024]{1,0:T(8,128)(2,1)S(1)}, u32[]{:S(2)}, u32[]{:S(2)}) %collective-permute-start.8) | collective-permute-done | bytes 32800 | tf_op jit(solution)/shard_map/ppermute | solution.py:15
  61.6 3.3 %collective-permute-done.9 = bf16[16,1024]{1,0:T(8,128)(2,1)S(1)} collective-permute-done((bf16[16,1024]{1,0:T(8,128)(2,1)S(1)}, bf16[16,1024]{1,0:T(8,128)(2,1)S(1)}, u32[]{:S(2)}, u32[]{:S(2)}) %collective-permute-start.9) | collective-permute-done | bytes 32800 | tf_op jit(solution)/shard_map/ppermute | solution.py:15
  65.8 3.0 %collective-permute-done.10 = bf16[16,1024]{1,0:T(8,128)(2,1)S(1)} collective-permute-done((bf16[16,1024]{1,0:T(8,128)(2,1)S(1)}, bf16[16,1024]{1,0:T(8,128)(2,1)S(1)}, u32[]{:S(2)}, u32[]{:S(2)}) %collective-permute-start.10) | collective-permute-done | bytes 32800 | tf_op jit(solution)/shard_map/ppermute | solution.py:15
  68.9 3.3 %collective-permute-done.11 = bf16[16,1024]{1,0:T(8,128)(2,1)S(1)} collective-permute-done((bf16[16,1024]{1,0:T(8,128)(2,1)S(1)}, bf16[16,1024]{1,0:T(8,128)(2,1)S(1)}, u32[]{:S(2)}, u32[]{:S(2)}) %collective-permute-start.11) | collective-permute-done | bytes 32800 | tf_op jit(solution)/shard_map/ppermute | solution.py:15
  72.2 1.8 %collective-permute-start.12 = (bf16[16,1024]{1,0:T(8,128)(2,1)S(1)}, bf16[16,1024]{1,0:T(8,128)(2,1)S(1)}, u32[]{:S(2)}, u32[]{:S(2)}) collective-permute-start(bf16[16,1024]{1,0:T(8,128)(2,1)S(1)} %get-tuple-element.72), channel_id=1, source_target_pairs={{0,6},{1,7},{2,4},{3,5},{4,2},{5,3},{6,0},{7,1},{8,14},{9,15},{10,... | collective-permute-start | bytes 98312 | tf_op jit(solution)/shard_map/ppermute | solution.py:15
  74.0 3.0 %collective-permute-done.12 = bf16[16,1024]{1,0:T(8,128)(2,1)S(1)} collective-permute-done((bf16[16,1024]{1,0:T(8,128)(2,1)S(1)}, bf16[16,1024]{1,0:T(8,128)(2,1)S(1)}, u32[]{:S(2)}, u32[]{:S(2)}) %collective-permute-start.12) | collective-permute-done | bytes 32800 | tf_op jit(solution)/shard_map/ppermute | solution.py:15
  77.0 4.2 %collective-permute-done.13 = bf16[16,1024]{1,0:T(8,128)(2,1)S(1)} collective-permute-done((bf16[16,1024]{1,0:T(8,128)(2,1)S(1)}, bf16[16,1024]{1,0:T(8,128)(2,1)S(1)}, u32[]{:S(2)}, u32[]{:S(2)}) %collective-permute-start.13) | collective-permute-done | bytes 32800 | tf_op jit(solution)/shard_map/ppermute | solution.py:15
  81.4 1.2 collective-permute-done.21
  82.5 1.3 collective-permute-start.22
  83.8 2.6 %collective-permute-done.22 = bf16[16,1024]{1,0:T(8,128)(2,1)S(1)} collective-permute-done((bf16[16,1024]{1,0:T(8,128)(2,1)S(1)}, bf16[16,1024]{1,0:T(8,128)(2,1)S(1)}, u32[]{:S(2)}, u32[]{:S(2)}) %collective-permute-start.22) | collective-permute-done | bytes 32800 | tf_op jit(solution)/shard_map/ppermute | solution.py:15
  86.5 3.5 %collective-permute-done.23 = bf16[16,1024]{1,0:T(8,128)(2,1)S(1)} collective-permute-done((bf16[16,1024]{1,0:T(8,128)(2,1)S(1)}, bf16[16,1024]{1,0:T(8,128)(2,1)S(1)}, u32[]{:S(2)}, u32[]{:S(2)}) %collective-permute-start.23) | collective-permute-done | bytes 32800 | tf_op jit(solution)/shard_map/ppermute | solution.py:15
  90.0 1.1 collective-permute-start.24
  91.1 2.8 %collective-permute-done.24 = bf16[16,1024]{1,0:T(8,128)(2,1)S(1)} collective-permute-done((bf16[16,1024]{1,0:T(8,128)(2,1)S(1)}, bf16[16,1024]{1,0:T(8,128)(2,1)S(1)}, u32[]{:S(2)}, u32[]{:S(2)}) %collective-permute-start.24) | collective-permute-done | bytes 32800 | tf_op jit(solution)/shard_map/ppermute | solution.py:15
  93.9 3.3 %collective-permute-done.25 = bf16[16,1024]{1,0:T(8,128)(2,1)S(1)} collective-permute-done((bf16[16,1024]{1,0:T(8,128)(2,1)S(1)}, bf16[16,1024]{1,0:T(8,128)(2,1)S(1)}, u32[]{:S(2)}, u32[]{:S(2)}) %collective-permute-start.25) | collective-permute-done | bytes 32800 | tf_op jit(solution)/shard_map/ppermute | solution.py:15
  97.2 1.6 collective-permute-start.26
  98.9 3.2 %collective-permute-done.26 = bf16[16,1024]{1,0:T(8,128)(2,1)S(1)} collective-permute-done((bf16[16,1024]{1,0:T(8,128)(2,1)S(1)}, bf16[16,1024]{1,0:T(8,128)(2,1)S(1)}, u32[]{:S(2)}, u32[]{:S(2)}) %collective-permute-start.26) | collective-permute-done | bytes 32800 | tf_op jit(solution)/shard_map/ppermute | solution.py:15
  102.1 4.2 %collective-permute-done.27 = bf16[16,1024]{1,0:T(8,128)(2,1)S(1)} collective-permute-done((bf16[16,1024]{1,0:T(8,128)(2,1)S(1)}, bf16[16,1024]{1,0:T(8,128)(2,1)S(1)}, u32[]{:S(2)}, u32[]{:S(2)}) %collective-permute-start.27) | collective-permute-done | bytes 32800 | tf_op jit(solution)/shard_map/ppermute | solution.py:15
  107.0 6.1 %collective-permute-start.39 = (bf16[128,1024]{1,0:T(8,128)(2,1)S(1)}, bf16[128,1024]{1,0:T(8,128)(2,1)S(1)}, u32[]{:S(2)}, u32[]{:S(2)}) collective-permute-start(bf16[128,1024]{1,0:T(8,128)(2,1)S(1)} %get-tuple-element.51), channel_id=1, source_target_pairs={{0,8},{8,0},{16,24},{24,16},{1,9},{9,1},{17,25},{25,17},{2,10},{10... | collective-permute-start | bytes 786440 | tf_op jit(solution)/shard_map/ppermute | solution.py:15
  117.0 5.2 %collective-permute-done.32 = bf16[96,896]{1,0:T(8,128)(2,1)S(1)} collective-permute-done((bf16[96,896]{1,0:T(8,128)(2,1)S(1)}, bf16[96,896]{1,0:T(8,128)(2,1)S(1)}, u32[]{:S(2)}, u32[]{:S(2)}) %collective-permute-start.32) | collective-permute-done | bytes 172064 | tf_op jit(solution)/shard_map/ppermute | solution.py:15
  122.2 1.1 collective-permute-start.34
  123.3 1.8 %collective-permute-done.33 = bf16[96,896]{1,0:T(8,128)(2,1)S(1)} collective-permute-done((bf16[96,896]{1,0:T(8,128)(2,1)S(1)}, bf16[96,896]{1,0:T(8,128)(2,1)S(1)}, u32[]{:S(2)}, u32[]{:S(2)}) %collective-permute-start.33) | collective-permute-done | bytes 172064 | tf_op jit(solution)/shard_map/ppermute | solution.py:15
  126.0 1.8 %collective-permute-done.34 = bf16[96,896]{1,0:T(8,128)(2,1)S(1)} collective-permute-done((bf16[96,896]{1,0:T(8,128)(2,1)S(1)}, bf16[96,896]{1,0:T(8,128)(2,1)S(1)}, u32[]{:S(2)}, u32[]{:S(2)}) %collective-permute-start.34) | collective-permute-done | bytes 172064 | tf_op jit(solution)/shard_map/ppermute | solution.py:15
  127.8 1.6 collective-permute-start.36
  129.4 5.7 %collective-permute-done.35 = bf16[96,896]{1,0:T(8,128)(2,1)S(1)} collective-permute-done((bf16[96,896]{1,0:T(8,128)(2,1)S(1)}, bf16[96,896]{1,0:T(8,128)(2,1)S(1)}, u32[]{:S(2)}, u32[]{:S(2)}) %collective-permute-start.35) | collective-permute-done | bytes 172064 | tf_op jit(solution)/shard_map/ppermute | solution.py:15
  135.1 1.4 collective-permute-start.37
  137.2 5.1 %collective-permute-done.37 = bf16[96,896]{1,0:T(8,128)(2,1)S(1)} collective-permute-done((bf16[96,896]{1,0:T(8,128)(2,1)S(1)}, bf16[96,896]{1,0:T(8,128)(2,1)S(1)}, u32[]{:S(2)}, u32[]{:S(2)}) %collective-permute-start.37) | collective-permute-done | bytes 172064 | tf_op jit(solution)/shard_map/ppermute | solution.py:15
  142.7 1.3 collective-permute-start.41
  145.4 1.3 collective-permute-start.44
  146.8 1.3 collective-permute-start.46
  148.1 1.3 collective-permute-start.47
  149.4 3.5 %collective-permute-done.41 = bf16[128,1024]{1,0:T(8,128)(2,1)S(1)} collective-permute-done((bf16[128,1024]{1,0:T(8,128)(2,1)S(1)}, bf16[128,1024]{1,0:T(8,128)(2,1)S(1)}, u32[]{:S(2)}, u32[]{:S(2)}) %collective-permute-start.41) | collective-permute-done | bytes 262176 | tf_op jit(solution)/shard_map/ppermute | solution.py:146
  153.0 8.0 %collective-permute-done.44 = bf16[128,1024]{1,0:T(8,128)(2,1)S(1)} collective-permute-done((bf16[128,1024]{1,0:T(8,128)(2,1)S(1)}, bf16[128,1024]{1,0:T(8,128)(2,1)S(1)}, u32[]{:S(2)}, u32[]{:S(2)}) %collective-permute-start.44) | collective-permute-done | bytes 262176 | tf_op jit(solution)/shard_map/ppermute | solution.py:146
  161.1 5.5 %collective-permute-done.46 = bf16[128,1024]{1,0:T(8,128)(2,1)S(1)} collective-permute-done((bf16[128,1024]{1,0:T(8,128)(2,1)S(1)}, bf16[128,1024]{1,0:T(8,128)(2,1)S(1)}, u32[]{:S(2)}, u32[]{:S(2)}) %collective-permute-start.46) | collective-permute-done | bytes 262176 | tf_op jit(solution)/shard_map/ppermute | solution.py:147
  166.8 4.1 %collective-permute-done.47 = bf16[128,1024]{1,0:T(8,128)(2,1)S(1)} collective-permute-done((bf16[128,1024]{1,0:T(8,128)(2,1)S(1)}, bf16[128,1024]{1,0:T(8,128)(2,1)S(1)}, u32[]{:S(2)}, u32[]{:S(2)}) %collective-permute-start.47) | collective-permute-done | bytes 262176 | tf_op jit(solution)/shard_map/ppermute | solution.py:147
  170.9 4.0 %convolution_bitcast_fusion = f32[1,896,1024]{2,1,0:T(8,128)} fusion(bf16[1024,896]{1,0:T(8,128)(2,1)S(1)} %constant_dynamic-update-slice_fusion.40, bf16[1024,1024]{1,0:T(8,128)(2,1)S(1)} %select_dynamic-update-slice_fusion), kind=kOutput, calls=%fused_computation.4 | convolution fusion | flops 1879048192 | bytes 7602176 | tf_op jit(solution)/shard_map/dot_general | solution.py:170
  (138 shorter events, 25.8 us)
Async XLA Ops:
  5.0 18.8 %collective-permute-start = (bf16[16,4736]{1,0:T(8,128)(2,1)S(1)}, bf16[16,4736]{1,0:T(8,128)(2,1)}, u32[]{:S(2)}, u32[]{:S(2)}) collective-permute-start(bf16[16,4736]{1,0:T(8,128)(2,1)S(1)} %get-tuple-element.27), channel_id=1, source_target_pairs={{0,1},{1,0},{2,3},{3,2},{4,5},{5,4},{6,7},{7,6},{8,9},{9,8},{10,11... | collective-permute-start | bytes 454664 | tf_op jit(solution)/shard_map/ppermute | solution.py:15
  5.5 21.7 %collective-permute-start.1 = (bf16[16,4736]{1,0:T(8,128)(2,1)S(1)}, bf16[16,4736]{1,0:T(8,128)(2,1)}, u32[]{:S(2)}, u32[]{:S(2)}) collective-permute-start(bf16[16,4736]{1,0:T(8,128)(2,1)S(1)} %get-tuple-element.28), channel_id=1, source_target_pairs={{0,2},{1,3},{2,0},{3,1},{4,6},{5,7},{6,4},{7,5},{8,10},{9,11},{10,... | collective-permute-start | bytes 454664 | tf_op jit(solution)/shard_map/ppermute | solution.py:15
  8.1 20.2 %collective-permute-start.2 = (bf16[16,4736]{1,0:T(8,128)(2,1)S(1)}, bf16[16,4736]{1,0:T(8,128)(2,1)}, u32[]{:S(2)}, u32[]{:S(2)}) collective-permute-start(bf16[16,4736]{1,0:T(8,128)(2,1)S(1)} %get-tuple-element.29), channel_id=1, source_target_pairs={{0,3},{1,2},{2,1},{3,0},{4,7},{5,6},{6,5},{7,4},{8,11},{9,10},{10,... | collective-permute-start | bytes 454664 | tf_op jit(solution)/shard_map/ppermute | solution.py:15
  8.1 22.3 %collective-permute-start.3 = (bf16[16,4736]{1,0:T(8,128)(2,1)S(1)}, bf16[16,4736]{1,0:T(8,128)(2,1)}, u32[]{:S(2)}, u32[]{:S(2)}) collective-permute-start(bf16[16,4736]{1,0:T(8,128)(2,1)S(1)} %get-tuple-element.30), channel_id=1, source_target_pairs={{0,4},{1,5},{2,6},{3,7},{4,0},{5,1},{6,2},{7,3},{8,12},{9,13},{10,... | collective-permute-start | bytes 454664 | tf_op jit(solution)/shard_map/ppermute | solution.py:15
  9.9 22.4 %collective-permute-start.4 = (bf16[16,4736]{1,0:T(8,128)(2,1)S(1)}, bf16[16,4736]{1,0:T(8,128)(2,1)S(1)}, u32[]{:S(2)}, u32[]{:S(2)}) collective-permute-start(bf16[16,4736]{1,0:T(8,128)(2,1)S(1)} %get-tuple-element.31), channel_id=1, source_target_pairs={{0,5},{1,4},{2,7},{3,6},{4,1},{5,0},{6,3},{7,2},{8,13},{9,12},{10,... | collective-permute-start | bytes 454664 | tf_op jit(solution)/shard_map/ppermute | solution.py:15
  23.8 9.1 %collective-permute-start.5 = (bf16[16,4736]{1,0:T(8,128)(2,1)S(1)}, bf16[16,4736]{1,0:T(8,128)(2,1)S(1)}, u32[]{:S(2)}, u32[]{:S(2)}) collective-permute-start(bf16[16,4736]{1,0:T(8,128)(2,1)S(1)} %get-tuple-element.32), channel_id=1, source_target_pairs={{0,6},{1,7},{2,4},{3,5},{4,2},{5,3},{6,0},{7,1},{8,14},{9,15},{10,... | collective-permute-start | bytes 454664 | tf_op jit(solution)/shard_map/ppermute | solution.py:15
  27.2 6.8 %collective-permute-start.6 = (bf16[16,4736]{1,0:T(8,128)(2,1)S(1)}, bf16[16,4736]{1,0:T(8,128)(2,1)S(1)}, u32[]{:S(2)}, u32[]{:S(2)}) collective-permute-start(bf16[16,4736]{1,0:T(8,128)(2,1)S(1)} %get-tuple-element.33), channel_id=1, source_target_pairs={{0,7},{1,6},{2,5},{3,4},{4,3},{5,2},{6,1},{7,0},{8,15},{9,14},{10,... | collective-permute-start | bytes 454664 | tf_op jit(solution)/shard_map/ppermute | solution.py:15
  28.2 7.0 %collective-permute-start.14 = (bf16[16,4736]{1,0:T(8,128)(2,1)S(1)}, bf16[16,4736]{1,0:T(8,128)(2,1)S(1)}, u32[]{:S(2)}, u32[]{:S(2)}) collective-permute-start(bf16[16,4736]{1,0:T(8,128)(2,1)S(1)} %get-tuple-element.35), channel_id=1, source_target_pairs={{0,1},{1,0},{2,3},{3,2},{4,5},{5,4},{6,7},{7,6},{8,9},{9,8},{10,11... | collective-permute-start | bytes 454664 | tf_op jit(solution)/shard_map/ppermute | solution.py:15
  30.5 6.9 %collective-permute-start.15 = (bf16[16,4736]{1,0:T(8,128)(2,1)S(1)}, bf16[16,4736]{1,0:T(8,128)(2,1)S(1)}, u32[]{:S(2)}, u32[]{:S(2)}) collective-permute-start(bf16[16,4736]{1,0:T(8,128)(2,1)S(1)} %get-tuple-element.36), channel_id=1, source_target_pairs={{0,2},{1,3},{2,0},{3,1},{4,6},{5,7},{6,4},{7,5},{8,10},{9,11},{10,... | collective-permute-start | bytes 454664 | tf_op jit(solution)/shard_map/ppermute | solution.py:15
  32.3 6.7 %collective-permute-start.16 = (bf16[16,4736]{1,0:T(8,128)(2,1)S(1)}, bf16[16,4736]{1,0:T(8,128)(2,1)S(1)}, u32[]{:S(2)}, u32[]{:S(2)}) collective-permute-start(bf16[16,4736]{1,0:T(8,128)(2,1)S(1)} %get-tuple-element.37), channel_id=1, source_target_pairs={{0,3},{1,2},{2,1},{3,0},{4,7},{5,6},{6,5},{7,4},{8,11},{9,10},{10,... | collective-permute-start | bytes 454664 | tf_op jit(solution)/shard_map/ppermute | solution.py:15
  32.9 7.0 %collective-permute-start.17 = (bf16[16,4736]{1,0:T(8,128)(2,1)S(1)}, bf16[16,4736]{1,0:T(8,128)(2,1)S(1)}, u32[]{:S(2)}, u32[]{:S(2)}) collective-permute-start(bf16[16,4736]{1,0:T(8,128)(2,1)S(1)} %get-tuple-element.38), channel_id=1, source_target_pairs={{0,4},{1,5},{2,6},{3,7},{4,0},{5,1},{6,2},{7,3},{8,12},{9,13},{10,... | collective-permute-start | bytes 454664 | tf_op jit(solution)/shard_map/ppermute | solution.py:15
  34.0 15.1 %collective-permute-start.18 = (bf16[16,4736]{1,0:T(8,128)(2,1)S(1)}, bf16[16,4736]{1,0:T(8,128)(2,1)S(1)}, u32[]{:S(2)}, u32[]{:S(2)}) collective-permute-start(bf16[16,4736]{1,0:T(8,128)(2,1)S(1)} %get-tuple-element.39), channel_id=1, source_target_pairs={{0,5},{1,4},{2,7},{3,6},{4,1},{5,0},{6,3},{7,2},{8,13},{9,12},{10,... | collective-permute-start | bytes 454664 | tf_op jit(solution)/shard_map/ppermute | solution.py:15
  35.2 13.9 %collective-permute-start.19 = (bf16[16,4736]{1,0:T(8,128)(2,1)S(1)}, bf16[16,4736]{1,0:T(8,128)(2,1)S(1)}, u32[]{:S(2)}, u32[]{:S(2)}) collective-permute-start(bf16[16,4736]{1,0:T(8,128)(2,1)S(1)} %get-tuple-element.40), channel_id=1, source_target_pairs={{0,6},{1,7},{2,4},{3,5},{4,2},{5,3},{6,0},{7,1},{8,14},{9,15},{10,... | collective-permute-start | bytes 454664 | tf_op jit(solution)/shard_map/ppermute | solution.py:15
  37.4 12.0 %collective-permute-start.20 = (bf16[16,4736]{1,0:T(8,128)(2,1)S(1)}, bf16[16,4736]{1,0:T(8,128)(2,1)S(1)}, u32[]{:S(2)}, u32[]{:S(2)}) collective-permute-start(bf16[16,4736]{1,0:T(8,128)(2,1)S(1)} %get-tuple-element.41), channel_id=1, source_target_pairs={{0,7},{1,6},{2,5},{3,4},{4,3},{5,2},{6,1},{7,0},{8,15},{9,14},{10,... | collective-permute-start | bytes 454664 | tf_op jit(solution)/shard_map/ppermute | solution.py:15
  39.0 68.0 %collective-permute-start.28 = (bf16[128,896]{1,0:T(8,128)(2,1)S(1)}, bf16[128,896]{1,0:T(8,128)(2,1)S(1)}, u32[]{:S(2)}, u32[]{:S(2)}) collective-permute-start(bf16[128,896]{1,0:T(8,128)(2,1)S(1)} %get-tuple-element.61), channel_id=1, source_target_pairs={{0,8},{8,0},{16,24},{24,16},{1,9},{9,1},{17,25},{25,17},{2,10},{10... | collective-permute-start | bytes 688136 | tf_op jit(solution)/shard_map/ppermute | solution.py:15
  39.9 73.1 %collective-permute-start.29 = (bf16[128,896]{1,0:T(8,128)(2,1)S(1)}, bf16[128,896]{1,0:T(8,128)(2,1)S(1)}, u32[]{:S(2)}, u32[]{:S(2)}) collective-permute-start(bf16[128,896]{1,0:T(8,128)(2,1)S(1)} %get-tuple-element.62), channel_id=1, source_target_pairs={{0,16},{8,24},{16,0},{24,8},{1,17},{9,25},{17,1},{25,9},{2,18},{10... | collective-permute-start | bytes 688136 | tf_op jit(solution)/shard_map/ppermute | solution.py:15
  49.1 63.9 %collective-permute-start.30 = (bf16[128,896]{1,0:T(8,128)(2,1)S(1)}, bf16[128,896]{1,0:T(8,128)(2,1)S(1)}, u32[]{:S(2)}, u32[]{:S(2)}) collective-permute-start(bf16[128,896]{1,0:T(8,128)(2,1)S(1)} %get-tuple-element.60), channel_id=1, source_target_pairs={{0,24},{8,16},{16,8},{24,0},{1,25},{9,17},{17,9},{25,1},{2,26},{10... | collective-permute-start | bytes 688136 | tf_op jit(solution)/shard_map/ppermute | solution.py:15
  56.1 87.9 %collective-permute-start.38 = (bf16[128,1024]{1,0:T(8,128)(2,1)S(1)}, bf16[128,1024]{1,0:T(8,128)(2,1)S(1)}, u32[]{:S(2)}, u32[]{:S(2)}) collective-permute-start(bf16[128,1024]{1,0:T(8,128)(2,1)S(1)} %get-tuple-element.53), channel_id=1, source_target_pairs={{0,8},{8,0},{16,24},{24,16},{1,9},{9,1},{17,25},{25,17},{2,10},{10... | collective-permute-start | bytes 786440 | tf_op jit(solution)/shard_map/ppermute | solution.py:15
  56.4 1.3 collective-permute-start.7
  57.7 3.9 %collective-permute-start.8 = (bf16[16,1024]{1,0:T(8,128)(2,1)S(1)}, bf16[16,1024]{1,0:T(8,128)(2,1)S(1)}, u32[]{:S(2)}, u32[]{:S(2)}) collective-permute-start(bf16[16,1024]{1,0:T(8,128)(2,1)S(1)} %get-tuple-element.76), channel_id=1, source_target_pairs={{0,2},{1,3},{2,0},{3,1},{4,6},{5,7},{6,4},{7,5},{8,10},{9,11},{10,... | collective-permute-start | bytes 98312 | tf_op jit(solution)/shard_map/ppermute | solution.py:15
  61.6 3.3 %collective-permute-start.9 = (bf16[16,1024]{1,0:T(8,128)(2,1)S(1)}, bf16[16,1024]{1,0:T(8,128)(2,1)S(1)}, u32[]{:S(2)}, u32[]{:S(2)}) collective-permute-start(bf16[16,1024]{1,0:T(8,128)(2,1)S(1)} %get-tuple-element.75), channel_id=1, source_target_pairs={{0,3},{1,2},{2,1},{3,0},{4,7},{5,6},{6,5},{7,4},{8,11},{9,10},{10,... | collective-permute-start | bytes 98312 | tf_op jit(solution)/shard_map/ppermute | solution.py:15
  64.9 3.9 %collective-permute-start.10 = (bf16[16,1024]{1,0:T(8,128)(2,1)S(1)}, bf16[16,1024]{1,0:T(8,128)(2,1)S(1)}, u32[]{:S(2)}, u32[]{:S(2)}) collective-permute-start(bf16[16,1024]{1,0:T(8,128)(2,1)S(1)} %get-tuple-element.74), channel_id=1, source_target_pairs={{0,4},{1,5},{2,6},{3,7},{4,0},{5,1},{6,2},{7,3},{8,12},{9,13},{10,... | collective-permute-start | bytes 98312 | tf_op jit(solution)/shard_map/ppermute | solution.py:15
  68.9 3.3 %collective-permute-start.11 = (bf16[16,1024]{1,0:T(8,128)(2,1)S(1)}, bf16[16,1024]{1,0:T(8,128)(2,1)S(1)}, u32[]{:S(2)}, u32[]{:S(2)}) collective-permute-start(bf16[16,1024]{1,0:T(8,128)(2,1)S(1)} %get-tuple-element.73), channel_id=1, source_target_pairs={{0,5},{1,4},{2,7},{3,6},{4,1},{5,0},{6,3},{7,2},{8,13},{9,12},{10,... | collective-permute-start | bytes 98312 | tf_op jit(solution)/shard_map/ppermute | solution.py:15
  72.2 4.8 %collective-permute-start.12 = (bf16[16,1024]{1,0:T(8,128)(2,1)S(1)}, bf16[16,1024]{1,0:T(8,128)(2,1)S(1)}, u32[]{:S(2)}, u32[]{:S(2)}) collective-permute-start(bf16[16,1024]{1,0:T(8,128)(2,1)S(1)} %get-tuple-element.72), channel_id=1, source_target_pairs={{0,6},{1,7},{2,4},{3,5},{4,2},{5,3},{6,0},{7,1},{8,14},{9,15},{10,... | collective-permute-start | bytes 98312 | tf_op jit(solution)/shard_map/ppermute | solution.py:15
  77.0 4.2 %collective-permute-start.13 = (bf16[16,1024]{1,0:T(8,128)(2,1)S(1)}, bf16[16,1024]{1,0:T(8,128)(2,1)S(1)}, u32[]{:S(2)}, u32[]{:S(2)}) collective-permute-start(bf16[16,1024]{1,0:T(8,128)(2,1)S(1)} %get-tuple-element.71), channel_id=1, source_target_pairs={{0,7},{1,6},{2,5},{3,4},{4,3},{5,2},{6,1},{7,0},{8,15},{9,14},{10,... | collective-permute-start | bytes 98312 | tf_op jit(solution)/shard_map/ppermute | solution.py:15
  81.3 1.3 collective-permute-start.21
  82.5 3.9 %collective-permute-start.22 = (bf16[16,1024]{1,0:T(8,128)(2,1)S(1)}, bf16[16,1024]{1,0:T(8,128)(2,1)S(1)}, u32[]{:S(2)}, u32[]{:S(2)}) collective-permute-start(bf16[16,1024]{1,0:T(8,128)(2,1)S(1)} %get-tuple-element.68), channel_id=1, source_target_pairs={{0,2},{1,3},{2,0},{3,1},{4,6},{5,7},{6,4},{7,5},{8,10},{9,11},{10,... | collective-permute-start | bytes 98312 | tf_op jit(solution)/shard_map/ppermute | solution.py:15
  86.5 3.5 %collective-permute-start.23 = (bf16[16,1024]{1,0:T(8,128)(2,1)S(1)}, bf16[16,1024]{1,0:T(8,128)(2,1)S(1)}, u32[]{:S(2)}, u32[]{:S(2)}) collective-permute-start(bf16[16,1024]{1,0:T(8,128)(2,1)S(1)} %get-tuple-element.67), channel_id=1, source_target_pairs={{0,3},{1,2},{2,1},{3,0},{4,7},{5,6},{6,5},{7,4},{8,11},{9,10},{10,... | collective-permute-start | bytes 98312 | tf_op jit(solution)/shard_map/ppermute | solution.py:15
  90.0 3.9 %collective-permute-start.24 = (bf16[16,1024]{1,0:T(8,128)(2,1)S(1)}, bf16[16,1024]{1,0:T(8,128)(2,1)S(1)}, u32[]{:S(2)}, u32[]{:S(2)}) collective-permute-start(bf16[16,1024]{1,0:T(8,128)(2,1)S(1)} %get-tuple-element.66), channel_id=1, source_target_pairs={{0,4},{1,5},{2,6},{3,7},{4,0},{5,1},{6,2},{7,3},{8,12},{9,13},{10,... | collective-permute-start | bytes 98312 | tf_op jit(solution)/shard_map/ppermute | solution.py:15
  93.9 3.3 %collective-permute-start.25 = (bf16[16,1024]{1,0:T(8,128)(2,1)S(1)}, bf16[16,1024]{1,0:T(8,128)(2,1)S(1)}, u32[]{:S(2)}, u32[]{:S(2)}) collective-permute-start(bf16[16,1024]{1,0:T(8,128)(2,1)S(1)} %get-tuple-element.65), channel_id=1, source_target_pairs={{0,5},{1,4},{2,7},{3,6},{4,1},{5,0},{6,3},{7,2},{8,13},{9,12},{10,... | collective-permute-start | bytes 98312 | tf_op jit(solution)/shard_map/ppermute | solution.py:15
  97.2 4.8 %collective-permute-start.26 = (bf16[16,1024]{1,0:T(8,128)(2,1)S(1)}, bf16[16,1024]{1,0:T(8,128)(2,1)S(1)}, u32[]{:S(2)}, u32[]{:S(2)}) collective-permute-start(bf16[16,1024]{1,0:T(8,128)(2,1)S(1)} %get-tuple-element.64), channel_id=1, source_target_pairs={{0,6},{1,7},{2,4},{3,5},{4,2},{5,3},{6,0},{7,1},{8,14},{9,15},{10,... | collective-permute-start | bytes 98312 | tf_op jit(solution)/shard_map/ppermute | solution.py:15
  102.1 4.2 %collective-permute-start.27 = (bf16[16,1024]{1,0:T(8,128)(2,1)S(1)}, bf16[16,1024]{1,0:T(8,128)(2,1)S(1)}, u32[]{:S(2)}, u32[]{:S(2)}) collective-permute-start(bf16[16,1024]{1,0:T(8,128)(2,1)S(1)} %get-tuple-element.63), channel_id=1, source_target_pairs={{0,7},{1,6},{2,5},{3,4},{4,3},{5,2},{6,1},{7,0},{8,15},{9,14},{10,... | collective-permute-start | bytes 98312 | tf_op jit(solution)/shard_map/ppermute | solution.py:15
  106.3 36.4 %collective-permute-start.40 = (bf16[128,1024]{1,0:T(8,128)(2,1)S(1)}, bf16[128,1024]{1,0:T(8,128)(2,1)S(1)}, u32[]{:S(2)}, u32[]{:S(2)}) collective-permute-start(bf16[128,1024]{1,0:T(8,128)(2,1)S(1)} %get-tuple-element.53), channel_id=1, source_target_pairs={{8,16},{16,8},{9,17},{17,9},{10,18},{18,10},{11,19},{19,11},{12,20... | collective-permute-start | bytes 786440 | tf_op jit(solution)/shard_map/ppermute | solution.py:143
  107.0 37.7 %collective-permute-start.39 = (bf16[128,1024]{1,0:T(8,128)(2,1)S(1)}, bf16[128,1024]{1,0:T(8,128)(2,1)S(1)}, u32[]{:S(2)}, u32[]{:S(2)}) collective-permute-start(bf16[128,1024]{1,0:T(8,128)(2,1)S(1)} %get-tuple-element.51), channel_id=1, source_target_pairs={{0,8},{8,0},{16,24},{24,16},{1,9},{9,1},{17,25},{25,17},{2,10},{10... | collective-permute-start | bytes 786440 | tf_op jit(solution)/shard_map/ppermute | solution.py:15
  114.0 2.2 %collective-permute-start.31 = (bf16[96,896]{1,0:T(8,128)(2,1)S(1)}, bf16[96,896]{1,0:T(8,128)(2,1)S(1)}, u32[]{:S(2)}, u32[]{:S(2)}) collective-permute-start(bf16[96,896]{1,0:T(8,128)(2,1)S(1)} %get-tuple-element.43), channel_id=1, source_target_pairs={{0,1},{1,0},{2,3},{3,2},{4,5},{5,4},{6,7},{7,6},{8,9},{9,8},{10,11... | collective-permute-start | bytes 516104 | tf_op jit(solution)/shard_map/ppermute | solution.py:15
  115.0 7.2 %collective-permute-start.32 = (bf16[96,896]{1,0:T(8,128)(2,1)S(1)}, bf16[96,896]{1,0:T(8,128)(2,1)S(1)}, u32[]{:S(2)}, u32[]{:S(2)}) collective-permute-start(bf16[96,896]{1,0:T(8,128)(2,1)S(1)} %get-tuple-element.44), channel_id=1, source_target_pairs={{0,2},{1,3},{2,0},{3,1},{4,6},{5,7},{6,4},{7,5},{8,10},{9,11},{10,... | collective-permute-start | bytes 516104 | tf_op jit(solution)/shard_map/ppermute | solution.py:15
  116.1 8.9 %collective-permute-start.33 = (bf16[96,896]{1,0:T(8,128)(2,1)S(1)}, bf16[96,896]{1,0:T(8,128)(2,1)S(1)}, u32[]{:S(2)}, u32[]{:S(2)}) collective-permute-start(bf16[96,896]{1,0:T(8,128)(2,1)S(1)} %get-tuple-element.45), channel_id=1, source_target_pairs={{0,3},{1,2},{2,1},{3,0},{4,7},{5,6},{6,5},{7,4},{8,11},{9,10},{10,... | collective-permute-start | bytes 516104 | tf_op jit(solution)/shard_map/ppermute | solution.py:15
  122.2 5.6 %collective-permute-start.34 = (bf16[96,896]{1,0:T(8,128)(2,1)S(1)}, bf16[96,896]{1,0:T(8,128)(2,1)S(1)}, u32[]{:S(2)}, u32[]{:S(2)}) collective-permute-start(bf16[96,896]{1,0:T(8,128)(2,1)S(1)} %get-tuple-element.46), channel_id=1, source_target_pairs={{0,4},{1,5},{2,6},{3,7},{4,0},{5,1},{6,2},{7,3},{8,12},{9,13},{10,... | collective-permute-start | bytes 516104 | tf_op jit(solution)/shard_map/ppermute | solution.py:15
  125.1 10.0 %collective-permute-start.35 = (bf16[96,896]{1,0:T(8,128)(2,1)S(1)}, bf16[96,896]{1,0:T(8,128)(2,1)S(1)}, u32[]{:S(2)}, u32[]{:S(2)}) collective-permute-start(bf16[96,896]{1,0:T(8,128)(2,1)S(1)} %get-tuple-element.47), channel_id=1, source_target_pairs={{0,5},{1,4},{2,7},{3,6},{4,1},{5,0},{6,3},{7,2},{8,13},{9,12},{10,... | collective-permute-start | bytes 516104 | tf_op jit(solution)/shard_map/ppermute | solution.py:15
  127.8 8.7 %collective-permute-start.36 = (bf16[96,896]{1,0:T(8,128)(2,1)S(1)}, bf16[96,896]{1,0:T(8,128)(2,1)S(1)}, u32[]{:S(2)}, u32[]{:S(2)}) collective-permute-start(bf16[96,896]{1,0:T(8,128)(2,1)S(1)} %get-tuple-element.48), channel_id=1, source_target_pairs={{0,6},{1,7},{2,4},{3,5},{4,2},{5,3},{6,0},{7,1},{8,14},{9,15},{10,... | collective-permute-start | bytes 516104 | tf_op jit(solution)/shard_map/ppermute | solution.py:15
  135.1 7.3 %collective-permute-start.37 = (bf16[96,896]{1,0:T(8,128)(2,1)S(1)}, bf16[96,896]{1,0:T(8,128)(2,1)S(1)}, u32[]{:S(2)}, u32[]{:S(2)}) collective-permute-start(bf16[96,896]{1,0:T(8,128)(2,1)S(1)} %get-tuple-element.49), channel_id=1, source_target_pairs={{0,7},{1,6},{2,5},{3,4},{4,3},{5,2},{6,1},{7,0},{8,15},{9,14},{10,... | collective-permute-start | bytes 516104 | tf_op jit(solution)/shard_map/ppermute | solution.py:15
  136.5 8.9 %collective-permute-start.43 = (bf16[128,1024]{1,0:T(8,128)(2,1)S(1)}, bf16[128,1024]{1,0:T(8,128)(2,1)S(1)}, u32[]{:S(2)}, u32[]{:S(2)}) collective-permute-start(bf16[128,1024]{1,0:T(8,128)(2,1)S(1)} %get-tuple-element.51), channel_id=1, source_target_pairs={{8,16},{16,8},{9,17},{17,9},{10,18},{18,10},{11,19},{19,11},{12,20... | collective-permute-start | bytes 786440 | tf_op jit(solution)/shard_map/ppermute | solution.py:143
  142.7 10.2 %collective-permute-start.41 = (bf16[128,1024]{1,0:T(8,128)(2,1)S(1)}, bf16[128,1024]{1,0:T(8,128)(2,1)S(1)}, u32[]{:S(2)}, u32[]{:S(2)}) collective-permute-start(bf16[128,1024]{1,0:T(8,128)(2,1)S(1)} %collective-permute-done.40), channel_id=1, source_target_pairs={{8,0},{16,24},{9,1},{17,25},{10,2},{18,26},{11,3},{19,27},{12,4},{... | collective-permute-start | bytes 786440 | tf_op jit(solution)/shard_map/ppermute | solution.py:146
  144.0 2.8 %collective-permute-start.42 = (bf16[128,1024]{1,0:T(8,128)(2,1)S(1)}, bf16[128,1024]{1,0:T(8,128)(2,1)S(1)}, u32[]{:S(2)}, u32[]{:S(2)}) collective-permute-start(bf16[128,1024]{1,0:T(8,128)(2,1)S(1)} %collective-permute-done.38), channel_id=1, source_target_pairs={{8,16},{16,8},{9,17},{17,9},{10,18},{18,10},{11,19},{19,11},{12,20... | collective-permute-start | bytes 786440 | tf_op jit(solution)/shard_map/ppermute | solution.py:144
  144.7 3.4 %collective-permute-start.45 = (bf16[128,1024]{1,0:T(8,128)(2,1)S(1)}, bf16[128,1024]{1,0:T(8,128)(2,1)S(1)}, u32[]{:S(2)}, u32[]{:S(2)}) collective-permute-start(bf16[128,1024]{1,0:T(8,128)(2,1)S(1)} %collective-permute-done.39), channel_id=1, source_target_pairs={{8,16},{16,8},{9,17},{17,9},{10,18},{18,10},{11,19},{19,11},{12,20... | collective-permute-start | bytes 786440 | tf_op jit(solution)/shard_map/ppermute | solution.py:144
  145.4 15.6 %collective-permute-start.44 = (bf16[128,1024]{1,0:T(8,128)(2,1)S(1)}, bf16[128,1024]{1,0:T(8,128)(2,1)S(1)}, u32[]{:S(2)}, u32[]{:S(2)}) collective-permute-start(bf16[128,1024]{1,0:T(8,128)(2,1)S(1)} %collective-permute-done.43), channel_id=1, source_target_pairs={{8,0},{16,24},{9,1},{17,25},{10,2},{18,26},{11,3},{19,27},{12,4},{... | collective-permute-start | bytes 786440 | tf_op jit(solution)/shard_map/ppermute | solution.py:146
  146.8 19.9 %collective-permute-start.46 = (bf16[128,1024]{1,0:T(8,128)(2,1)S(1)}, bf16[128,1024]{1,0:T(8,128)(2,1)S(1)}, u32[]{:S(2)}, u32[]{:S(2)}) collective-permute-start(bf16[128,1024]{1,0:T(8,128)(2,1)S(1)} %collective-permute-done.42), channel_id=1, source_target_pairs={{8,0},{16,24},{9,1},{17,25},{10,2},{18,26},{11,3},{19,27},{12,4},{... | collective-permute-start | bytes 786440 | tf_op jit(solution)/shard_map/ppermute | solution.py:147
  148.1 22.8 %collective-permute-start.47 = (bf16[128,1024]{1,0:T(8,128)(2,1)S(1)}, bf16[128,1024]{1,0:T(8,128)(2,1)S(1)}, u32[]{:S(2)}, u32[]{:S(2)}) collective-permute-start(bf16[128,1024]{1,0:T(8,128)(2,1)S(1)} %collective-permute-done.45), channel_id=1, source_target_pairs={{8,0},{16,24},{9,1},{17,25},{10,2},{18,26},{11,3},{19,27},{12,4},{... | collective-permute-start | bytes 786440 | tf_op jit(solution)/shard_map/ppermute | solution.py:147
  (9 other events, 49.1 us)

commit v2 on v0

v2 whole, which is shorter than its diff:
```python
import functools

import jax
import jax.numpy as jnp
from jax import lax
from jax.experimental import pallas as pl
from jax.experimental.pallas import tpu as pltpu
from jax.sharding import PartitionSpec as P

LANES = 128
TAIL = 16
F32, BF16 = jnp.float32, jnp.bfloat16
HBM = pl.BlockSpec(memory_space=pltpu.HBM)
VMEM = pl.BlockSpec(memory_space=pltpu.VMEM)
ANY = pl.BlockSpec(memory_space=pl.ANY)


def limit(mebibytes):
    return pltpu.CompilerParams(vmem_limit_bytes=mebibytes << 20)


def struct(*shape):
    return jax.ShapeDtypeStruct(shape, BF16)


def swap(value, axis, offset):
    count = lax.axis_size(axis)
    return lax.ppermute(value, axis, [(i, i ^ offset) for i in range(count)])


def hold_kernel(*refs):
    pass


def after(values, *others):
    return pl.pallas_call(
        hold_kernel,
        out_shape=[jax.ShapeDtypeStruct(value.shape, value.dtype) for value in values],
        in_specs=[ANY] * (len(values) + len(others)),
        out_specs=[ANY] * len(values),
        input_output_aliases={i: i for i in range(len(values))},
        compiler_params=limit(1),
        name="hold",
    )(*values, *others)


def fetch(pairs, sems):
    copies = [pltpu.make_async_copy(a, b, sems.at[i]) for i, (a, b) in enumerate(pairs)]
    for copy in copies:
        copy.start()
    return copies


def placing_of(ids, me, step, experts, slots):
    count = ids.shape[1]
    named = lax.broadcasted_iota(jnp.int32, (experts, count), 0) == ids
    earlier = (
        lax.broadcasted_iota(jnp.int32, (count, count), 0)
        < lax.broadcasted_iota(jnp.int32, (count, count), 1)
    ).astype(BF16)
    before = jnp.dot(named.astype(BF16), earlier, preferred_element_type=F32)
    rank = jnp.sum(jnp.where(named, before, 0.0), axis=0, keepdims=True).astype(jnp.int32)
    offset = ids ^ me
    row = jnp.where(offset % step == 0, (offset // step) * slots + rank, -1)
    return lax.broadcasted_iota(jnp.int32, (experts // step * slots, count), 0) == row


def columns(ref, index, share):
    if share % LANES == 0:
        return ref[:, pl.ds(pl.multiple_of(index * share, LANES), share)]
    value = ref[...]
    total = jnp.zeros((value.shape[0], share), value.dtype)
    for g in range(value.shape[1] // share):
        total = jnp.where(index == g, value[:, g * share : (g + 1) * share], total)
    return total


def place_kernel(sizes, *refs):
    experts, slots = sizes
    hbm, outs, scratch, sems = refs[:4], refs[4:-5], refs[-5:-1], refs[-1]
    for copy in fetch(list(zip(hbm, scratch)), sems):
        copy.wait()
    outs, cuts = outs[:experts], outs[experts:]
    ids_ref, gates_ref, cots_ref, tokens_ref = scratch
    count, width = tokens_ref.shape
    inner = cots_ref.shape[1]
    names = jnp.broadcast_to(ids_ref[...].astype(F32), (TAIL, count)).astype(BF16)
    group = lax.axis_index("dp")
    for k, out in enumerate(cuts):
        share = out.shape[1]
        out[:count, :] = columns(tokens_ref, group ^ (k + 1), share)
        out[count:, :count] = names
        if share > count:
            out[count:, count:] = jnp.zeros((TAIL, share - count), BF16)
    placing = placing_of(ids_ref[...], lax.axis_index("expert"), 1, experts, slots)
    one_hot = placing.astype(BF16)
    gate = jnp.sum(jnp.where(placing, gates_ref[...].astype(F32), 0.0), axis=1, keepdims=True)
    gate = jnp.broadcast_to(gate, (gate.shape[0], LANES)).astype(BF16)
    cots = jnp.dot(one_hot, cots_ref[...], preferred_element_type=F32).astype(BF16)
    rows = jnp.dot(one_hot, tokens_ref[...], preferred_element_type=F32).astype(BF16)
    for k, out in enumerate(outs):
        here = slice(k * slots, (k + 1) * slots)
        out[:, :width] = rows[here]
        out[:, width : width + inner] = cots[here]
        out[:, width + inner :] = gate[here]


def forward_kernel(sizes, weight_ref, *rest):
    experts, width, inner, share, parts = sizes
    pairs = experts // 2
    blocks, rest = rest[:experts], rest[experts + pairs :]
    sent, rest = rest[:pairs], rest[pairs:]
    dpre_refs, (own_ref, all_ref) = rest[:parts], rest[parts:]
    slots = blocks[0].shape[0]
    for k, block in enumerate(blocks):
        all_ref[k * slots : (k + 1) * slots, :] = block[...]
    pre = jnp.dot(all_ref[:, :width], weight_ref[0], preferred_element_type=F32)
    cots = all_ref[:, width : width + inner].astype(F32)
    gate = all_ref[:, width + inner :][:, :1].astype(F32)
    sig = jax.nn.sigmoid(pre)
    gated = gate * sig
    dpre = (cots * gated * (1.0 + pre * (1.0 - sig))).astype(BF16)
    height = dpre.shape[0] // parts
    for p, out in enumerate(dpre_refs):
        out[...] = dpre[p * height : (p + 1) * height]
    act = (gated * pre).astype(BF16)
    for j, out in enumerate(sent):
        out[:, out.shape[1] - inner :] = act[2 * j * slots : 2 * (j + 1) * slots]
    own_ref[...] = columns(all_ref.at[:, :width], lax.axis_index("dp"), share)


def share_kernel(sizes, *refs):
    experts, slots, groups, count = sizes
    pairs = experts // 2
    mine, theirs, outs = refs[:groups], refs[groups : 2 * groups], refs[-pairs:]
    share = mine[0].shape[1]
    for out in outs:
        out[:, groups * share :] = jnp.zeros_like(out[:, groups * share :])
    me = lax.axis_index("expert")
    for g in range(groups):
        placed = []
        for block in (mine[g], theirs[g]):
            ids = block[count:, :count][:1].astype(F32).astype(jnp.int32)
            one_hot = placing_of(ids, me, 2, experts, slots).astype(BF16)
            placed.append(
                jnp.dot(one_hot, block[:count, :], preferred_element_type=F32).astype(BF16)
            )
        for j, out in enumerate(outs):
            here = slice(j * slots, (j + 1) * slots)
            out[:, g * share : (g + 1) * share] = jnp.concatenate([p[here] for p in placed], axis=0)


def split_kernel(slots, inner, *refs):
    *blocks, out_ref = refs
    for j, block in enumerate(blocks):
        out_ref[j * slots : (j + 1) * slots] = block[slots:, block.shape[1] - inner :]


def unplace_kernel(sizes, ids_ref, theirs_ref, *refs):
    experts, slots = sizes
    *blocks, out_ref = refs
    inner = out_ref.shape[1]
    me = lax.axis_index("expert")
    mine = [block[:slots, block.shape[1] - inner :] for block in blocks]
    total = jnp.zeros(out_ref.shape, F32)
    for r, value in enumerate((jnp.concatenate(mine, axis=0), theirs_ref[...])):
        one_hot = placing_of(ids_ref[...], me ^ r, 2, experts, slots).astype(BF16)
        total = total + lax.dot_general(
            one_hot, value, (((0,), (0,)), ((), ())), preferred_element_type=F32
        )
    out_ref[...] = total.astype(BF16)


def turn_kernel(groups, own_ref, *refs):
    *blocks, out_ref = refs
    share, rows = out_ref.shape[0], own_ref.shape[0]
    out_ref[:, :rows] = own_ref[...].T
    for g in range(groups):
        value = [block[:, g * share : (g + 1) * share] for block in blocks]
        out_ref[:, (g + 1) * rows : (g + 2) * rows] = jnp.concatenate(value, axis=0).T


def sum_kernel(groups, left_ref, *refs):
    pieces, (out_ref, right_ref) = refs[:-2], refs[-2:]
    rows = left_ref.shape[1] // 4
    at = 0
    for piece in pieces:
        right_ref[at : at + piece.shape[0], :] = piece[...]
        at += piece.shape[0]
    total = jnp.zeros(out_ref.shape, F32)
    for i, g in enumerate(groups):
        total = total + jnp.dot(
            left_ref[:, g * rows : (g + 1) * rows],
            right_ref[i * rows : (i + 1) * rows, :],
            preferred_element_type=F32,
        )
    out_ref[...] = total


def grad_kernel(group, left_ref, before_ref, *refs):
    pieces, (out_hbm, right_ref, total_ref, sems) = refs[:-4], refs[-4:]
    rows = left_ref.shape[1] // 4
    at = 0
    for piece in pieces:
        right_ref[at : at + piece.shape[0], :] = piece[...]
        at += piece.shape[0]
    steps, tall = total_ref.shape[:2]
    copies = []
    for i in range(steps):
        here = slice(i * tall, (i + 1) * tall)
        total_ref[i] = before_ref[here, :] + jnp.dot(
            left_ref[here, group * rows : (group + 1) * rows],
            right_ref[...],
            preferred_element_type=F32,
        )
        copies.append(pltpu.make_async_copy(total_ref.at[i], out_hbm.at[here, :], sems.at[i]))
        copies[-1].start()
    for copy in copies:
        copy.wait()


def on_device(tokens, expert_ids, gates, cotangent, weights):
    experts, members = lax.axis_size("expert"), lax.axis_size("dp")
    group = lax.axis_index("dp")
    pairs, groups = experts // 2, members - 1
    count, width = tokens.shape
    inner = cotangent.shape[1]
    share = width // members
    slots = max(2, 2 * count // experts)
    rows = experts * slots
    wide = width + inner + LANES
    chain = slots % 16 == 0 and share % LANES == 0 and members == 4
    ids, gates = expert_ids.reshape(1, count), gates.reshape(1, count)

    mine = (ids, gates, cotangent, tokens)
    placed = pl.pallas_call(
        functools.partial(place_kernel, (experts, slots)),
        out_shape=[struct(slots, wide)] * experts + [struct(count + TAIL, share)] * groups,
        in_specs=[HBM] * 4,
        out_specs=[VMEM] * (experts + groups),
        scratch_shapes=[pltpu.VMEM(value.shape, value.dtype) for value in mine]
        + [pltpu.SemaphoreType.DMA((4,))],
        compiler_params=limit(BIG),
        name="place",
    )(*mine)
    placed, cuts = placed[:experts], placed[experts:]
    got = list(placed)
    for k in range(2, experts, 2):
        got[k] = swap(placed[k], "expert", k)
    for k, value in zip(range(1, experts, 2), after(placed[1::2], *got[2::2])):
        got[k] = swap(value, "expert", k)
    cuts = [swap(cut, "dp", k + 1) for k, cut in enumerate(cuts)]

    sent = pl.pallas_call(
        functools.partial(share_kernel, (experts, slots, groups, count)),
        out_shape=[struct(2 * slots, groups * share + inner)] * pairs,
        in_specs=[VMEM] * (1 + 2 * groups),
        out_specs=[VMEM] * pairs,
        compiler_params=limit(SMALL),
        name="place_shares",
    )(*cuts, *[swap(cut, "expert", 1) for cut in cuts], weights)
    sent, dpres, own = (lambda a: (a[:pairs], list(a[pairs:-1]), a[-1]))(
        pl.pallas_call(
            functools.partial(forward_kernel, (experts, width, inner, share, PARTS)),
            out_shape=[struct(2 * slots, groups * share + inner)] * pairs
            + [struct(rows // PARTS, inner)] * PARTS
            + [struct(rows, share)],
            in_specs=[VMEM] * (1 + experts + pairs),
            out_specs=[VMEM] * (1 + pairs + PARTS),
            input_output_aliases={1 + experts + j: j for j in range(pairs)},
            scratch_shapes=[pltpu.VMEM((rows, wide), BF16)],
            compiler_params=limit(SMALL),
            name="forward",
        )(weights, *got, *sent)
    )

    gathered = [[] for _ in range(groups)]
    for value in dpres:
        for k in range(1, members):
            if not (chain and k == 2):
                gathered[k - 1].append(swap(value, "dp", k))
    if chain:
        ends = (group == 0) | (group == 3)
        for value, far in zip(dpres, gathered[2]):
            value = jnp.where(ends, value, far)
            gathered[1].append(lax.ppermute(value, "dp", [(0, 2), (1, 0), (2, 3), (3, 1)]))

    lefts = [sent[0]] + [swap(sent[j], "expert", 2 * j) for j in range(1, pairs)]
    theirs = pl.pallas_call(
        functools.partial(split_kernel, slots, inner),
        out_shape=struct(pairs * slots, inner),
        in_specs=[VMEM] * pairs,
        out_specs=VMEM,
        compiler_params=limit(SMALL),
        name="split",
    )(*lefts)
    hidden = pl.pallas_call(
        functools.partial(unplace_kernel, (experts, slots)),
        out_shape=struct(count, inner),
        in_specs=[VMEM] * (2 + pairs),
        out_specs=VMEM,
        compiler_params=limit(SMALL),
        name="unplace",
    )(ids, swap(theirs, "expert", 1), *lefts)

    if chain:
        left = pl.pallas_call(
            functools.partial(turn_kernel, groups),
            out_shape=struct(share, members * rows),
            in_specs=[VMEM] * (1 + pairs),
            out_specs=VMEM,
            compiler_params=limit(SMALL),
            name="turn",
        )(own, *lefts)
        pieces = [*dpres] + gathered[0] + gathered[2]
        before = pl.pallas_call(
            functools.partial(sum_kernel, (0, 1, 3)),
            out_shape=jax.ShapeDtypeStruct((share, inner), F32),
            in_specs=[VMEM] * (1 + len(pieces)),
            out_specs=VMEM,
            scratch_shapes=[pltpu.VMEM((3 * rows, inner), BF16)],
            compiler_params=limit(SMALL),
            name="sum",
        )(left, *pieces)
        steps = 2
        grad = pl.pallas_call(
            functools.partial(grad_kernel, 2),
            out_shape=jax.ShapeDtypeStruct((share, inner), F32),
            in_specs=[VMEM] * (2 + len(dpres)),
            out_specs=HBM,
            scratch_shapes=[
                pltpu.VMEM((rows, inner), BF16),
                pltpu.VMEM((steps, share // steps, inner), F32),
                pltpu.SemaphoreType.DMA((steps,)),
            ],
            compiler_params=limit(SMALL),
            name="grad",
        )(left, before, *gathered[1])
        return (hidden, grad[None])
    left, right = [own], list(dpres)
    for g in range(groups):
        left += [block[:, g * share : (g + 1) * share] for block in lefts]
        right += gathered[g]
    grad = lax.dot_general(
        jnp.concatenate(left, axis=0),
        jnp.concatenate(right, axis=0),
        (((0,), (0,)), ((), ())),
        preferred_element_type=F32,
    )
    return (hidden, grad[None])


BIG, SMALL, PARTS = 40, 12, 1


def solution(mesh):
    return jax.shard_map(
        on_device,
        mesh=mesh,
        in_specs=(
            P(("dp", "expert"), None),
            P(("dp", "expert"), None),
            P(("dp", "expert")),
            P(("dp", "expert"), None),
            P("expert", None, None),
        ),
        out_specs=(P(("dp", "expert"), None), P("expert", "dp", None)),
        check_vma=False,
    )
```

time: 185 us -> 92.7 us (0.50)
  waiting for transfers between devices: 112 us -> 35.8 us
  matrix products: 29.9 us -> 0 us
  starting transfers between devices: 20.7 us -> 38.8 us
  between operations: 14.1 us -> 0.77 us
  Pallas kernels: 0 us -> 10.5 us
  other arithmetic: 2.51 us -> 0.06 us
    all_to_all x5 -> x0, waiting for transfers between devices: 112 us -> none  [the longest x1 73 us: on_device(): sliced = lax.all_to_all(rows, 'dp', split_axis=1, concat_axis=0, tiled=True)]
    ppermute x0 -> x20, starting transfers between devices: none -> 38.8 us  [the longest x19 25.2 us: swap(): return lax.ppermute(value, axis, [(i, i ^ offset) for i in range(count)])]
    ppermute x0 -> x20, waiting for transfers between devices: none -> 35.8 us  [the longest x19 27.9 us: swap(): return lax.ppermute(value, axis, [(i, i ^ offset) for i in range(count)])]
    dot_general x9 -> x0, matrix products: 29.9 us -> none  [the longest x4 17.7 us: add_member(): lax.dot_general(left, right, (((0,), (0,)), ((), ())), preferred_element_...]
    all_to_all x5 -> x0, starting transfers between devices: 20.6 us -> none  [the longest x1 5.17 us: on_device(): lax.all_to_all(g_slots, 'expert', split_axis=0, concat_axis=0, tiled=True)]
    pallas_call x0 -> x9, Pallas kernels: none -> 10.5 us  [the longest x1 2.39 us: on_device(): pl.pallas_call(functools.partial(forward_kernel, (experts, width, inner,...]
    unnamed x2 -> x14, local copies, waits for them, and re-layouts: 0.01 us -> 6.52 us
    all_to_all x3 -> x0, local copies, waits for them, and re-layouts: 5.09 us -> none  [the longest x2 4.39 us: on_device(): sliced = lax.all_to_all(rows, 'dp', split_axis=1, concat_axis=0, tiled=True)]
  transfers between devices with their start and end apart: 6 -> 20, of which waited for: 5 -> 7; matrix products, arithmetic and copies ran while one was open for 4% -> 0% of each run, Pallas kernels for 0% -> 5%
where the time goes in v2:
time: 92.7 us; the launch traced here: 92.5 us
  starting transfers between devices  38.8 us (42%)
  waiting for transfers between devices  35.8 us (39%)
  Pallas kernels  10.5 us (11%)
  local copies, waits for them, and re-layouts  6.52 us (7%)
    ppermute x19, waiting for transfers between devices, swap(): return lax.ppermute(value, axis, [(i, i ^ offset) for i in range(count)])  27.9 us
    ppermute x19, starting transfers between devices, swap(): return lax.ppermute(value, axis, [(i, i ^ offset) for i in range(count)])  25.2 us
    ppermute x1, starting transfers between devices, on_device(): lax.ppermute(value, 'dp', [(0, 2), (1, 0), (2, 3), (3, 1)])  13.6 us
    ppermute x1, waiting for transfers between devices, on_device(): lax.ppermute(value, 'dp', [(0, 2), (1, 0), (2, 3), (3, 1)])  7.87 us
    unnamed x14, local copies, waits for them, and re-layouts  6.52 us
    pallas_call x1, Pallas kernels, on_device(): pl.pallas_call(functools.partial(forward_kernel, (experts, width, inner,...  2.39 us
    pallas_call x1, Pallas kernels, on_device(): pl.pallas_call(functools.partial(grad_kernel, 2), out_shape=jax.ShapeDtyp...  2.25 us
  transfers between devices with their start and end apart: 20, of which 7 were waited for; matrix products, arithmetic and copies ran while one was open for 0% of the time, Pallas kernels for 5%

profile of v2, /device:TPU:0, one launch (start us, length us, event | category | flops | bytes accessed | tf_op | source)
XLA Modules:
  0.0 92.5 jit_solution(1390956328616528089)
XLA Ops:
  0.6 1.2 %copy-done.2 = bf16[128,3584]{1,0:T(8,128)(2,1)S(1)} copy-done((bf16[128,3584]{1,0:T(8,128)(2,1)S(1)}, bf16[128,3584]{1,0:T(8,128)(2,1)}, u32[]{:S(2)}) %copy-start.2) | copy-done | bytes 917528
  1.8 0.9 %copy-done.3 = bf16[128,1024]{1,0:T(8,128)(2,1)S(1)} copy-done((bf16[128,1024]{1,0:T(8,128)(2,1)S(1)}, bf16[128,1024]{1,0:T(8,128)(2,1)}, u32[]{:S(2)}) %copy-start.3) | copy-done | bytes 262168
  2.8 0.7 copy-done.4
  3.4 0.7 copy-done.6
  4.1 1.2 %place.1 = (bf16[32,4736]{1,0:T(8,128)(2,1)S(1)}, bf16[32,4736]{1,0:T(8,128)(2,1)S(1)}, bf16[32,4736]{1,0:T(8,128)(2,1)S(1)}, bf16[32,4736]{1,0:T(8,128)(2,1)S(1...) custom-call(s32[1,128]{1,0:T(1,128)S(1)} %bitcast.3, ...), custom_call_target="tpu_custom_call" | custom-call | tf_op jit(solution)/shard_map/place/pallas_call | solution.py:236
  5.3 3.0 %collective-permute-start = (bf16[32,4736]{1,0:T(8,128)(2,1)S(1)}, bf16[32,4736]{1,0:T(8,128)(2,1)S(1)}, u32[]{:S(2)}, u32[]{:S(2)}) collective-permute-start(bf16[32,4736]{1,0:T(8,128)(2,1)S(1)} %get-tuple-element.32), channel_id=1, source_target_pairs={{0,2},{1,3},{2,0},{3,1},{4,6},{5,7},{6,4},{7,5},{8,10},{9,11},{10,... | collective-permute-start | bytes 909320 | tf_op jit(solution)/shard_map/ppermute | solution.py:28
  8.3 1.6 %collective-permute-start.7 = (bf16[144,896]{1,0:T(8,128)(2,1)S(1)}, bf16[144,896]{1,0:T(8,128)(2,1)S(1)}, u32[]{:S(2)}, u32[]{:S(2)}) collective-permute-start(bf16[144,896]{1,0:T(8,128)(2,1)S(1)} %get-tuple-element.39), channel_id=1, source_target_pairs={{0,8},{8,0},{16,24},{24,16},{1,9},{9,1},{17,25},{25,17},{2,10},{10... | collective-permute-start | bytes 774152 | tf_op jit(solution)/shard_map/ppermute | solution.py:28
  9.8 2.6 %collective-permute-start.8 = (bf16[144,896]{1,0:T(8,128)(2,1)S(1)}, bf16[144,896]{1,0:T(8,128)(2,1)S(1)}, u32[]{:S(2)}, u32[]{:S(2)}) collective-permute-start(bf16[144,896]{1,0:T(8,128)(2,1)S(1)} %get-tuple-element.40), channel_id=1, source_target_pairs={{0,16},{8,24},{16,0},{24,8},{1,17},{9,25},{17,1},{25,9},{2,18},{10... | collective-permute-start | bytes 774152 | tf_op jit(solution)/shard_map/ppermute | solution.py:28
  12.4 1.5 %collective-permute-start.1 = (bf16[32,4736]{1,0:T(8,128)(2,1)S(1)}, bf16[32,4736]{1,0:T(8,128)(2,1)S(1)}, u32[]{:S(2)}, u32[]{:S(2)}) collective-permute-start(bf16[32,4736]{1,0:T(8,128)(2,1)S(1)} %get-tuple-element.33), channel_id=1, source_target_pairs={{0,4},{1,5},{2,6},{3,7},{4,0},{5,1},{6,2},{7,3},{8,12},{9,13},{10,... | collective-permute-start | bytes 909320 | tf_op jit(solution)/shard_map/ppermute | solution.py:28
  14.0 0.5 collective-permute-start.2
  14.4 6.9 %collective-permute-done.7.refs_0_ = bf16[144,896]{1,0:T(8,128)(2,1)S(1)} collective-permute-done((bf16[144,896]{1,0:T(8,128)(2,1)S(1)}, bf16[144,896]{1,0:T(8,128)(2,1)S(1)}, u32[]{:S(2)}, u32[]{:S(2)}) %collective-permute-start.7) | collective-permute-done | bytes 258080 | tf_op jit(solution)/shard_map/ppermute | solution.py:28
  21.4 2.5 %collective-permute-start.9 = (bf16[144,896]{1,0:T(8,128)(2,1)S(1)}, bf16[144,896]{1,0:T(8,128)(2,1)S(1)}, u32[]{:S(2)}, u32[]{:S(2)}) collective-permute-start(bf16[144,896]{1,0:T(8,128)(2,1)S(1)} %get-tuple-element.41), channel_id=1, source_target_pairs={{0,24},{8,16},{16,8},{24,0},{1,25},{9,17},{17,9},{25,1},{2,26},{10... | collective-permute-start | bytes 774152 | tf_op jit(solution)/shard_map/ppermute | solution.py:28
  23.8 0.0 collective-permute-done.8.refs_1_
  23.8 0.0 collective-permute-start.10
  23.8 0.5 collective-permute-start.11
  24.4 2.7 %collective-permute-done.1.refs_5_.rest_4_ = bf16[32,4736]{1,0:T(8,128)(2,1)S(1)} collective-permute-done((bf16[32,4736]{1,0:T(8,128)(2,1)S(1)}, bf16[32,4736]{1,0:T(8,128)(2,1)S(1)}, u32[]{:S(2)}, u32[]{:S(2)}) %collective-permute-start.1) | collective-permute-done | bytes 303136 | tf_op jit(solution)/shard_map/ppermute | solution.py:28
  27.0 0.0 collective-permute-done.2.refs_6_.rest_6_
  27.0 0.6 collective-permute-start.4
  27.7 2.4 %collective-permute-done.9.refs_2_ = bf16[144,896]{1,0:T(8,128)(2,1)S(1)} collective-permute-done((bf16[144,896]{1,0:T(8,128)(2,1)S(1)}, bf16[144,896]{1,0:T(8,128)(2,1)S(1)}, u32[]{:S(2)}, u32[]{:S(2)}) %collective-permute-start.9) | collective-permute-done | bytes 258080 | tf_op jit(solution)/shard_map/ppermute | solution.py:28
  30.0 0.0 collective-permute-done.10.refs_3_
  30.0 1.9 %collective-permute-start.6 = (bf16[32,4736]{1,0:T(8,128)(2,1)S(1)}, bf16[32,4736]{1,0:T(8,128)(2,1)S(1)}, u32[]{:S(2)}, u32[]{:S(2)}) collective-permute-start(bf16[32,4736]{1,0:T(8,128)(2,1)S(1)} %get-tuple-element.38), channel_id=1, source_target_pairs={{0,7},{1,6},{2,5},{3,4},{4,3},{5,2},{6,1},{7,0},{8,15},{9,14},{10,... | collective-permute-start | bytes 909320 | tf_op jit(solution)/shard_map/ppermute | solution.py:28
  31.9 0.0 collective-permute-done.11.refs_4_
  31.9 0.0 collective-permute-start.12
  31.9 1.5 %collective-permute-done.12.refs_5_ = bf16[144,896]{1,0:T(8,128)(2,1)S(1)} collective-permute-done((bf16[144,896]{1,0:T(8,128)(2,1)S(1)}, bf16[144,896]{1,0:T(8,128)(2,1)S(1)}, u32[]{:S(2)}, u32[]{:S(2)}) %collective-permute-start.12) | collective-permute-done | bytes 258080 | tf_op jit(solution)/shard_map/ppermute | solution.py:28
  33.4 3.1 %copy-done = bf16[1,3584,1024]{2,1,0:T(8,128)(2,1)S(1)} copy-done((bf16[1,3584,1024]{2,1,0:T(8,128)(2,1)S(1)}, bf16[1,3584,1024]{2,1,0:T(8,128)(2,1)}, u32[]{:S(2)}) %copy-start) | copy-done | bytes 7340056
  36.5 1.3 %place_shares.1 = (bf16[64,3712]{1,0:T(8,128)(2,1)S(1)}, bf16[64,3712]{1,0:T(8,128)(2,1)S(1)}, bf16[64,3712]{1,0:T(8,128)(2,1)S(1)}, bf16[64,3712]{1,0:T(8,128)(2,1)S(1)}) custom-call(bf16[144,896]{1,0:T(8,128)(2,1)S(1)} %collective-permute-done.7.refs_0_, bf16[144,896]{1,0:T(8,128)(2,1)S(1)} %collective-permute-done.8.refs_1_, ...), custom_call_target="tpu_custom_call" | custom-call | tf_op jit(solution)/shard_map/place_shares/pallas_call | solution.py:254
  37.9 0.0 collective-permute-done.3.rest_1_
  37.9 8.1 %collective-permute-done.5.rest_5_ = bf16[32,4736]{1,0:T(8,128)(2,1)S(1)} collective-permute-done((bf16[32,4736]{1,0:T(8,128)(2,1)S(1)}, bf16[32,4736]{1,0:T(8,128)(2,1)S(1)}, u32[]{:S(2)}, u32[]{:S(2)}) %collective-permute-start.5) | collective-permute-done | bytes 303136 | tf_op jit(solution)/shard_map/ppermute | solution.py:28
  45.9 0.0 collective-permute-done.6.rest_7_
  45.9 2.4 %forward.1 = (bf16[64,3712]{1,0:T(8,128)(2,1)S(1)}, bf16[64,3712]{1,0:T(8,128)(2,1)S(1)}, bf16[64,3712]{1,0:T(8,128)(2,1)S(1)}, bf16[64,3712]{1,0:T(8,128)(2,1)S...) custom-call(bf16[1,3584,1024]{2,1,0:T(8,128)(2,1)S(1)} %copy-done.1,, ...), custom_call_target="tpu_custom_call", output_to_operand_aliasing={{0}: (9, {}), {1}: (10, {}), {2}: (11, {}), {3}: (12, {})} | custom-call | tf_op jit(solution)/shard_map/forward/pallas_call | solution.py:263
  48.3 4.0 %collective-permute-start.18 = (bf16[256,1024]{1,0:T(8,128)(2,1)S(1)}, bf16[256,1024]{1,0:T(8,128)(2,1)S(1)}, u32[]{:S(2)}, u32[]{:S(2)}) collective-permute-start(bf16[256,1024]{1,0:T(8,128)(2,1)S(1)} %get-tuple-element.51.refs_0_), channel_id=1, source_target_pairs={{0,24},{8,16},{16,8},{24,0},{1,25},{9,17},{17,9},{25,1},{2,26},{10... | collective-permute-start | bytes 1572872 | tf_op jit(solution)/shard_map/ppermute | solution.py:28
  52.3 3.0 %collective-permute-start.17 = (bf16[256,1024]{1,0:T(8,128)(2,1)S(1)}, bf16[256,1024]{1,0:T(8,128)(2,1)S(1)}, u32[]{:S(2)}, u32[]{:S(2)}) collective-permute-start(bf16[256,1024]{1,0:T(8,128)(2,1)S(1)} %get-tuple-element.51.refs_0_), channel_id=1, source_target_pairs={{0,8},{8,0},{16,24},{24,16},{1,9},{9,1},{17,25},{25,17},{2,10},{10... | collective-permute-start | bytes 1572872 | tf_op jit(solution)/shard_map/ppermute | solution.py:28
  55.3 0.5 collective-permute-start.13
  55.8 0.7 collective-permute-start.14
  56.5 2.2 %collective-permute-start.15 = (bf16[64,3712]{1,0:T(8,128)(2,1)S(1)}, bf16[64,3712]{1,0:T(8,128)(2,1)S(1)}, u32[]{:S(2)}, u32[]{:S(2)}) collective-permute-start(bf16[64,3712]{1,0:T(8,128)(2,1)S(1)} %get-tuple-element.49), channel_id=1, source_target_pairs={{0,6},{1,7},{2,4},{3,5},{4,2},{5,3},{6,0},{7,1},{8,14},{9,15},{10,... | collective-permute-start | bytes 1425416 | tf_op jit(solution)/shard_map/ppermute | solution.py:28
  58.8 6.4 %collective-permute-done.18.refs_2_ = bf16[256,1024]{1,0:T(8,128)(2,1)S(1)} collective-permute-done((bf16[256,1024]{1,0:T(8,128)(2,1)S(1)}, bf16[256,1024]{1,0:T(8,128)(2,1)S(1)}, u32[]{:S(2)}, u32[]{:S(2)}) %collective-permute-start.18) | collective-permute-done | bytes 524320 | tf_op jit(solution)/shard_map/ppermute | solution.py:28
  65.2 0.1 broadcast_select_fusion
  65.2 13.6 %collective-permute-start.19 = (bf16[256,1024]{1,0:T(8,128)(2,1)S(1)}, bf16[256,1024]{1,0:T(8,128)(2,1)S(1)}, u32[]{:S(2)}, u32[]{:S(2)}) collective-permute-start(bf16[256,1024]{1,0:T(8,128)(2,1)S(1)} %broadcast_select_fusion), channel_id=1, source_target_pairs={{0,16},{8,0},{16,24},{24,8},{1,17},{9,1},{17,25},{25,9},{2,18},{10... | collective-permute-start | bytes 1572872 | tf_op jit(solution)/shard_map/ppermute | solution.py:286
  78.8 0.0 collective-permute-done.13.refs_1_
  78.8 0.0 collective-permute-done.14.refs_2_
  78.8 0.0 collective-permute-done.15.refs_3_
  78.9 0.1 collective-permute-start.16
  79.0 0.6 turn.1.left_ref
  79.5 0.0 copy-start.5
  79.5 1.6 %sum.1.before_ref = f32[896,1024]{1,0:T(8,128)S(1)} custom-call(bf16[896,1024]{1,0:T(8,128)(2,1)S(1)} %turn.1.left_ref, bf16[256,1024]{1,0:T(8,128)(2,1)S(1)} %get-tuple-element.51.refs_0_, bf16[256,1024]{1,0:T(8,128)(2,1)S(1)} %collective-permute-done.17.refs_1_, bf16[256,1024]{1,0:T(8,128)(2,1)S(1)} %collective-permute-done.18.refs_2_), custom_call_target="tpu_custom_call" | custom-call | tf_op jit(solution)/shard_map/sum/pallas_call | solution.py:316
  81.2 1.2 %unplace.1 = bf16[128,1024]{1,0:T(8,128)(2,1)} custom-call(s32[1,128]{1,0:T(1,128)S(1)} %bitcast.4, bf16[128,1024]{1,0:T(8,128)(2,1)S(1)} %collective-permute-done.16.theirs_ref, bf16[64,3712]{1,0:T(8,128)(2,1)S(1)} %get-tuple-element.46.refs_0_, bf16[64,3712]{1,0:T(8,128)(2,1)S(1)} %collective-permute-done.13.refs_1_, ...), custom_call_target="tpu_custom_call" | custom-call | tf_op jit(solution)/shard_map/unplace/pallas_call | solution.py:297
  82.3 7.9 %collective-permute-done.19.refs_0_ = bf16[256,1024]{1,0:T(8,128)(2,1)S(1)} collective-permute-done((bf16[256,1024]{1,0:T(8,128)(2,1)S(1)}, bf16[256,1024]{1,0:T(8,128)(2,1)S(1)}, u32[]{:S(2)}, u32[]{:S(2)}) %collective-permute-start.19) | collective-permute-done | bytes 524320 | tf_op jit(solution)/shard_map/ppermute | solution.py:286
  90.2 2.3 %grad.1 = f32[896,1024]{1,0:T(8,128)} custom-call(bf16[896,1024]{1,0:T(8,128)(2,1)S(1)} %turn.1.left_ref, f32[896,1024]{1,0:T(8,128)S(1)} %sum.1.before_ref, bf16[256,1024]{1,0:T(8,128)(2,1)S(1)} %collective-permute-done.19.refs_0_), custom_call_target="tpu_custom_call" | custom-call | tf_op jit(solution)/shard_map/grad/pallas_call | solution.py:326
  (16 shorter events, 0.1 us)
Async XLA Ops:
  0.6 1.2 %copy-start.2 = (bf16[128,3584]{1,0:T(8,128)(2,1)S(1)}, bf16[128,3584]{1,0:T(8,128)(2,1)}, u32[]{:S(2)}) copy-start(bf16[128,3584]{1,0:T(8,128)(2,1)} %refs_3_.1) | copy-start | bytes 2752516
  1.8 0.9 %copy-start.3 = (bf16[128,1024]{1,0:T(8,128)(2,1)S(1)}, bf16[128,1024]{1,0:T(8,128)(2,1)}, u32[]{:S(2)}) copy-start(bf16[128,1024]{1,0:T(8,128)(2,1)} %refs_2_.1) | copy-start | bytes 786436
  2.8 0.7 copy-start.4
  3.4 0.7 copy-start.6
  5.3 18.6 %collective-permute-start = (bf16[32,4736]{1,0:T(8,128)(2,1)S(1)}, bf16[32,4736]{1,0:T(8,128)(2,1)S(1)}, u32[]{:S(2)}, u32[]{:S(2)}) collective-permute-start(bf16[32,4736]{1,0:T(8,128)(2,1)S(1)} %get-tuple-element.32), channel_id=1, source_target_pairs={{0,2},{1,3},{2,0},{3,1},{4,6},{5,7},{6,4},{7,5},{8,10},{9,11},{10,... | collective-permute-start | bytes 909320 | tf_op jit(solution)/shard_map/ppermute | solution.py:28
  8.3 13.1 %collective-permute-start.7 = (bf16[144,896]{1,0:T(8,128)(2,1)S(1)}, bf16[144,896]{1,0:T(8,128)(2,1)S(1)}, u32[]{:S(2)}, u32[]{:S(2)}) collective-permute-start(bf16[144,896]{1,0:T(8,128)(2,1)S(1)} %get-tuple-element.39), channel_id=1, source_target_pairs={{0,8},{8,0},{16,24},{24,16},{1,9},{9,1},{17,25},{25,17},{2,10},{10... | collective-permute-start | bytes 774152 | tf_op jit(solution)/shard_map/ppermute | solution.py:28
  9.8 14.0 %collective-permute-start.8 = (bf16[144,896]{1,0:T(8,128)(2,1)S(1)}, bf16[144,896]{1,0:T(8,128)(2,1)S(1)}, u32[]{:S(2)}, u32[]{:S(2)}) collective-permute-start(bf16[144,896]{1,0:T(8,128)(2,1)S(1)} %get-tuple-element.40), channel_id=1, source_target_pairs={{0,16},{8,24},{16,0},{24,8},{1,17},{9,25},{17,1},{25,9},{2,18},{10... | collective-permute-start | bytes 774152 | tf_op jit(solution)/shard_map/ppermute | solution.py:28
  12.4 14.6 %collective-permute-start.1 = (bf16[32,4736]{1,0:T(8,128)(2,1)S(1)}, bf16[32,4736]{1,0:T(8,128)(2,1)S(1)}, u32[]{:S(2)}, u32[]{:S(2)}) collective-permute-start(bf16[32,4736]{1,0:T(8,128)(2,1)S(1)} %get-tuple-element.33), channel_id=1, source_target_pairs={{0,4},{1,5},{2,6},{3,7},{4,0},{5,1},{6,2},{7,3},{8,12},{9,13},{10,... | collective-permute-start | bytes 909320 | tf_op jit(solution)/shard_map/ppermute | solution.py:28
  14.0 13.1 %collective-permute-start.2 = (bf16[32,4736]{1,0:T(8,128)(2,1)S(1)}, bf16[32,4736]{1,0:T(8,128)(2,1)S(1)}, u32[]{:S(2)}, u32[]{:S(2)}) collective-permute-start(bf16[32,4736]{1,0:T(8,128)(2,1)S(1)} %get-tuple-element.34), channel_id=1, source_target_pairs={{0,6},{1,7},{2,4},{3,5},{4,2},{5,3},{6,0},{7,1},{8,14},{9,15},{10,... | collective-permute-start | bytes 909320 | tf_op jit(solution)/shard_map/ppermute | solution.py:28
  21.4 8.7 %collective-permute-start.9 = (bf16[144,896]{1,0:T(8,128)(2,1)S(1)}, bf16[144,896]{1,0:T(8,128)(2,1)S(1)}, u32[]{:S(2)}, u32[]{:S(2)}) collective-permute-start(bf16[144,896]{1,0:T(8,128)(2,1)S(1)} %get-tuple-element.41), channel_id=1, source_target_pairs={{0,24},{8,16},{16,8},{24,0},{1,25},{9,17},{17,9},{25,1},{2,26},{10... | collective-permute-start | bytes 774152 | tf_op jit(solution)/shard_map/ppermute | solution.py:28
  23.8 6.2 %collective-permute-start.10 = (bf16[144,896]{1,0:T(8,128)(2,1)S(1)}, bf16[144,896]{1,0:T(8,128)(2,1)S(1)}, u32[]{:S(2)}, u32[]{:S(2)}) collective-permute-start(bf16[144,896]{1,0:T(8,128)(2,1)S(1)} %collective-permute-done.7.refs_0_), channel_id=1, source_target_pairs={{0,1},{1,0},{2,3},{3,2},{4,5},{5,4},{6,7},{7,6},{8,9},{9,8},{10,11... | collective-permute-start | bytes 774152 | tf_op jit(solution)/shard_map/ppermute | solution.py:28
  23.8 8.1 %collective-permute-start.11 = (bf16[144,896]{1,0:T(8,128)(2,1)S(1)}, bf16[144,896]{1,0:T(8,128)(2,1)S(1)}, u32[]{:S(2)}, u32[]{:S(2)}) collective-permute-start(bf16[144,896]{1,0:T(8,128)(2,1)S(1)} %collective-permute-done.8.refs_1_), channel_id=1, source_target_pairs={{0,1},{1,0},{2,3},{3,2},{4,5},{5,4},{6,7},{7,6},{8,9},{9,8},{10,11... | collective-permute-start | bytes 774152 | tf_op jit(solution)/shard_map/ppermute | solution.py:28
  27.0 10.8 %collective-permute-start.3 = (bf16[32,4736]{1,0:T(8,128)(2,1)S(1)}, bf16[32,4736]{1,0:T(8,128)(2,1)S(1)}, u32[]{:S(2)}, u32[]{:S(2)}) collective-permute-start(bf16[32,4736]{1,0:T(8,128)(2,1)S(1)} %get-tuple-element.35), channel_id=1, source_target_pairs={{0,1},{1,0},{2,3},{3,2},{4,5},{5,4},{6,7},{7,6},{8,9},{9,8},{10,11... | collective-permute-start | bytes 909320 | tf_op jit(solution)/shard_map/ppermute | solution.py:28
  27.0 10.9 %collective-permute-start.4 = (bf16[32,4736]{1,0:T(8,128)(2,1)S(1)}, bf16[32,4736]{1,0:T(8,128)(2,1)S(1)}, u32[]{:S(2)}, u32[]{:S(2)}) collective-permute-start(bf16[32,4736]{1,0:T(8,128)(2,1)S(1)} %get-tuple-element.36), channel_id=1, source_target_pairs={{0,3},{1,2},{2,1},{3,0},{4,7},{5,6},{6,5},{7,4},{8,11},{9,10},{10,... | collective-permute-start | bytes 909320 | tf_op jit(solution)/shard_map/ppermute | solution.py:28
  30.0 15.9 %collective-permute-start.5 = (bf16[32,4736]{1,0:T(8,128)(2,1)S(1)}, bf16[32,4736]{1,0:T(8,128)(2,1)S(1)}, u32[]{:S(2)}, u32[]{:S(2)}) collective-permute-start(bf16[32,4736]{1,0:T(8,128)(2,1)S(1)} %get-tuple-element.37), channel_id=1, source_target_pairs={{0,5},{1,4},{2,7},{3,6},{4,1},{5,0},{6,3},{7,2},{8,13},{9,12},{10,... | collective-permute-start | bytes 909320 | tf_op jit(solution)/shard_map/ppermute | solution.py:28
  30.0 15.9 %collective-permute-start.6 = (bf16[32,4736]{1,0:T(8,128)(2,1)S(1)}, bf16[32,4736]{1,0:T(8,128)(2,1)S(1)}, u32[]{:S(2)}, u32[]{:S(2)}) collective-permute-start(bf16[32,4736]{1,0:T(8,128)(2,1)S(1)} %get-tuple-element.38), channel_id=1, source_target_pairs={{0,7},{1,6},{2,5},{3,4},{4,3},{5,2},{6,1},{7,0},{8,15},{9,14},{10,... | collective-permute-start | bytes 909320 | tf_op jit(solution)/shard_map/ppermute | solution.py:28
  31.9 1.5 %collective-permute-start.12 = (bf16[144,896]{1,0:T(8,128)(2,1)S(1)}, bf16[144,896]{1,0:T(8,128)(2,1)S(1)}, u32[]{:S(2)}, u32[]{:S(2)}) collective-permute-start(bf16[144,896]{1,0:T(8,128)(2,1)S(1)} %collective-permute-done.9.refs_2_), channel_id=1, source_target_pairs={{0,1},{1,0},{2,3},{3,2},{4,5},{5,4},{6,7},{7,6},{8,9},{9,8},{10,11... | collective-permute-start | bytes 774152 | tf_op jit(solution)/shard_map/ppermute | solution.py:28
  33.4 3.1 %copy-start = (bf16[1,3584,1024]{2,1,0:T(8,128)(2,1)S(1)}, bf16[1,3584,1024]{2,1,0:T(8,128)(2,1)}, u32[]{:S(2)}) copy-start(bf16[1,3584,1024]{2,1,0:T(8,128)(2,1)} %weight_ref.1) | copy-start | bytes 22020100
  36.5 9.4 %copy-start.1 = (bf16[1,3584,1024]{2,1,0:T(8,128)(2,1)S(1)}, bf16[1,3584,1024]{2,1,0:T(8,128)(2,1)}, u32[]{:S(2)}) copy-start(bf16[1,3584,1024]{2,1,0:T(8,128)(2,1)} %weight_ref.1) | copy-start | bytes 22020100
  48.3 16.8 %collective-permute-start.18 = (bf16[256,1024]{1,0:T(8,128)(2,1)S(1)}, bf16[256,1024]{1,0:T(8,128)(2,1)S(1)}, u32[]{:S(2)}, u32[]{:S(2)}) collective-permute-start(bf16[256,1024]{1,0:T(8,128)(2,1)S(1)} %get-tuple-element.51.refs_0_), channel_id=1, source_target_pairs={{0,24},{8,16},{16,8},{24,0},{1,25},{9,17},{17,9},{25,1},{2,26},{10... | collective-permute-start | bytes 1572872 | tf_op jit(solution)/shard_map/ppermute | solution.py:28
  52.3 27.2 %collective-permute-start.17 = (bf16[256,1024]{1,0:T(8,128)(2,1)S(1)}, bf16[256,1024]{1,0:T(8,128)(2,1)S(1)}, u32[]{:S(2)}, u32[]{:S(2)}) collective-permute-start(bf16[256,1024]{1,0:T(8,128)(2,1)S(1)} %get-tuple-element.51.refs_0_), channel_id=1, source_target_pairs={{0,8},{8,0},{16,24},{24,16},{1,9},{9,1},{17,25},{25,17},{2,10},{10... | collective-permute-start | bytes 1572872 | tf_op jit(solution)/shard_map/ppermute | solution.py:28
  55.3 23.5 %collective-permute-start.13 = (bf16[64,3712]{1,0:T(8,128)(2,1)S(1)}, bf16[64,3712]{1,0:T(8,128)(2,1)S(1)}, u32[]{:S(2)}, u32[]{:S(2)}) collective-permute-start(bf16[64,3712]{1,0:T(8,128)(2,1)S(1)} %get-tuple-element.47), channel_id=1, source_target_pairs={{0,2},{1,3},{2,0},{3,1},{4,6},{5,7},{6,4},{7,5},{8,10},{9,11},{10,... | collective-permute-start | bytes 1425416 | tf_op jit(solution)/shard_map/ppermute | solution.py:28
  55.8 23.0 %collective-permute-start.14 = (bf16[64,3712]{1,0:T(8,128)(2,1)S(1)}, bf16[64,3712]{1,0:T(8,128)(2,1)S(1)}, u32[]{:S(2)}, u32[]{:S(2)}) collective-permute-start(bf16[64,3712]{1,0:T(8,128)(2,1)S(1)} %get-tuple-element.48), channel_id=1, source_target_pairs={{0,4},{1,5},{2,6},{3,7},{4,0},{5,1},{6,2},{7,3},{8,12},{9,13},{10,... | collective-permute-start | bytes 1425416 | tf_op jit(solution)/shard_map/ppermute | solution.py:28
  56.5 22.3 %collective-permute-start.15 = (bf16[64,3712]{1,0:T(8,128)(2,1)S(1)}, bf16[64,3712]{1,0:T(8,128)(2,1)S(1)}, u32[]{:S(2)}, u32[]{:S(2)}) collective-permute-start(bf16[64,3712]{1,0:T(8,128)(2,1)S(1)} %get-tuple-element.49), channel_id=1, source_target_pairs={{0,6},{1,7},{2,4},{3,5},{4,2},{5,3},{6,0},{7,1},{8,14},{9,15},{10,... | collective-permute-start | bytes 1425416 | tf_op jit(solution)/shard_map/ppermute | solution.py:28
  65.2 25.0 %collective-permute-start.19 = (bf16[256,1024]{1,0:T(8,128)(2,1)S(1)}, bf16[256,1024]{1,0:T(8,128)(2,1)S(1)}, u32[]{:S(2)}, u32[]{:S(2)}) collective-permute-start(bf16[256,1024]{1,0:T(8,128)(2,1)S(1)} %broadcast_select_fusion), channel_id=1, source_target_pairs={{0,16},{8,0},{16,24},{24,8},{1,17},{9,1},{17,25},{25,9},{2,18},{10... | collective-permute-start | bytes 1572872 | tf_op jit(solution)/shard_map/ppermute | solution.py:286
  78.9 2.3 %collective-permute-start.16 = (bf16[128,1024]{1,0:T(8,128)(2,1)S(1)}, bf16[128,1024]{1,0:T(8,128)(2,1)S(1)}, u32[]{:S(2)}, u32[]{:S(2)}) collective-permute-start(bf16[128,1024]{1,0:T(8,128)(2,1)S(1)} %split.1), channel_id=1, source_target_pairs={{0,1},{1,0},{2,3},{3,2},{4,5},{5,4},{6,7},{7,6},{8,9},{9,8},{10,11... | collective-permute-start | bytes 786440 | tf_op jit(solution)/shard_map/ppermute | solution.py:28
  79.5 1.6 %copy-start.5 = (s32[128,1]{0,1:T(1,128)S(1)}, s32[128,1]{0,1:T(1,128)}, u32[]{:S(2)}) copy-start(s32[128,1]{0,1:T(1,128)} %param.6) | copy-start | bytes 1540

commit v3 on v2

--- a/solution.py
+++ b/solution.py
@@ -105,12 +105,13 @@
         out[:, width + inner :] = gate[here]
 
 
+def touch_kernel(weight_ref, tie, out_ref):
+    out_ref[...] = weight_ref[0, :8, :LANES]
+
+
 def forward_kernel(sizes, weight_ref, *rest):
-    experts, width, inner, share, parts = sizes
-    pairs = experts // 2
-    blocks, rest = rest[:experts], rest[experts + pairs :]
-    sent, rest = rest[:pairs], rest[pairs:]
-    dpre_refs, (own_ref, all_ref) = rest[:parts], rest[parts:]
+    experts, width, inner, share = sizes
+    blocks, (act_ref, dpre_ref, own_ref, all_ref) = rest[:experts], rest[-4:]
     slots = blocks[0].shape[0]
     for k, block in enumerate(blocks):
         all_ref[k * slots : (k + 1) * slots, :] = block[...]
@@ -119,24 +120,20 @@
     gate = all_ref[:, width + inner :][:, :1].astype(F32)
     sig = jax.nn.sigmoid(pre)
     gated = gate * sig
-    dpre = (cots * gated * (1.0 + pre * (1.0 - sig))).astype(BF16)
-    height = dpre.shape[0] // parts
-    for p, out in enumerate(dpre_refs):
-        out[...] = dpre[p * height : (p + 1) * height]
-    act = (gated * pre).astype(BF16)
-    for j, out in enumerate(sent):
-        out[:, out.shape[1] - inner :] = act[2 * j * slots : 2 * (j + 1) * slots]
+    dpre_ref[...] = (cots * gated * (1.0 + pre * (1.0 - sig))).astype(BF16)
+    act_ref[...] = (gated * pre).astype(BF16)
     own_ref[...] = columns(all_ref.at[:, :width], lax.axis_index("dp"), share)
 
 
 def share_kernel(sizes, *refs):
     experts, slots, groups, count = sizes
     pairs = experts // 2
-    mine, theirs, outs = refs[:groups], refs[groups : 2 * groups], refs[-pairs:]
+    mine, theirs, act_ref = refs[:groups], refs[groups : 2 * groups], refs[2 * groups]
+    outs = refs[2 * groups + 1 :]
     share = mine[0].shape[1]
-    for out in outs:
-        out[:, groups * share :] = jnp.zeros_like(out[:, groups * share :])
     me = lax.axis_index("expert")
+    for j, out in enumerate(outs):
+        out[:, groups * share :] = act_ref[2 * j * slots : 2 * (j + 1) * slots]
     for g in range(groups):
         placed = []
         for block in (mine[g], theirs[g]):
@@ -244,35 +241,33 @@
         name="place",
     )(*mine)
     placed, cuts = placed[:experts], placed[experts:]
+    touched = pl.pallas_call(
+        touch_kernel,
+        out_shape=struct(8, LANES),
+        in_specs=[VMEM, ANY],
+        out_specs=VMEM,
+        compiler_params=limit(1),
+        name="touch",
+    )(weights, placed[0])
     got = list(placed)
     for k in range(2, experts, 2):
         got[k] = swap(placed[k], "expert", k)
-    for k, value in zip(range(1, experts, 2), after(placed[1::2], *got[2::2])):
+    later = after(placed[1::2], *got[2::2], *([touched] if TOUCH else []))
+    for k, value in zip(range(1, experts, 2), later):
         got[k] = swap(value, "expert", k)
+    cuts = [cuts[0], *after([cuts[1]], got[2]), *cuts[2:]] if groups > 1 else cuts
     cuts = [swap(cut, "dp", k + 1) for k, cut in enumerate(cuts)]
 
-    sent = pl.pallas_call(
-        functools.partial(share_kernel, (experts, slots, groups, count)),
-        out_shape=[struct(2 * slots, groups * share + inner)] * pairs,
-        in_specs=[VMEM] * (1 + 2 * groups),
-        out_specs=[VMEM] * pairs,
+    act, dpre, own = pl.pallas_call(
+        functools.partial(forward_kernel, (experts, width, inner, share)),
+        out_shape=[struct(rows, inner), struct(rows, inner), struct(rows, share)],
+        in_specs=[VMEM] * (1 + experts) + [ANY] * groups,
+        out_specs=[VMEM] * 3,
+        scratch_shapes=[pltpu.VMEM((rows, wide), BF16)],
         compiler_params=limit(SMALL),
-        name="place_shares",
-    )(*cuts, *[swap(cut, "expert", 1) for cut in cuts], weights)
-    sent, dpres, own = (lambda a: (a[:pairs], list(a[pairs:-1]), a[-1]))(
-        pl.pallas_call(
-            functools.partial(forward_kernel, (experts, width, inner, share, PARTS)),
-            out_shape=[struct(2 * slots, groups * share + inner)] * pairs
-            + [struct(rows // PARTS, inner)] * PARTS
-            + [struct(rows, share)],
-            in_specs=[VMEM] * (1 + experts + pairs),
-            out_specs=[VMEM] * (1 + pairs + PARTS),
-            input_output_aliases={1 + experts + j: j for j in range(pairs)},
-            scratch_shapes=[pltpu.VMEM((rows, wide), BF16)],
-            compiler_params=limit(SMALL),
-            name="forward",
-        )(weights, *got, *sent)
-    )
+        name="forward",
+    )(weights, *got, *cuts)
+    dpres = [dpre]
 
     gathered = [[] for _ in range(groups)]
     for value in dpres:
@@ -285,6 +280,14 @@
             value = jnp.where(ends, value, far)
             gathered[1].append(lax.ppermute(value, "dp", [(0, 2), (1, 0), (2, 3), (3, 1)]))
 
+    sent = pl.pallas_call(
+        functools.partial(share_kernel, (experts, slots, groups, count)),
+        out_shape=[struct(2 * slots, groups * share + inner)] * pairs,
+        in_specs=[VMEM] * (1 + 2 * groups),
+        out_specs=[VMEM] * pairs,
+        compiler_params=limit(SMALL),
+        name="place_shares",
+    )(*cuts, *[swap(cut, "expert", 1) for cut in cuts], act)
     lefts = [sent[0]] + [swap(sent[j], "expert", 2 * j) for j in range(1, pairs)]
     theirs = pl.pallas_call(
         functools.partial(split_kernel, slots, inner),
@@ -350,7 +353,7 @@
     return (hidden, grad[None])
 
 
-BIG, SMALL, PARTS = 40, 12, 1
+BIG, SMALL, TOUCH = 40, 12, True
 
 
 def solution(mesh):

time: 92.7 us -> 84.6 us (0.913)
  starting transfers between devices: 38.8 us -> 33 us
  waiting for transfers between devices: 35.8 us -> 32.5 us
  Pallas kernels: 10.5 us -> 11.5 us
    ppermute x1, waiting for transfers between devices: 7.87 us -> 2.37 us  [on_device(): lax.ppermute(value, 'dp', [(0, 2), (1, 0), (2, 3), (3, 1)])]
    ppermute x1, starting transfers between devices: 13.6 us -> 10.3 us  [on_device(): lax.ppermute(value, 'dp', [(0, 2), (1, 0), (2, 3), (3, 1)])]
    ppermute x19, starting transfers between devices: 25.2 us -> 22.7 us  [swap(): return lax.ppermute(value, axis, [(i, i ^ offset) for i in range(count)])]
    ppermute x19, waiting for transfers between devices: 27.9 us -> 30.1 us  [swap(): return lax.ppermute(value, axis, [(i, i ^ offset) for i in range(count)])]
    pallas_call x1, Pallas kernels: 1.33 us -> 2.3 us  [on_device(): pl.pallas_call(functools.partial(share_kernel, (experts, slots, groups, c...]
  transfers between devices with their start and end apart: 20 -> 20, of which waited for: 7 -> 9; matrix products, arithmetic and copies ran while one was open for 0% -> 0% of each run, Pallas kernels for 5% -> 7%
where the time goes in v3:
time: 84.6 us; the launch traced here: 84.3 us
  starting transfers between devices  33 us (39%)
  waiting for transfers between devices  32.5 us (38%)
  Pallas kernels  11.5 us (14%)
  local copies, waits for them, and re-layouts  6.52 us (8%)
    ppermute x19, waiting for transfers between devices, swap(): return lax.ppermute(value, axis, [(i, i ^ offset) for i in range(count)])  30.1 us
    ppermute x19, starting transfers between devices, swap(): return lax.ppermute(value, axis, [(i, i ^ offset) for i in range(count)])  22.7 us
    ppermute x1, starting transfers between devices, on_device(): lax.ppermute(value, 'dp', [(0, 2), (1, 0), (2, 3), (3, 1)])  10.3 us
    unnamed x14, local copies, waits for them, and re-layouts  6.52 us
    pallas_call x1, Pallas kernels, on_device(): pl.pallas_call(functools.partial(forward_kernel, (experts, width, inner,...  2.38 us
    ppermute x1, waiting for transfers between devices, on_device(): lax.ppermute(value, 'dp', [(0, 2), (1, 0), (2, 3), (3, 1)])  2.37 us
    pallas_call x1, Pallas kernels, on_device(): pl.pallas_call(functools.partial(share_kernel, (experts, slots, groups, c...  2.3 us
    pallas_call x1, Pallas kernels, on_device(): pl.pallas_call(functools.partial(grad_kernel, 2), out_shape=jax.ShapeDtyp...  2.25 us
  transfers between devices with their start and end apart: 20, of which 9 were waited for; matrix products, arithmetic and copies ran while one was open for 0% of the time, Pallas kernels for 7%

profile of v3, /device:TPU:0, one launch (start us, length us, event | category | flops | bytes accessed | tf_op | source)
XLA Modules:
  0.0 84.3 jit_solution(1307783994945516889)
XLA Ops:
  0.6 1.2 %copy-done.2 = bf16[128,3584]{1,0:T(8,128)(2,1)S(1)} copy-done((bf16[128,3584]{1,0:T(8,128)(2,1)S(1)}, bf16[128,3584]{1,0:T(8,128)(2,1)}, u32[]{:S(2)}) %copy-start.2) | copy-done | bytes 917528
  1.8 0.9 %copy-done.3 = bf16[128,1024]{1,0:T(8,128)(2,1)S(1)} copy-done((bf16[128,1024]{1,0:T(8,128)(2,1)S(1)}, bf16[128,1024]{1,0:T(8,128)(2,1)}, u32[]{:S(2)}) %copy-start.3) | copy-done | bytes 262168
  2.8 0.7 copy-done.4
  3.4 0.7 copy-done.6
  4.1 1.2 %place.1 = (bf16[32,4736]{1,0:T(8,128)(2,1)S(1)}, bf16[32,4736]{1,0:T(8,128)(2,1)S(1)}, bf16[32,4736]{1,0:T(8,128)(2,1)S(1)}, bf16[32,4736]{1,0:T(8,128)(2,1)S(1...) custom-call(s32[1,128]{1,0:T(1,128)S(1)} %bitcast.3, ...), custom_call_target="tpu_custom_call" | custom-call | tf_op jit(solution)/shard_map/place/pallas_call | solution.py:233
  5.3 3.0 %collective-permute-start.1 = (bf16[32,4736]{1,0:T(8,128)(2,1)S(1)}, bf16[32,4736]{1,0:T(8,128)(2,1)S(1)}, u32[]{:S(2)}, u32[]{:S(2)}) collective-permute-start(bf16[32,4736]{1,0:T(8,128)(2,1)S(1)} %get-tuple-element.26), channel_id=1, source_target_pairs={{0,2},{1,3},{2,0},{3,1},{4,6},{5,7},{6,4},{7,5},{8,10},{9,11},{10,... | collective-permute-start | bytes 909320 | tf_op jit(solution)/shard_map/ppermute | solution.py:28
  8.3 1.5 %collective-permute-start.7 = (bf16[32,4736]{1,0:T(8,128)(2,1)S(1)}, bf16[32,4736]{1,0:T(8,128)(2,1)S(1)}, u32[]{:S(2)}, u32[]{:S(2)}) collective-permute-start(bf16[32,4736]{1,0:T(8,128)(2,1)S(1)} %get-tuple-element.33), channel_id=1, source_target_pairs={{0,4},{1,5},{2,6},{3,7},{4,0},{5,1},{6,2},{7,3},{8,12},{9,13},{10,... | collective-permute-start | bytes 909320 | tf_op jit(solution)/shard_map/ppermute | solution.py:28
  9.8 0.0 collective-permute-start.8
  9.8 2.0 %collective-permute-start = (bf16[144,896]{1,0:T(8,128)(2,1)S(1)}, bf16[144,896]{1,0:T(8,128)(2,1)S(1)}, u32[]{:S(2)}, u32[]{:S(2)}) collective-permute-start(bf16[144,896]{1,0:T(8,128)(2,1)S(1)} %get-tuple-element.24), channel_id=1, source_target_pairs={{0,8},{8,0},{16,24},{24,16},{1,9},{9,1},{17,25},{25,17},{2,10},{10... | collective-permute-start | bytes 774152 | tf_op jit(solution)/shard_map/ppermute | solution.py:28
  11.8 2.5 %collective-permute-start.3 = (bf16[144,896]{1,0:T(8,128)(2,1)S(1)}, bf16[144,896]{1,0:T(8,128)(2,1)S(1)}, u32[]{:S(2)}, u32[]{:S(2)}) collective-permute-start(bf16[144,896]{1,0:T(8,128)(2,1)S(1)} %get-tuple-element.27), channel_id=1, source_target_pairs={{0,24},{8,16},{16,8},{24,0},{1,25},{9,17},{17,9},{25,1},{2,26},{10... | collective-permute-start | bytes 774152 | tf_op jit(solution)/shard_map/ppermute | solution.py:28
  14.3 3.1 %copy-done = bf16[1,3584,1024]{2,1,0:T(8,128)(2,1)S(1)} copy-done((bf16[1,3584,1024]{2,1,0:T(8,128)(2,1)S(1)}, bf16[1,3584,1024]{2,1,0:T(8,128)(2,1)}, u32[]{:S(2)}) %copy-start) | copy-done | bytes 7340056
  17.4 0.0 collective-permute-done.1.refs_1_.refs_4_.rest_2_
  17.4 6.0 %collective-permute-done.7.refs_5_.rest_4_ = bf16[32,4736]{1,0:T(8,128)(2,1)S(1)} collective-permute-done((bf16[32,4736]{1,0:T(8,128)(2,1)S(1)}, bf16[32,4736]{1,0:T(8,128)(2,1)S(1)}, u32[]{:S(2)}, u32[]{:S(2)}) %collective-permute-start.7) | collective-permute-done | bytes 303136 | tf_op jit(solution)/shard_map/ppermute | solution.py:28
  23.4 0.0 collective-permute-done.8.refs_6_.rest_6_
  23.4 1.3 %collective-permute-start.10 = (bf16[32,4736]{1,0:T(8,128)(2,1)S(1)}, bf16[32,4736]{1,0:T(8,128)(2,1)S(1)}, u32[]{:S(2)}, u32[]{:S(2)}) collective-permute-start(bf16[32,4736]{1,0:T(8,128)(2,1)S(1)} %get-tuple-element.36), channel_id=1, source_target_pairs={{0,3},{1,2},{2,1},{3,0},{4,7},{5,6},{6,5},{7,4},{8,11},{9,10},{10,... | collective-permute-start | bytes 909320 | tf_op jit(solution)/shard_map/ppermute | solution.py:28
  24.8 0.5 collective-permute-start.11
  25.2 0.0 collective-permute-done.rest_8_.refs_0_
  25.3 1.5 %collective-permute-start.12 = (bf16[32,4736]{1,0:T(8,128)(2,1)S(1)}, bf16[32,4736]{1,0:T(8,128)(2,1)S(1)}, u32[]{:S(2)}, u32[]{:S(2)}) collective-permute-start(bf16[32,4736]{1,0:T(8,128)(2,1)S(1)} %get-tuple-element.38), channel_id=1, source_target_pairs={{0,7},{1,6},{2,5},{3,4},{4,3},{5,2},{6,1},{7,0},{8,15},{9,14},{10,... | collective-permute-start | bytes 909320 | tf_op jit(solution)/shard_map/ppermute | solution.py:28
  26.7 0.0 collective-permute-done.3.rest_10_.refs_2_
  26.7 2.6 %collective-permute-start.2 = (bf16[144,896]{1,0:T(8,128)(2,1)S(1)}, bf16[144,896]{1,0:T(8,128)(2,1)S(1)}, u32[]{:S(2)}, u32[]{:S(2)}) collective-permute-start(bf16[144,896]{1,0:T(8,128)(2,1)S(1)} %hold.2), channel_id=1, source_target_pairs={{0,16},{8,24},{16,0},{24,8},{1,17},{9,25},{17,1},{25,9},{2,18},{10... | collective-permute-start | bytes 774152 | tf_op jit(solution)/shard_map/ppermute | solution.py:28
  29.3 12.0 %collective-permute-done.2.rest_9_.refs_1_ = bf16[144,896]{1,0:T(8,128)(2,1)S(1)} collective-permute-done((bf16[144,896]{1,0:T(8,128)(2,1)S(1)}, bf16[144,896]{1,0:T(8,128)(2,1)S(1)}, u32[]{:S(2)}, u32[]{:S(2)}) %collective-permute-start.2) | collective-permute-done | bytes 258080 | tf_op jit(solution)/shard_map/ppermute | solution.py:28
  41.4 0.0 collective-permute-done.9.rest_1_
  41.4 0.0 collective-permute-done.10.rest_3_
  41.4 0.0 collective-permute-done.11.rest_5_
  41.4 0.0 collective-permute-done.12.rest_7_
  41.4 2.4 %forward.1 = (bf16[256,1024]{1,0:T(8,128)(2,1)S(1)}, bf16[256,1024]{1,0:T(8,128)(2,1)S(1)}, bf16[256,896]{1,0:T(8,128)(2,1)S(1)}) custom-call(bf16[1,3584,1024]{2,1,0:T(8,128)(2,1)S(1)} %copy-done.1, bf16[32,4736]{1,0:T(8,128)(2,1)S(1)} %get-tuple-element.28.tie.rest_0_, bf16[32,4736]{1,0:T(8,128)(2,1)S(1)} %collective-permute-done.9.rest_1_, ...), custom_call_target="tpu_custom_call" | custom-call | tf_op jit(solution)/shard_map/forward/pallas_call | solution.py:261
  43.8 3.6 %collective-permute-start.18 = (bf16[256,1024]{1,0:T(8,128)(2,1)S(1)}, bf16[256,1024]{1,0:T(8,128)(2,1)S(1)}, u32[]{:S(2)}, u32[]{:S(2)}) collective-permute-start(bf16[256,1024]{1,0:T(8,128)(2,1)S(1)} %get-tuple-element.45.refs_0_), channel_id=1, source_target_pairs={{0,24},{8,16},{16,8},{24,0},{1,25},{9,17},{17,9},{25,1},{2,26},{10... | collective-permute-start | bytes 1572872 | tf_op jit(solution)/shard_map/ppermute | solution.py:28
  47.3 0.0 collective-permute-start.4
  47.3 0.5 collective-permute-start.6
  47.9 1.0 %collective-permute-done.4.refs_3_ = bf16[144,896]{1,0:T(8,128)(2,1)S(1)} collective-permute-done((bf16[144,896]{1,0:T(8,128)(2,1)S(1)}, bf16[144,896]{1,0:T(8,128)(2,1)S(1)}, u32[]{:S(2)}, u32[]{:S(2)}) %collective-permute-start.4) | collective-permute-done | bytes 258080 | tf_op jit(solution)/shard_map/ppermute | solution.py:28
  48.9 0.5 collective-permute-done.6.refs_5_
  49.3 0.4 collective-permute-done.5.refs_4_
  49.7 2.3 %place_shares.1 = (bf16[64,3712]{1,0:T(8,128)(2,1)S(1)}, bf16[64,3712]{1,0:T(8,128)(2,1)S(1)}, bf16[64,3712]{1,0:T(8,128)(2,1)S(1)}, bf16[64,3712]{1,0:T(8,128)(2,1)S(1)}) custom-call(bf16[144,896]{1,0:T(8,128)(2,1)S(1)} %collective-permute-done.rest_8_.refs_0_, bf16[144,896]{1,0:T(8,128)(2,1)S(1)} %collective-permute-done.2.rest_9_.refs_1_, ...), custom_call_target="tpu_custom_call" | custom-call | tf_op jit(solution)/shard_map/place_shares/pallas_call | solution.py:283
  52.0 1.2 %collective-permute-start.13 = (bf16[64,3712]{1,0:T(8,128)(2,1)S(1)}, bf16[64,3712]{1,0:T(8,128)(2,1)S(1)}, u32[]{:S(2)}, u32[]{:S(2)}) collective-permute-start(bf16[64,3712]{1,0:T(8,128)(2,1)S(1)} %get-tuple-element.41), channel_id=1, source_target_pairs={{0,2},{1,3},{2,0},{3,1},{4,6},{5,7},{6,4},{7,5},{8,10},{9,11},{10,... | collective-permute-start | bytes 1425416 | tf_op jit(solution)/shard_map/ppermute | solution.py:28
  53.3 0.9 %collective-permute-start.14 = (bf16[64,3712]{1,0:T(8,128)(2,1)S(1)}, bf16[64,3712]{1,0:T(8,128)(2,1)S(1)}, u32[]{:S(2)}, u32[]{:S(2)}) collective-permute-start(bf16[64,3712]{1,0:T(8,128)(2,1)S(1)} %get-tuple-element.42), channel_id=1, source_target_pairs={{0,4},{1,5},{2,6},{3,7},{4,0},{5,1},{6,2},{7,3},{8,12},{9,13},{10,... | collective-permute-start | bytes 1425416 | tf_op jit(solution)/shard_map/ppermute | solution.py:28
  54.2 1.4 %collective-permute-start.15 = (bf16[64,3712]{1,0:T(8,128)(2,1)S(1)}, bf16[64,3712]{1,0:T(8,128)(2,1)S(1)}, u32[]{:S(2)}, u32[]{:S(2)}) collective-permute-start(bf16[64,3712]{1,0:T(8,128)(2,1)S(1)} %get-tuple-element.43), channel_id=1, source_target_pairs={{0,6},{1,7},{2,4},{3,5},{4,2},{5,3},{6,0},{7,1},{8,14},{9,15},{10,... | collective-permute-start | bytes 1425416 | tf_op jit(solution)/shard_map/ppermute | solution.py:28
  55.6 4.9 %collective-permute-done.18.refs_2_ = bf16[256,1024]{1,0:T(8,128)(2,1)S(1)} collective-permute-done((bf16[256,1024]{1,0:T(8,128)(2,1)S(1)}, bf16[256,1024]{1,0:T(8,128)(2,1)S(1)}, u32[]{:S(2)}, u32[]{:S(2)}) %collective-permute-start.18) | collective-permute-done | bytes 524320 | tf_op jit(solution)/shard_map/ppermute | solution.py:28
  60.5 0.1 broadcast_select_fusion
  60.6 10.3 %collective-permute-start.19 = (bf16[256,1024]{1,0:T(8,128)(2,1)S(1)}, bf16[256,1024]{1,0:T(8,128)(2,1)S(1)}, u32[]{:S(2)}, u32[]{:S(2)}) collective-permute-start(bf16[256,1024]{1,0:T(8,128)(2,1)S(1)} %broadcast_select_fusion), channel_id=1, source_target_pairs={{0,16},{8,0},{16,24},{24,8},{1,17},{9,1},{17,25},{25,9},{2,18},{10... | collective-permute-start | bytes 1572872 | tf_op jit(solution)/shard_map/ppermute | solution.py:281
  70.9 3.6 %collective-permute-done.14.refs_2_ = bf16[64,3712]{1,0:T(8,128)(2,1)S(1)} collective-permute-done((bf16[64,3712]{1,0:T(8,128)(2,1)S(1)}, bf16[64,3712]{1,0:T(8,128)(2,1)S(1)}, u32[]{:S(2)}, u32[]{:S(2)}) %collective-permute-start.14) | collective-permute-done | bytes 475168 | tf_op jit(solution)/shard_map/ppermute | solution.py:28
  74.5 1.6 %collective-permute-done.15.refs_3_ = bf16[64,3712]{1,0:T(8,128)(2,1)S(1)} collective-permute-done((bf16[64,3712]{1,0:T(8,128)(2,1)S(1)}, bf16[64,3712]{1,0:T(8,128)(2,1)S(1)}, u32[]{:S(2)}, u32[]{:S(2)}) %collective-permute-start.15) | collective-permute-done | bytes 475168 | tf_op jit(solution)/shard_map/ppermute | solution.py:28
  76.2 0.1 collective-permute-start.16
  76.3 0.6 turn.1.left_ref
  76.8 0.0 copy-start.5
  76.9 1.6 %sum.1.before_ref = f32[896,1024]{1,0:T(8,128)S(1)} custom-call(bf16[896,1024]{1,0:T(8,128)(2,1)S(1)} %turn.1.left_ref, bf16[256,1024]{1,0:T(8,128)(2,1)S(1)} %get-tuple-element.45.refs_0_, bf16[256,1024]{1,0:T(8,128)(2,1)S(1)} %collective-permute-done.17.refs_1_, bf16[256,1024]{1,0:T(8,128)(2,1)S(1)} %collective-permute-done.18.refs_2_), custom_call_target="tpu_custom_call" | custom-call | tf_op jit(solution)/shard_map/sum/pallas_call | solution.py:319
  78.5 1.2 %unplace.1 = bf16[128,1024]{1,0:T(8,128)(2,1)} custom-call(s32[1,128]{1,0:T(1,128)S(1)} %bitcast.4, bf16[128,1024]{1,0:T(8,128)(2,1)S(1)} %collective-permute-done.16.theirs_ref, bf16[64,3712]{1,0:T(8,128)(2,1)S(1)} %get-tuple-element.40.refs_0_, bf16[64,3712]{1,0:T(8,128)(2,1)S(1)} %collective-permute-done.13.refs_1_, ...), custom_call_target="tpu_custom_call" | custom-call | tf_op jit(solution)/shard_map/unplace/pallas_call | solution.py:300
  79.7 2.4 %collective-permute-done.19.refs_0_ = bf16[256,1024]{1,0:T(8,128)(2,1)S(1)} collective-permute-done((bf16[256,1024]{1,0:T(8,128)(2,1)S(1)}, bf16[256,1024]{1,0:T(8,128)(2,1)S(1)}, u32[]{:S(2)}, u32[]{:S(2)}) %collective-permute-start.19) | collective-permute-done | bytes 524320 | tf_op jit(solution)/shard_map/ppermute | solution.py:281
  82.0 2.3 %grad.1 = f32[896,1024]{1,0:T(8,128)} custom-call(bf16[896,1024]{1,0:T(8,128)(2,1)S(1)} %turn.1.left_ref, f32[896,1024]{1,0:T(8,128)S(1)} %sum.1.before_ref, bf16[256,1024]{1,0:T(8,128)(2,1)S(1)} %collective-permute-done.19.refs_0_), custom_call_target="tpu_custom_call" | custom-call | tf_op jit(solution)/shard_map/grad/pallas_call | solution.py:329
  (18 shorter events, 0.1 us)
Async XLA Ops:
  0.6 1.2 %copy-start.2 = (bf16[128,3584]{1,0:T(8,128)(2,1)S(1)}, bf16[128,3584]{1,0:T(8,128)(2,1)}, u32[]{:S(2)}) copy-start(bf16[128,3584]{1,0:T(8,128)(2,1)} %refs_3_.1) | copy-start | bytes 2752516
  1.8 0.9 %copy-start.3 = (bf16[128,1024]{1,0:T(8,128)(2,1)S(1)}, bf16[128,1024]{1,0:T(8,128)(2,1)}, u32[]{:S(2)}) copy-start(bf16[128,1024]{1,0:T(8,128)(2,1)} %refs_2_.1) | copy-start | bytes 786436
  2.8 0.7 copy-start.4
  3.4 0.7 copy-start.6
  5.3 12.1 %collective-permute-start.1 = (bf16[32,4736]{1,0:T(8,128)(2,1)S(1)}, bf16[32,4736]{1,0:T(8,128)(2,1)S(1)}, u32[]{:S(2)}, u32[]{:S(2)}) collective-permute-start(bf16[32,4736]{1,0:T(8,128)(2,1)S(1)} %get-tuple-element.26), channel_id=1, source_target_pairs={{0,2},{1,3},{2,0},{3,1},{4,6},{5,7},{6,4},{7,5},{8,10},{9,11},{10,... | collective-permute-start | bytes 909320 | tf_op jit(solution)/shard_map/ppermute | solution.py:28
  8.3 15.1 %collective-permute-start.7 = (bf16[32,4736]{1,0:T(8,128)(2,1)S(1)}, bf16[32,4736]{1,0:T(8,128)(2,1)S(1)}, u32[]{:S(2)}, u32[]{:S(2)}) collective-permute-start(bf16[32,4736]{1,0:T(8,128)(2,1)S(1)} %get-tuple-element.33), channel_id=1, source_target_pairs={{0,4},{1,5},{2,6},{3,7},{4,0},{5,1},{6,2},{7,3},{8,12},{9,13},{10,... | collective-permute-start | bytes 909320 | tf_op jit(solution)/shard_map/ppermute | solution.py:28
  9.8 13.6 %collective-permute-start.8 = (bf16[32,4736]{1,0:T(8,128)(2,1)S(1)}, bf16[32,4736]{1,0:T(8,128)(2,1)S(1)}, u32[]{:S(2)}, u32[]{:S(2)}) collective-permute-start(bf16[32,4736]{1,0:T(8,128)(2,1)S(1)} %get-tuple-element.34), channel_id=1, source_target_pairs={{0,6},{1,7},{2,4},{3,5},{4,2},{5,3},{6,0},{7,1},{8,14},{9,15},{10,... | collective-permute-start | bytes 909320 | tf_op jit(solution)/shard_map/ppermute | solution.py:28
  9.8 15.4 %collective-permute-start = (bf16[144,896]{1,0:T(8,128)(2,1)S(1)}, bf16[144,896]{1,0:T(8,128)(2,1)S(1)}, u32[]{:S(2)}, u32[]{:S(2)}) collective-permute-start(bf16[144,896]{1,0:T(8,128)(2,1)S(1)} %get-tuple-element.24), channel_id=1, source_target_pairs={{0,8},{8,0},{16,24},{24,16},{1,9},{9,1},{17,25},{25,17},{2,10},{10... | collective-permute-start | bytes 774152 | tf_op jit(solution)/shard_map/ppermute | solution.py:28
  11.8 14.9 %collective-permute-start.3 = (bf16[144,896]{1,0:T(8,128)(2,1)S(1)}, bf16[144,896]{1,0:T(8,128)(2,1)S(1)}, u32[]{:S(2)}, u32[]{:S(2)}) collective-permute-start(bf16[144,896]{1,0:T(8,128)(2,1)S(1)} %get-tuple-element.27), channel_id=1, source_target_pairs={{0,24},{8,16},{16,8},{24,0},{1,25},{9,17},{17,9},{25,1},{2,26},{10... | collective-permute-start | bytes 774152 | tf_op jit(solution)/shard_map/ppermute | solution.py:28
  14.3 3.1 %copy-start = (bf16[1,3584,1024]{2,1,0:T(8,128)(2,1)S(1)}, bf16[1,3584,1024]{2,1,0:T(8,128)(2,1)}, u32[]{:S(2)}) copy-start(bf16[1,3584,1024]{2,1,0:T(8,128)(2,1)} %weight_ref.3) | copy-start | bytes 22020100
  17.4 24.0 %copy-start.1 = (bf16[1,3584,1024]{2,1,0:T(8,128)(2,1)S(1)}, bf16[1,3584,1024]{2,1,0:T(8,128)(2,1)}, u32[]{:S(2)}) copy-start(bf16[1,3584,1024]{2,1,0:T(8,128)(2,1)} %weight_ref.3) | copy-start | bytes 22020100
  23.4 18.0 %collective-permute-start.9 = (bf16[32,4736]{1,0:T(8,128)(2,1)S(1)}, bf16[32,4736]{1,0:T(8,128)(2,1)S(1)}, u32[]{:S(2)}, u32[]{:S(2)}) collective-permute-start(bf16[32,4736]{1,0:T(8,128)(2,1)S(1)} %get-tuple-element.35), channel_id=1, source_target_pairs={{0,1},{1,0},{2,3},{3,2},{4,5},{5,4},{6,7},{7,6},{8,9},{9,8},{10,11... | collective-permute-start | bytes 909320 | tf_op jit(solution)/shard_map/ppermute | solution.py:28
  23.4 18.0 %collective-permute-start.10 = (bf16[32,4736]{1,0:T(8,128)(2,1)S(1)}, bf16[32,4736]{1,0:T(8,128)(2,1)S(1)}, u32[]{:S(2)}, u32[]{:S(2)}) collective-permute-start(bf16[32,4736]{1,0:T(8,128)(2,1)S(1)} %get-tuple-element.36), channel_id=1, source_target_pairs={{0,3},{1,2},{2,1},{3,0},{4,7},{5,6},{6,5},{7,4},{8,11},{9,10},{10,... | collective-permute-start | bytes 909320 | tf_op jit(solution)/shard_map/ppermute | solution.py:28
  24.8 16.6 %collective-permute-start.11 = (bf16[32,4736]{1,0:T(8,128)(2,1)S(1)}, bf16[32,4736]{1,0:T(8,128)(2,1)S(1)}, u32[]{:S(2)}, u32[]{:S(2)}) collective-permute-start(bf16[32,4736]{1,0:T(8,128)(2,1)S(1)} %get-tuple-element.37), channel_id=1, source_target_pairs={{0,5},{1,4},{2,7},{3,6},{4,1},{5,0},{6,3},{7,2},{8,13},{9,12},{10,... | collective-permute-start | bytes 909320 | tf_op jit(solution)/shard_map/ppermute | solution.py:28
  25.3 16.1 %collective-permute-start.12 = (bf16[32,4736]{1,0:T(8,128)(2,1)S(1)}, bf16[32,4736]{1,0:T(8,128)(2,1)S(1)}, u32[]{:S(2)}, u32[]{:S(2)}) collective-permute-start(bf16[32,4736]{1,0:T(8,128)(2,1)S(1)} %get-tuple-element.38), channel_id=1, source_target_pairs={{0,7},{1,6},{2,5},{3,4},{4,3},{5,2},{6,1},{7,0},{8,15},{9,14},{10,... | collective-permute-start | bytes 909320 | tf_op jit(solution)/shard_map/ppermute | solution.py:28
  26.7 14.6 %collective-permute-start.2 = (bf16[144,896]{1,0:T(8,128)(2,1)S(1)}, bf16[144,896]{1,0:T(8,128)(2,1)S(1)}, u32[]{:S(2)}, u32[]{:S(2)}) collective-permute-start(bf16[144,896]{1,0:T(8,128)(2,1)S(1)} %hold.2), channel_id=1, source_target_pairs={{0,16},{8,24},{16,0},{24,8},{1,17},{9,25},{17,1},{25,9},{2,18},{10... | collective-permute-start | bytes 774152 | tf_op jit(solution)/shard_map/ppermute | solution.py:28
  43.8 16.7 %collective-permute-start.18 = (bf16[256,1024]{1,0:T(8,128)(2,1)S(1)}, bf16[256,1024]{1,0:T(8,128)(2,1)S(1)}, u32[]{:S(2)}, u32[]{:S(2)}) collective-permute-start(bf16[256,1024]{1,0:T(8,128)(2,1)S(1)} %get-tuple-element.45.refs_0_), channel_id=1, source_target_pairs={{0,24},{8,16},{16,8},{24,0},{1,25},{9,17},{17,9},{25,1},{2,26},{10... | collective-permute-start | bytes 1572872 | tf_op jit(solution)/shard_map/ppermute | solution.py:28
  47.3 1.5 %collective-permute-start.4 = (bf16[144,896]{1,0:T(8,128)(2,1)S(1)}, bf16[144,896]{1,0:T(8,128)(2,1)S(1)}, u32[]{:S(2)}, u32[]{:S(2)}) collective-permute-start(bf16[144,896]{1,0:T(8,128)(2,1)S(1)} %collective-permute-done.rest_8_.refs_0_), channel_id=1, source_target_pairs={{0,1},{1,0},{2,3},{3,2},{4,5},{5,4},{6,7},{7,6},{8,9},{9,8},{10,11... | collective-permute-start | bytes 774152 | tf_op jit(solution)/shard_map/ppermute | solution.py:28
  47.3 2.0 %collective-permute-start.6 = (bf16[144,896]{1,0:T(8,128)(2,1)S(1)}, bf16[144,896]{1,0:T(8,128)(2,1)S(1)}, u32[]{:S(2)}, u32[]{:S(2)}) collective-permute-start(bf16[144,896]{1,0:T(8,128)(2,1)S(1)} %collective-permute-done.3.rest_10_.refs_2_), channel_id=1, source_target_pairs={{0,1},{1,0},{2,3},{3,2},{4,5},{5,4},{6,7},{7,6},{8,9},{9,8},{10,11... | collective-permute-start | bytes 774152 | tf_op jit(solution)/shard_map/ppermute | solution.py:28
  47.8 1.9 %collective-permute-start.5 = (bf16[144,896]{1,0:T(8,128)(2,1)S(1)}, bf16[144,896]{1,0:T(8,128)(2,1)}, u32[]{:S(2)}, u32[]{:S(2)}) collective-permute-start(bf16[144,896]{1,0:T(8,128)(2,1)S(1)} %collective-permute-done.2.rest_9_.refs_1_), channel_id=1, source_target_pairs={{0,1},{1,0},{2,3},{3,2},{4,5},{5,4},{6,7},{7,6},{8,9},{9,8},{10,11... | collective-permute-start | bytes 774152 | tf_op jit(solution)/shard_map/ppermute | solution.py:28
  47.8 29.0 %collective-permute-start.17 = (bf16[256,1024]{1,0:T(8,128)(2,1)S(1)}, bf16[256,1024]{1,0:T(8,128)(2,1)S(1)}, u32[]{:S(2)}, u32[]{:S(2)}) collective-permute-start(bf16[256,1024]{1,0:T(8,128)(2,1)S(1)} %get-tuple-element.45.refs_0_), channel_id=1, source_target_pairs={{0,8},{8,0},{16,24},{24,16},{1,9},{9,1},{17,25},{25,17},{2,10},{10... | collective-permute-start | bytes 1572872 | tf_op jit(solution)/shard_map/ppermute | solution.py:28
  52.0 18.9 %collective-permute-start.13 = (bf16[64,3712]{1,0:T(8,128)(2,1)S(1)}, bf16[64,3712]{1,0:T(8,128)(2,1)S(1)}, u32[]{:S(2)}, u32[]{:S(2)}) collective-permute-start(bf16[64,3712]{1,0:T(8,128)(2,1)S(1)} %get-tuple-element.41), channel_id=1, source_target_pairs={{0,2},{1,3},{2,0},{3,1},{4,6},{5,7},{6,4},{7,5},{8,10},{9,11},{10,... | collective-permute-start | bytes 1425416 | tf_op jit(solution)/shard_map/ppermute | solution.py:28
  53.3 21.3 %collective-permute-start.14 = (bf16[64,3712]{1,0:T(8,128)(2,1)S(1)}, bf16[64,3712]{1,0:T(8,128)(2,1)S(1)}, u32[]{:S(2)}, u32[]{:S(2)}) collective-permute-start(bf16[64,3712]{1,0:T(8,128)(2,1)S(1)} %get-tuple-element.42), channel_id=1, source_target_pairs={{0,4},{1,5},{2,6},{3,7},{4,0},{5,1},{6,2},{7,3},{8,12},{9,13},{10,... | collective-permute-start | bytes 1425416 | tf_op jit(solution)/shard_map/ppermute | solution.py:28
  54.2 22.0 %collective-permute-start.15 = (bf16[64,3712]{1,0:T(8,128)(2,1)S(1)}, bf16[64,3712]{1,0:T(8,128)(2,1)S(1)}, u32[]{:S(2)}, u32[]{:S(2)}) collective-permute-start(bf16[64,3712]{1,0:T(8,128)(2,1)S(1)} %get-tuple-element.43), channel_id=1, source_target_pairs={{0,6},{1,7},{2,4},{3,5},{4,2},{5,3},{6,0},{7,1},{8,14},{9,15},{10,... | collective-permute-start | bytes 1425416 | tf_op jit(solution)/shard_map/ppermute | solution.py:28
  60.6 21.5 %collective-permute-start.19 = (bf16[256,1024]{1,0:T(8,128)(2,1)S(1)}, bf16[256,1024]{1,0:T(8,128)(2,1)S(1)}, u32[]{:S(2)}, u32[]{:S(2)}) collective-permute-start(bf16[256,1024]{1,0:T(8,128)(2,1)S(1)} %broadcast_select_fusion), channel_id=1, source_target_pairs={{0,16},{8,0},{16,24},{24,8},{1,17},{9,1},{17,25},{25,9},{2,18},{10... | collective-permute-start | bytes 1572872 | tf_op jit(solution)/shard_map/ppermute | solution.py:281
  76.2 2.3 %collective-permute-start.16 = (bf16[128,1024]{1,0:T(8,128)(2,1)S(1)}, bf16[128,1024]{1,0:T(8,128)(2,1)S(1)}, u32[]{:S(2)}, u32[]{:S(2)}) collective-permute-start(bf16[128,1024]{1,0:T(8,128)(2,1)S(1)} %split.1), channel_id=1, source_target_pairs={{0,1},{1,0},{2,3},{3,2},{4,5},{5,4},{6,7},{7,6},{8,9},{9,8},{10,11... | collective-permute-start | bytes 786440 | tf_op jit(solution)/shard_map/ppermute | solution.py:28
  76.8 1.6 %copy-start.5 = (s32[128,1]{0,1:T(1,128)S(1)}, s32[128,1]{0,1:T(1,128)}, u32[]{:S(2)}) copy-start(s32[128,1]{0,1:T(1,128)} %param.6) | copy-start | bytes 1540

commit v4 on v3

--- a/solution.py
+++ b/solution.py
@@ -252,10 +252,9 @@
     got = list(placed)
     for k in range(2, experts, 2):
         got[k] = swap(placed[k], "expert", k)
-    later = after(placed[1::2], *got[2::2], *([touched] if TOUCH else []))
-    for k, value in zip(range(1, experts, 2), later):
-        got[k] = swap(value, "expert", k)
-    cuts = [cuts[0], *after([cuts[1]], got[2]), *cuts[2:]] if groups > 1 else cuts
+    for k in range(3, experts, 2):
+        got[k] = swap(after([placed[k]], got[experts - k + 1 if k > 1 else 2], *([touched] if k == 3 else []))[0], "expert", k)
+    got[1] = swap(after([placed[1]], got[2])[0], "expert", 1)
     cuts = [swap(cut, "dp", k + 1) for k, cut in enumerate(cuts)]
 
     act, dpre, own = pl.pallas_call(

time: 84.6 us -> 83.2 us (0.983)
  waiting for transfers between devices: 32.5 us -> 29.3 us
  starting transfers between devices: 33 us -> 34.7 us
    ppermute x19, waiting for transfers between devices: 30.1 us -> 26.5 us  [swap(): return lax.ppermute(value, axis, [(i, i ^ offset) for i in range(count)])]
    ppermute x1, starting transfers between devices: 10.3 us -> 11.7 us  [on_device(): lax.ppermute(value, 'dp', [(0, 2), (1, 0), (2, 3), (3, 1)])]
  transfers between devices with their start and end apart: 20 -> 20, of which waited for: 9 -> 11; matrix products, arithmetic and copies ran while one was open for 0% -> 0% of each run, Pallas kernels for 7% -> 7%
where the time goes in v4:
time: 83.2 us; the launch traced here: 82.8 us
  starting transfers between devices  34.7 us (42%)
  waiting for transfers between devices  29.3 us (35%)
  Pallas kernels  11.5 us (14%)
  local copies, waits for them, and re-layouts  6.52 us (8%)
    ppermute x19, waiting for transfers between devices, swap(): return lax.ppermute(value, axis, [(i, i ^ offset) for i in range(count)])  26.5 us
    ppermute x19, starting transfers between devices, swap(): return lax.ppermute(value, axis, [(i, i ^ offset) for i in range(count)])  23.1 us
    ppermute x1, starting transfers between devices, on_device(): lax.ppermute(value, 'dp', [(0, 2), (1, 0), (2, 3), (3, 1)])  11.7 us
    unnamed x14, local copies, waits for them, and re-layouts  6.52 us
    ppermute x1, waiting for transfers between devices, on_device(): lax.ppermute(value, 'dp', [(0, 2), (1, 0), (2, 3), (3, 1)])  2.77 us
    pallas_call x1, Pallas kernels, on_device(): pl.pallas_call(functools.partial(forward_kernel, (experts, width, inner,...  2.37 us
    pallas_call x1, Pallas kernels, on_device(): pl.pallas_call(functools.partial(share_kernel, (experts, slots, groups, c...  2.3 us
    pallas_call x1, Pallas kernels, on_device(): pl.pallas_call(functools.partial(grad_kernel, 2), out_shape=jax.ShapeDtyp...  2.25 us
  transfers between devices with their start and end apart: 20, of which 11 were waited for; matrix products, arithmetic and copies ran while one was open for 0% of the time, Pallas kernels for 7%

profile of v4, /device:TPU:0, one launch (start us, length us, event | category | flops | bytes accessed | tf_op | source)
XLA Modules:
  0.0 82.8 jit_solution(9491548492651547600)
XLA Ops:
  0.6 1.2 %copy-done.2 = bf16[128,3584]{1,0:T(8,128)(2,1)S(1)} copy-done((bf16[128,3584]{1,0:T(8,128)(2,1)S(1)}, bf16[128,3584]{1,0:T(8,128)(2,1)}, u32[]{:S(2)}) %copy-start.2) | copy-done | bytes 917528
  1.8 0.9 %copy-done.3 = bf16[128,1024]{1,0:T(8,128)(2,1)S(1)} copy-done((bf16[128,1024]{1,0:T(8,128)(2,1)S(1)}, bf16[128,1024]{1,0:T(8,128)(2,1)}, u32[]{:S(2)}) %copy-start.3) | copy-done | bytes 262168
  2.8 0.7 copy-done.4
  3.4 0.7 copy-done.6
  4.1 1.2 %place.1 = (bf16[32,4736]{1,0:T(8,128)(2,1)S(1)}, bf16[32,4736]{1,0:T(8,128)(2,1)S(1)}, bf16[32,4736]{1,0:T(8,128)(2,1)S(1)}, bf16[32,4736]{1,0:T(8,128)(2,1)S(1...) custom-call(s32[1,128]{1,0:T(1,128)S(1)} %bitcast.3, ...), custom_call_target="tpu_custom_call" | custom-call | tf_op jit(solution)/shard_map/place/pallas_call | solution.py:233
  5.3 3.0 %collective-permute-start.6 = (bf16[32,4736]{1,0:T(8,128)(2,1)S(1)}, bf16[32,4736]{1,0:T(8,128)(2,1)S(1)}, u32[]{:S(2)}, u32[]{:S(2)}) collective-permute-start(bf16[32,4736]{1,0:T(8,128)(2,1)S(1)} %get-tuple-element.25), channel_id=1, source_target_pairs={{0,2},{1,3},{2,0},{3,1},{4,6},{5,7},{6,4},{7,5},{8,10},{9,11},{10,... | collective-permute-start | bytes 909320 | tf_op jit(solution)/shard_map/ppermute | solution.py:28
  8.3 1.5 %collective-permute-start.8 = (bf16[32,4736]{1,0:T(8,128)(2,1)S(1)}, bf16[32,4736]{1,0:T(8,128)(2,1)S(1)}, u32[]{:S(2)}, u32[]{:S(2)}) collective-permute-start(bf16[32,4736]{1,0:T(8,128)(2,1)S(1)} %get-tuple-element.27), channel_id=1, source_target_pairs={{0,6},{1,7},{2,4},{3,5},{4,2},{5,3},{6,0},{7,1},{8,14},{9,15},{10,... | collective-permute-start | bytes 909320 | tf_op jit(solution)/shard_map/ppermute | solution.py:28
  9.8 0.1 collective-permute-start.10
  9.8 2.0 %collective-permute-start = (bf16[144,896]{1,0:T(8,128)(2,1)S(1)}, bf16[144,896]{1,0:T(8,128)(2,1)S(1)}, u32[]{:S(2)}, u32[]{:S(2)}) collective-permute-start(bf16[144,896]{1,0:T(8,128)(2,1)S(1)} %get-tuple-element.20), channel_id=1, source_target_pairs={{0,8},{8,0},{16,24},{24,16},{1,9},{9,1},{17,25},{25,17},{2,10},{10... | collective-permute-start | bytes 774152 | tf_op jit(solution)/shard_map/ppermute | solution.py:28
  11.8 2.6 %collective-permute-start.1 = (bf16[144,896]{1,0:T(8,128)(2,1)S(1)}, bf16[144,896]{1,0:T(8,128)(2,1)S(1)}, u32[]{:S(2)}, u32[]{:S(2)}) collective-permute-start(bf16[144,896]{1,0:T(8,128)(2,1)S(1)} %get-tuple-element.21), channel_id=1, source_target_pairs={{0,16},{8,24},{16,0},{24,8},{1,17},{9,25},{17,1},{25,9},{2,18},{10... | collective-permute-start | bytes 774152 | tf_op jit(solution)/shard_map/ppermute | solution.py:28
  14.4 3.1 %copy-done = bf16[1,3584,1024]{2,1,0:T(8,128)(2,1)S(1)} copy-done((bf16[1,3584,1024]{2,1,0:T(8,128)(2,1)S(1)}, bf16[1,3584,1024]{2,1,0:T(8,128)(2,1)}, u32[]{:S(2)}) %copy-start) | copy-done | bytes 7340056
  17.5 0.0 collective-permute-done.6.refs_1_.rest_2_
  17.5 0.1 collective-permute-start.7
  17.6 5.6 %collective-permute-done.8.refs_1_.rest_6_ = bf16[32,4736]{1,0:T(8,128)(2,1)S(1)} collective-permute-done((bf16[32,4736]{1,0:T(8,128)(2,1)S(1)}, bf16[32,4736]{1,0:T(8,128)(2,1)S(1)}, u32[]{:S(2)}, u32[]{:S(2)}) %collective-permute-start.8) | collective-permute-done | bytes 303136 | tf_op jit(solution)/shard_map/ppermute | solution.py:28
  23.3 0.0 collective-permute-start.12
  23.3 1.4 %collective-permute-done.10.refs_1_.rest_4_ = bf16[32,4736]{1,0:T(8,128)(2,1)S(1)} collective-permute-done((bf16[32,4736]{1,0:T(8,128)(2,1)S(1)}, bf16[32,4736]{1,0:T(8,128)(2,1)S(1)}, u32[]{:S(2)}, u32[]{:S(2)}) %collective-permute-start.10) | collective-permute-done | bytes 303136 | tf_op jit(solution)/shard_map/ppermute | solution.py:28
  24.6 0.1 collective-permute-start.9
  24.7 0.0 collective-permute-done.rest_8_.refs_0_
  24.7 1.6 %collective-permute-start.11 = (bf16[32,4736]{1,0:T(8,128)(2,1)S(1)}, bf16[32,4736]{1,0:T(8,128)(2,1)S(1)}, u32[]{:S(2)}, u32[]{:S(2)}) collective-permute-start(bf16[32,4736]{1,0:T(8,128)(2,1)S(1)} %hold.6), channel_id=1, source_target_pairs={{0,5},{1,4},{2,7},{3,6},{4,1},{5,0},{6,3},{7,2},{8,13},{9,12},{10,... | collective-permute-start | bytes 909320 | tf_op jit(solution)/shard_map/ppermute | solution.py:28
  26.3 0.0 collective-permute-done.1.rest_9_.refs_1_
  26.3 3.6 %collective-permute-start.2 = (bf16[144,896]{1,0:T(8,128)(2,1)S(1)}, bf16[144,896]{1,0:T(8,128)(2,1)S(1)}, u32[]{:S(2)}, u32[]{:S(2)}) collective-permute-start(bf16[144,896]{1,0:T(8,128)(2,1)S(1)} %get-tuple-element.22), channel_id=1, source_target_pairs={{0,24},{8,16},{16,8},{24,0},{1,25},{9,17},{17,9},{25,1},{2,26},{10... | collective-permute-start | bytes 774152 | tf_op jit(solution)/shard_map/ppermute | solution.py:28
  29.9 6.7 %collective-permute-done.2.rest_10_.refs_2_ = bf16[144,896]{1,0:T(8,128)(2,1)S(1)} collective-permute-done((bf16[144,896]{1,0:T(8,128)(2,1)S(1)}, bf16[144,896]{1,0:T(8,128)(2,1)S(1)}, u32[]{:S(2)}, u32[]{:S(2)}) %collective-permute-start.2) | collective-permute-done | bytes 258080 | tf_op jit(solution)/shard_map/ppermute | solution.py:28
  36.7 2.0 %collective-permute-done.9.rest_3_ = bf16[32,4736]{1,0:T(8,128)(2,1)S(1)} collective-permute-done((bf16[32,4736]{1,0:T(8,128)(2,1)S(1)}, bf16[32,4736]{1,0:T(8,128)(2,1)S(1)}, u32[]{:S(2)}, u32[]{:S(2)}) %collective-permute-start.9) | collective-permute-done | bytes 303136 | tf_op jit(solution)/shard_map/ppermute | solution.py:28
  38.7 0.4 collective-permute-done.11.rest_5_
  39.1 2.4 %forward.1 = (bf16[256,1024]{1,0:T(8,128)(2,1)S(1)}, bf16[256,1024]{1,0:T(8,128)(2,1)S(1)}, bf16[256,896]{1,0:T(8,128)(2,1)S(1)}) custom-call(bf16[1,3584,1024]{2,1,0:T(8,128)(2,1)S(1)} %copy-done.1, bf16[32,4736]{1,0:T(8,128)(2,1)S(1)} %get-tuple-element.23.tie.rest_0_, bf16[32,4736]{1,0:T(8,128)(2,1)S(1)} %collective-permute-done.7.rest_1_, ...), custom_call_target="tpu_custom_call" | custom-call | tf_op jit(solution)/shard_map/forward/pallas_call | solution.py:260
  41.5 3.7 %collective-permute-start.18 = (bf16[256,1024]{1,0:T(8,128)(2,1)S(1)}, bf16[256,1024]{1,0:T(8,128)(2,1)S(1)}, u32[]{:S(2)}, u32[]{:S(2)}) collective-permute-start(bf16[256,1024]{1,0:T(8,128)(2,1)S(1)} %get-tuple-element.37.refs_0_), channel_id=1, source_target_pairs={{0,24},{8,16},{16,8},{24,0},{1,25},{9,17},{17,9},{25,1},{2,26},{10... | collective-permute-start | bytes 1572872 | tf_op jit(solution)/shard_map/ppermute | solution.py:28
  45.2 0.0 collective-permute-start.3
  45.2 0.5 collective-permute-start.4
  45.7 0.7 collective-permute-start.17
  46.4 0.3 collective-permute-done.3.refs_3_
  46.7 0.5 collective-permute-done.4.refs_4_
  47.2 0.4 collective-permute-done.5.refs_5_
  47.6 2.3 %place_shares.1 = (bf16[64,3712]{1,0:T(8,128)(2,1)S(1)}, bf16[64,3712]{1,0:T(8,128)(2,1)S(1)}, bf16[64,3712]{1,0:T(8,128)(2,1)S(1)}, bf16[64,3712]{1,0:T(8,128)(2,1)S(1)}) custom-call(bf16[144,896]{1,0:T(8,128)(2,1)S(1)} %collective-permute-done.rest_8_.refs_0_, bf16[144,896]{1,0:T(8,128)(2,1)S(1)} %collective-permute-done.1.rest_9_.refs_1_, ...), custom_call_target="tpu_custom_call" | custom-call | tf_op jit(solution)/shard_map/place_shares/pallas_call | solution.py:282
  49.9 1.6 %collective-permute-start.13 = (bf16[64,3712]{1,0:T(8,128)(2,1)S(1)}, bf16[64,3712]{1,0:T(8,128)(2,1)S(1)}, u32[]{:S(2)}, u32[]{:S(2)}) collective-permute-start(bf16[64,3712]{1,0:T(8,128)(2,1)S(1)} %get-tuple-element.33), channel_id=1, source_target_pairs={{0,2},{1,3},{2,0},{3,1},{4,6},{5,7},{6,4},{7,5},{8,10},{9,11},{10,... | collective-permute-start | bytes 1425416 | tf_op jit(solution)/shard_map/ppermute | solution.py:28
  51.5 0.7 collective-permute-start.14
  52.1 1.3 %collective-permute-start.15 = (bf16[64,3712]{1,0:T(8,128)(2,1)S(1)}, bf16[64,3712]{1,0:T(8,128)(2,1)S(1)}, u32[]{:S(2)}, u32[]{:S(2)}) collective-permute-start(bf16[64,3712]{1,0:T(8,128)(2,1)S(1)} %get-tuple-element.35), channel_id=1, source_target_pairs={{0,6},{1,7},{2,4},{3,5},{4,2},{5,3},{6,0},{7,1},{8,14},{9,15},{10,... | collective-permute-start | bytes 1425416 | tf_op jit(solution)/shard_map/ppermute | solution.py:28
  53.4 4.8 %collective-permute-done.18.refs_2_ = bf16[256,1024]{1,0:T(8,128)(2,1)S(1)} collective-permute-done((bf16[256,1024]{1,0:T(8,128)(2,1)S(1)}, bf16[256,1024]{1,0:T(8,128)(2,1)S(1)}, u32[]{:S(2)}, u32[]{:S(2)}) %collective-permute-start.18) | collective-permute-done | bytes 524320 | tf_op jit(solution)/shard_map/ppermute | solution.py:28
  58.2 0.1 broadcast_select_fusion
  58.3 11.7 %collective-permute-start.19 = (bf16[256,1024]{1,0:T(8,128)(2,1)S(1)}, bf16[256,1024]{1,0:T(8,128)(2,1)S(1)}, u32[]{:S(2)}, u32[]{:S(2)}) collective-permute-start(bf16[256,1024]{1,0:T(8,128)(2,1)S(1)} %broadcast_select_fusion), channel_id=1, source_target_pairs={{0,16},{8,0},{16,24},{24,8},{1,17},{9,1},{17,25},{25,9},{2,18},{10... | collective-permute-start | bytes 1572872 | tf_op jit(solution)/shard_map/ppermute | solution.py:280
  69.9 4.4 %collective-permute-done.14.refs_2_ = bf16[64,3712]{1,0:T(8,128)(2,1)S(1)} collective-permute-done((bf16[64,3712]{1,0:T(8,128)(2,1)S(1)}, bf16[64,3712]{1,0:T(8,128)(2,1)S(1)}, u32[]{:S(2)}, u32[]{:S(2)}) %collective-permute-start.14) | collective-permute-done | bytes 475168 | tf_op jit(solution)/shard_map/ppermute | solution.py:28
  74.3 0.1 collective-permute-start.16
  74.4 0.6 turn.1.left_ref
  75.0 0.0 copy-start.5
  75.0 1.6 %sum.1.before_ref = f32[896,1024]{1,0:T(8,128)S(1)} custom-call(bf16[896,1024]{1,0:T(8,128)(2,1)S(1)} %turn.1.left_ref, bf16[256,1024]{1,0:T(8,128)(2,1)S(1)} %get-tuple-element.37.refs_0_, bf16[256,1024]{1,0:T(8,128)(2,1)S(1)} %collective-permute-done.17.refs_1_, bf16[256,1024]{1,0:T(8,128)(2,1)S(1)} %collective-permute-done.18.refs_2_), custom_call_target="tpu_custom_call" | custom-call | tf_op jit(solution)/shard_map/sum/pallas_call | solution.py:318
  76.6 0.0 collective-permute-done.16.theirs_ref
  76.6 1.2 %unplace.1 = bf16[128,1024]{1,0:T(8,128)(2,1)} custom-call(s32[1,128]{1,0:T(1,128)S(1)} %bitcast.4, bf16[128,1024]{1,0:T(8,128)(2,1)S(1)} %collective-permute-done.16.theirs_ref, bf16[64,3712]{1,0:T(8,128)(2,1)S(1)} %get-tuple-element.32.refs_0_, bf16[64,3712]{1,0:T(8,128)(2,1)S(1)} %collective-permute-done.13.refs_1_, ...), custom_call_target="tpu_custom_call" | custom-call | tf_op jit(solution)/shard_map/unplace/pallas_call | solution.py:299
  77.8 2.8 %collective-permute-done.19.refs_0_ = bf16[256,1024]{1,0:T(8,128)(2,1)S(1)} collective-permute-done((bf16[256,1024]{1,0:T(8,128)(2,1)S(1)}, bf16[256,1024]{1,0:T(8,128)(2,1)S(1)}, u32[]{:S(2)}, u32[]{:S(2)}) %collective-permute-start.19) | collective-permute-done | bytes 524320 | tf_op jit(solution)/shard_map/ppermute | solution.py:280
  80.6 2.3 %grad.1 = f32[896,1024]{1,0:T(8,128)} custom-call(bf16[896,1024]{1,0:T(8,128)(2,1)S(1)} %turn.1.left_ref, f32[896,1024]{1,0:T(8,128)S(1)} %sum.1.before_ref, bf16[256,1024]{1,0:T(8,128)(2,1)S(1)} %collective-permute-done.19.refs_0_), custom_call_target="tpu_custom_call" | custom-call | tf_op jit(solution)/shard_map/grad/pallas_call | solution.py:328
  (20 shorter events, 0.1 us)
Async XLA Ops:
  0.6 1.2 %copy-start.2 = (bf16[128,3584]{1,0:T(8,128)(2,1)S(1)}, bf16[128,3584]{1,0:T(8,128)(2,1)}, u32[]{:S(2)}) copy-start(bf16[128,3584]{1,0:T(8,128)(2,1)} %refs_3_.1) | copy-start | bytes 2752516
  1.8 0.9 %copy-start.3 = (bf16[128,1024]{1,0:T(8,128)(2,1)S(1)}, bf16[128,1024]{1,0:T(8,128)(2,1)}, u32[]{:S(2)}) copy-start(bf16[128,1024]{1,0:T(8,128)(2,1)} %refs_2_.1) | copy-start | bytes 786436
  2.8 0.7 copy-start.4
  3.4 0.7 copy-start.6
  5.3 12.3 %collective-permute-start.6 = (bf16[32,4736]{1,0:T(8,128)(2,1)S(1)}, bf16[32,4736]{1,0:T(8,128)(2,1)S(1)}, u32[]{:S(2)}, u32[]{:S(2)}) collective-permute-start(bf16[32,4736]{1,0:T(8,128)(2,1)S(1)} %get-tuple-element.25), channel_id=1, source_target_pairs={{0,2},{1,3},{2,0},{3,1},{4,6},{5,7},{6,4},{7,5},{8,10},{9,11},{10,... | collective-permute-start | bytes 909320 | tf_op jit(solution)/shard_map/ppermute | solution.py:28
  8.3 15.0 %collective-permute-start.8 = (bf16[32,4736]{1,0:T(8,128)(2,1)S(1)}, bf16[32,4736]{1,0:T(8,128)(2,1)S(1)}, u32[]{:S(2)}, u32[]{:S(2)}) collective-permute-start(bf16[32,4736]{1,0:T(8,128)(2,1)S(1)} %get-tuple-element.27), channel_id=1, source_target_pairs={{0,6},{1,7},{2,4},{3,5},{4,2},{5,3},{6,0},{7,1},{8,14},{9,15},{10,... | collective-permute-start | bytes 909320 | tf_op jit(solution)/shard_map/ppermute | solution.py:28
  9.8 14.9 %collective-permute-start.10 = (bf16[32,4736]{1,0:T(8,128)(2,1)S(1)}, bf16[32,4736]{1,0:T(8,128)(2,1)S(1)}, u32[]{:S(2)}, u32[]{:S(2)}) collective-permute-start(bf16[32,4736]{1,0:T(8,128)(2,1)S(1)} %get-tuple-element.28), channel_id=1, source_target_pairs={{0,4},{1,5},{2,6},{3,7},{4,0},{5,1},{6,2},{7,3},{8,12},{9,13},{10,... | collective-permute-start | bytes 909320 | tf_op jit(solution)/shard_map/ppermute | solution.py:28
  9.8 14.9 %collective-permute-start = (bf16[144,896]{1,0:T(8,128)(2,1)S(1)}, bf16[144,896]{1,0:T(8,128)(2,1)S(1)}, u32[]{:S(2)}, u32[]{:S(2)}) collective-permute-start(bf16[144,896]{1,0:T(8,128)(2,1)S(1)} %get-tuple-element.20), channel_id=1, source_target_pairs={{0,8},{8,0},{16,24},{24,16},{1,9},{9,1},{17,25},{25,17},{2,10},{10... | collective-permute-start | bytes 774152 | tf_op jit(solution)/shard_map/ppermute | solution.py:28
  11.8 14.5 %collective-permute-start.1 = (bf16[144,896]{1,0:T(8,128)(2,1)S(1)}, bf16[144,896]{1,0:T(8,128)(2,1)S(1)}, u32[]{:S(2)}, u32[]{:S(2)}) collective-permute-start(bf16[144,896]{1,0:T(8,128)(2,1)S(1)} %get-tuple-element.21), channel_id=1, source_target_pairs={{0,16},{8,24},{16,0},{24,8},{1,17},{9,25},{17,1},{25,9},{2,18},{10... | collective-permute-start | bytes 774152 | tf_op jit(solution)/shard_map/ppermute | solution.py:28
  14.4 3.1 %copy-start = (bf16[1,3584,1024]{2,1,0:T(8,128)(2,1)S(1)}, bf16[1,3584,1024]{2,1,0:T(8,128)(2,1)}, u32[]{:S(2)}) copy-start(bf16[1,3584,1024]{2,1,0:T(8,128)(2,1)} %weight_ref.3) | copy-start | bytes 22020100
  17.5 21.6 %copy-start.1 = (bf16[1,3584,1024]{2,1,0:T(8,128)(2,1)S(1)}, bf16[1,3584,1024]{2,1,0:T(8,128)(2,1)}, u32[]{:S(2)}) copy-start(bf16[1,3584,1024]{2,1,0:T(8,128)(2,1)} %weight_ref.3) | copy-start | bytes 22020100
  17.5 19.2 %collective-permute-start.7 = (bf16[32,4736]{1,0:T(8,128)(2,1)S(1)}, bf16[32,4736]{1,0:T(8,128)(2,1)S(1)}, u32[]{:S(2)}, u32[]{:S(2)}) collective-permute-start(bf16[32,4736]{1,0:T(8,128)(2,1)S(1)} %hold.4), channel_id=1, source_target_pairs={{0,1},{1,0},{2,3},{3,2},{4,5},{5,4},{6,7},{7,6},{8,9},{9,8},{10,11... | collective-permute-start | bytes 909320 | tf_op jit(solution)/shard_map/ppermute | solution.py:28
  23.3 13.4 %collective-permute-start.12 = (bf16[32,4736]{1,0:T(8,128)(2,1)S(1)}, bf16[32,4736]{1,0:T(8,128)(2,1)S(1)}, u32[]{:S(2)}, u32[]{:S(2)}) collective-permute-start(bf16[32,4736]{1,0:T(8,128)(2,1)S(1)} %hold.7), channel_id=1, source_target_pairs={{0,7},{1,6},{2,5},{3,4},{4,3},{5,2},{6,1},{7,0},{8,15},{9,14},{10,... | collective-permute-start | bytes 909320 | tf_op jit(solution)/shard_map/ppermute | solution.py:28
  24.6 14.1 %collective-permute-start.9 = (bf16[32,4736]{1,0:T(8,128)(2,1)S(1)}, bf16[32,4736]{1,0:T(8,128)(2,1)S(1)}, u32[]{:S(2)}, u32[]{:S(2)}) collective-permute-start(bf16[32,4736]{1,0:T(8,128)(2,1)S(1)} %hold.5), channel_id=1, source_target_pairs={{0,3},{1,2},{2,1},{3,0},{4,7},{5,6},{6,5},{7,4},{8,11},{9,10},{10,... | collective-permute-start | bytes 909320 | tf_op jit(solution)/shard_map/ppermute | solution.py:28
  24.7 14.4 %collective-permute-start.11 = (bf16[32,4736]{1,0:T(8,128)(2,1)S(1)}, bf16[32,4736]{1,0:T(8,128)(2,1)S(1)}, u32[]{:S(2)}, u32[]{:S(2)}) collective-permute-start(bf16[32,4736]{1,0:T(8,128)(2,1)S(1)} %hold.6), channel_id=1, source_target_pairs={{0,5},{1,4},{2,7},{3,6},{4,1},{5,0},{6,3},{7,2},{8,13},{9,12},{10,... | collective-permute-start | bytes 909320 | tf_op jit(solution)/shard_map/ppermute | solution.py:28
  26.3 10.3 %collective-permute-start.2 = (bf16[144,896]{1,0:T(8,128)(2,1)S(1)}, bf16[144,896]{1,0:T(8,128)(2,1)S(1)}, u32[]{:S(2)}, u32[]{:S(2)}) collective-permute-start(bf16[144,896]{1,0:T(8,128)(2,1)S(1)} %get-tuple-element.22), channel_id=1, source_target_pairs={{0,24},{8,16},{16,8},{24,0},{1,25},{9,17},{17,9},{25,1},{2,26},{10... | collective-permute-start | bytes 774152 | tf_op jit(solution)/shard_map/ppermute | solution.py:28
  41.5 16.7 %collective-permute-start.18 = (bf16[256,1024]{1,0:T(8,128)(2,1)S(1)}, bf16[256,1024]{1,0:T(8,128)(2,1)S(1)}, u32[]{:S(2)}, u32[]{:S(2)}) collective-permute-start(bf16[256,1024]{1,0:T(8,128)(2,1)S(1)} %get-tuple-element.37.refs_0_), channel_id=1, source_target_pairs={{0,24},{8,16},{16,8},{24,0},{1,25},{9,17},{17,9},{25,1},{2,26},{10... | collective-permute-start | bytes 1572872 | tf_op jit(solution)/shard_map/ppermute | solution.py:28
  45.2 1.5 %collective-permute-start.3 = (bf16[144,896]{1,0:T(8,128)(2,1)S(1)}, bf16[144,896]{1,0:T(8,128)(2,1)S(1)}, u32[]{:S(2)}, u32[]{:S(2)}) collective-permute-start(bf16[144,896]{1,0:T(8,128)(2,1)S(1)} %collective-permute-done.rest_8_.refs_0_), channel_id=1, source_target_pairs={{0,1},{1,0},{2,3},{3,2},{4,5},{5,4},{6,7},{7,6},{8,9},{9,8},{10,11... | collective-permute-start | bytes 774152 | tf_op jit(solution)/shard_map/ppermute | solution.py:28
  45.2 2.0 %collective-permute-start.4 = (bf16[144,896]{1,0:T(8,128)(2,1)S(1)}, bf16[144,896]{1,0:T(8,128)(2,1)S(1)}, u32[]{:S(2)}, u32[]{:S(2)}) collective-permute-start(bf16[144,896]{1,0:T(8,128)(2,1)S(1)} %collective-permute-done.1.rest_9_.refs_1_), channel_id=1, source_target_pairs={{0,1},{1,0},{2,3},{3,2},{4,5},{5,4},{6,7},{7,6},{8,9},{9,8},{10,11... | collective-permute-start | bytes 774152 | tf_op jit(solution)/shard_map/ppermute | solution.py:28
  45.7 1.9 %collective-permute-start.5 = (bf16[144,896]{1,0:T(8,128)(2,1)S(1)}, bf16[144,896]{1,0:T(8,128)(2,1)}, u32[]{:S(2)}, u32[]{:S(2)}) collective-permute-start(bf16[144,896]{1,0:T(8,128)(2,1)S(1)} %collective-permute-done.2.rest_10_.refs_2_), channel_id=1, source_target_pairs={{0,1},{1,0},{2,3},{3,2},{4,5},{5,4},{6,7},{7,6},{8,9},{9,8},{10,11... | collective-permute-start | bytes 774152 | tf_op jit(solution)/shard_map/ppermute | solution.py:28
  45.7 29.3 %collective-permute-start.17 = (bf16[256,1024]{1,0:T(8,128)(2,1)S(1)}, bf16[256,1024]{1,0:T(8,128)(2,1)S(1)}, u32[]{:S(2)}, u32[]{:S(2)}) collective-permute-start(bf16[256,1024]{1,0:T(8,128)(2,1)S(1)} %get-tuple-element.37.refs_0_), channel_id=1, source_target_pairs={{0,8},{8,0},{16,24},{24,16},{1,9},{9,1},{17,25},{25,17},{2,10},{10... | collective-permute-start | bytes 1572872 | tf_op jit(solution)/shard_map/ppermute | solution.py:28
  49.9 20.1 %collective-permute-start.13 = (bf16[64,3712]{1,0:T(8,128)(2,1)S(1)}, bf16[64,3712]{1,0:T(8,128)(2,1)S(1)}, u32[]{:S(2)}, u32[]{:S(2)}) collective-permute-start(bf16[64,3712]{1,0:T(8,128)(2,1)S(1)} %get-tuple-element.33), channel_id=1, source_target_pairs={{0,2},{1,3},{2,0},{3,1},{4,6},{5,7},{6,4},{7,5},{8,10},{9,11},{10,... | collective-permute-start | bytes 1425416 | tf_op jit(solution)/shard_map/ppermute | solution.py:28
  51.5 22.8 %collective-permute-start.14 = (bf16[64,3712]{1,0:T(8,128)(2,1)S(1)}, bf16[64,3712]{1,0:T(8,128)(2,1)S(1)}, u32[]{:S(2)}, u32[]{:S(2)}) collective-permute-start(bf16[64,3712]{1,0:T(8,128)(2,1)S(1)} %get-tuple-element.34), channel_id=1, source_target_pairs={{0,4},{1,5},{2,6},{3,7},{4,0},{5,1},{6,2},{7,3},{8,12},{9,13},{10,... | collective-permute-start | bytes 1425416 | tf_op jit(solution)/shard_map/ppermute | solution.py:28
  52.1 22.2 %collective-permute-start.15 = (bf16[64,3712]{1,0:T(8,128)(2,1)S(1)}, bf16[64,3712]{1,0:T(8,128)(2,1)S(1)}, u32[]{:S(2)}, u32[]{:S(2)}) collective-permute-start(bf16[64,3712]{1,0:T(8,128)(2,1)S(1)} %get-tuple-element.35), channel_id=1, source_target_pairs={{0,6},{1,7},{2,4},{3,5},{4,2},{5,3},{6,0},{7,1},{8,14},{9,15},{10,... | collective-permute-start | bytes 1425416 | tf_op jit(solution)/shard_map/ppermute | solution.py:28
  58.3 22.3 %collective-permute-start.19 = (bf16[256,1024]{1,0:T(8,128)(2,1)S(1)}, bf16[256,1024]{1,0:T(8,128)(2,1)S(1)}, u32[]{:S(2)}, u32[]{:S(2)}) collective-permute-start(bf16[256,1024]{1,0:T(8,128)(2,1)S(1)} %broadcast_select_fusion), channel_id=1, source_target_pairs={{0,16},{8,0},{16,24},{24,8},{1,17},{9,1},{17,25},{25,9},{2,18},{10... | collective-permute-start | bytes 1572872 | tf_op jit(solution)/shard_map/ppermute | solution.py:280
  74.3 2.3 %collective-permute-start.16 = (bf16[128,1024]{1,0:T(8,128)(2,1)S(1)}, bf16[128,1024]{1,0:T(8,128)(2,1)S(1)}, u32[]{:S(2)}, u32[]{:S(2)}) collective-permute-start(bf16[128,1024]{1,0:T(8,128)(2,1)S(1)} %split.1), channel_id=1, source_target_pairs={{0,1},{1,0},{2,3},{3,2},{4,5},{5,4},{6,7},{7,6},{8,9},{9,8},{10,11... | collective-permute-start | bytes 786440 | tf_op jit(solution)/shard_map/ppermute | solution.py:28
  75.0 1.6 %copy-start.5 = (s32[128,1]{0,1:T(1,128)S(1)}, s32[128,1]{0,1:T(1,128)}, u32[]{:S(2)}) copy-start(s32[128,1]{0,1:T(1,128)} %param.6) | copy-start | bytes 1540

commit v5 on v4

--- a/solution.py
+++ b/solution.py
@@ -110,8 +110,11 @@
 
 
 def forward_kernel(sizes, weight_ref, *rest):
-    experts, width, inner, share = sizes
-    blocks, (act_ref, dpre_ref, own_ref, all_ref) = rest[:experts], rest[-4:]
+    count, width, inner, share = sizes
+    blocks, (act_ref, dpre_ref, own_ref, all_ref) = rest[:count], rest[-4:]
+    joined = dpre_ref.shape[0] - all_ref.shape[0]
+    if joined:
+        dpre_ref[:joined, :] = rest[count][...]
     slots = blocks[0].shape[0]
     for k, block in enumerate(blocks):
         all_ref[k * slots : (k + 1) * slots, :] = block[...]
@@ -120,7 +123,7 @@
     gate = all_ref[:, width + inner :][:, :1].astype(F32)
     sig = jax.nn.sigmoid(pre)
     gated = gate * sig
-    dpre_ref[...] = (cots * gated * (1.0 + pre * (1.0 - sig))).astype(BF16)
+    dpre_ref[joined:, :] = (cots * gated * (1.0 + pre * (1.0 - sig))).astype(BF16)
     act_ref[...] = (gated * pre).astype(BF16)
     own_ref[...] = columns(all_ref.at[:, :width], lax.axis_index("dp"), share)
 
@@ -128,12 +131,14 @@
 def share_kernel(sizes, *refs):
     experts, slots, groups, count = sizes
     pairs = experts // 2
-    mine, theirs, act_ref = refs[:groups], refs[groups : 2 * groups], refs[2 * groups]
-    outs = refs[2 * groups + 1 :]
+    mine, theirs, acts = refs[:groups], refs[groups : 2 * groups], refs[2 * groups : 2 * groups + 2]
+    outs = refs[2 * groups + 2 :]
     share = mine[0].shape[1]
     me = lax.axis_index("expert")
     for j, out in enumerate(outs):
-        out[:, groups * share :] = act_ref[2 * j * slots : 2 * (j + 1) * slots]
+        for r in range(2):
+            here = slice(j * slots, (j + 1) * slots)
+            out[r * slots : (r + 1) * slots, groups * share :] = acts[r][here]
     for g in range(groups):
         placed = []
         for block in (mine[g], theirs[g]):
@@ -168,13 +173,16 @@
     out_ref[...] = total.astype(BF16)
 
 
-def turn_kernel(groups, own_ref, *refs):
-    *blocks, out_ref = refs
-    share, rows = out_ref.shape[0], own_ref.shape[0]
-    out_ref[:, :rows] = own_ref[...].T
-    for g in range(groups):
-        value = [block[:, g * share : (g + 1) * share] for block in blocks]
-        out_ref[:, (g + 1) * rows : (g + 2) * rows] = jnp.concatenate(value, axis=0).T
+def turn_kernel(groups, *refs):
+    own, blocks, out_ref = refs[:2], refs[2:-1], refs[-1]
+    share, rows = out_ref.shape[0], own[0].shape[0]
+    slots = blocks[0].shape[0] // 2
+    for r in range(2):
+        out_ref[:, r * rows : (r + 1) * rows] = own[r][...].T
+        for g in range(groups):
+            value = [block[r * slots : (r + 1) * slots, g * share : (g + 1) * share] for block in blocks]
+            at = (2 * g + 2 + r) * rows
+            out_ref[:, at : at + rows] = jnp.concatenate(value, axis=0).T
 
 
 def sum_kernel(groups, left_ref, *refs):
@@ -257,36 +265,44 @@
     got[1] = swap(after([placed[1]], got[2])[0], "expert", 1)
     cuts = [swap(cut, "dp", k + 1) for k, cut in enumerate(cuts)]
 
-    act, dpre, own = pl.pallas_call(
-        functools.partial(forward_kernel, (experts, width, inner, share)),
-        out_shape=[struct(rows, inner), struct(rows, inner), struct(rows, share)],
-        in_specs=[VMEM] * (1 + experts) + [ANY] * groups,
-        out_specs=[VMEM] * 3,
-        scratch_shapes=[pltpu.VMEM((rows, wide), BF16)],
-        compiler_params=limit(SMALL),
-        name="forward",
-    )(weights, *got, *cuts)
-    dpres = [dpre]
-
+    def forward(blocks, before, *ties):
+        height = len(blocks) * slots
+        joined = height + sum(value.shape[0] for value in before)
+        return pl.pallas_call(
+            functools.partial(forward_kernel, (len(blocks), width, inner, share)),
+            out_shape=[struct(height, inner), struct(joined, inner), struct(height, share)],
+            in_specs=[VMEM] * (1 + len(blocks) + len(before)) + [ANY] * len(ties),
+            out_specs=[VMEM] * 3,
+            scratch_shapes=[pltpu.VMEM((height, wide), BF16)],
+            compiler_params=limit(SMALL),
+            name="forward",
+        )(weights, *blocks, *before, *ties)
+
+    act, half, own = forward(got[::2], [], cuts[0])
+    acts, owns = [act], [own]
+    early = [swap(half, "dp", 3)] if chain else []
+    crossed = [swap(cut, "expert", 1) for cut in cuts]
+    act, dpre, own = forward(got[1::2], [half], *cuts, crossed[0])
+    acts, owns, dpres = acts + [act], owns + [own], [dpre]
     gathered = [[] for _ in range(groups)]
-    for value in dpres:
-        for k in range(1, members):
-            if not (chain and k == 2):
-                gathered[k - 1].append(swap(value, "dp", k))
+    for k in range(1, members):
+        if chain and k == 3:
+            gathered[2] = [*early, swap(dpre[rows // 2 :], "dp", 3)]
+        elif not (chain and k == 2):
+            gathered[k - 1].append(swap(dpre, "dp", k))
     if chain:
         ends = (group == 0) | (group == 3)
-        for value, far in zip(dpres, gathered[2]):
-            value = jnp.where(ends, value, far)
-            gathered[1].append(lax.ppermute(value, "dp", [(0, 2), (1, 0), (2, 3), (3, 1)]))
+        value = jnp.where(ends, dpre, jnp.concatenate(gathered[2], axis=0))
+        gathered[1].append(lax.ppermute(value, "dp", [(0, 2), (1, 0), (2, 3), (3, 1)]))
 
     sent = pl.pallas_call(
         functools.partial(share_kernel, (experts, slots, groups, count)),
         out_shape=[struct(2 * slots, groups * share + inner)] * pairs,
-        in_specs=[VMEM] * (1 + 2 * groups),
+        in_specs=[VMEM] * (2 + 2 * groups),
         out_specs=[VMEM] * pairs,
         compiler_params=limit(SMALL),
         name="place_shares",
-    )(*cuts, *[swap(cut, "expert", 1) for cut in cuts], act)
+    )(*cuts, *crossed, *acts)
     lefts = [sent[0]] + [swap(sent[j], "expert", 2 * j) for j in range(1, pairs)]
     theirs = pl.pallas_call(
         functools.partial(split_kernel, slots, inner),
@@ -309,11 +325,11 @@
         left = pl.pallas_call(
             functools.partial(turn_kernel, groups),
             out_shape=struct(share, members * rows),
-            in_specs=[VMEM] * (1 + pairs),
+            in_specs=[VMEM] * (2 + pairs),
             out_specs=VMEM,
             compiler_params=limit(SMALL),
             name="turn",
-        )(own, *lefts)
+        )(*owns, *lefts)
         pieces = [*dpres] + gathered[0] + gathered[2]
         before = pl.pallas_call(
             functools.partial(sum_kernel, (0, 1, 3)),
@@ -339,9 +355,10 @@
             name="grad",
         )(left, before, *gathered[1])
         return (hidden, grad[None])
-    left, right = [own], list(dpres)
+    left, right = list(owns), list(dpres)
     for g in range(groups):
-        left += [block[:, g * share : (g + 1) * share] for block in lefts]
+        here = slice(g * share, (g + 1) * share)
+        left += [b[r * slots : (r + 1) * slots, here] for r in range(2) for b in lefts]
         right += gathered[g]
     grad = lax.dot_general(
         jnp.concatenate(left, axis=0),
@@ -352,7 +369,7 @@
     return (hidden, grad[None])
 
 
-BIG, SMALL, TOUCH = 40, 12, True
+BIG, SMALL, TOUCH, TIES = 40, 12, True, 1
 
 
 def solution(mesh):

time: 83.2 us -> 81 us (0.974)
  waiting for transfers between devices: 29.3 us -> 24.3 us
  starting transfers between devices: 34.7 us -> 36.6 us
  local copies, waits for them, and re-layouts: 6.52 us -> 7.92 us
    ppermute x19 -> x20, starting transfers between devices: 23.1 us -> 27.9 us  [swap(): return lax.ppermute(value, axis, [(i, i ^ offset) for i in range(count)])]
    ppermute x1, starting transfers between devices: 11.7 us -> 8.7 us  [on_device(): lax.ppermute(value, 'dp', [(0, 2), (1, 0), (2, 3), (3, 1)])]
    ppermute x1, waiting for transfers between devices: 2.77 us -> 0.01 us  [on_device(): lax.ppermute(value, 'dp', [(0, 2), (1, 0), (2, 3), (3, 1)])]
    ppermute x19 -> x20, waiting for transfers between devices: 26.5 us -> 24.3 us  [swap(): return lax.ppermute(value, axis, [(i, i ^ offset) for i in range(count)])]
    pallas_call x1, Pallas kernels: 2.3 us -> 1.33 us  [on_device(): pl.pallas_call(functools.partial(share_kernel, (experts, slots, groups, c...]
    unnamed x14 -> x22, local copies, waits for them, and re-layouts: 6.52 us -> 7.2 us
    pallas_call x1 -> x2, Pallas kernels: 2.37 us -> 2.67 us  [forward(): pl.pallas_call(functools.partial(forward_kernel, (len(blocks), width, inn...]
  transfers between devices with their start and end apart: 20 -> 21, of which waited for: 11 -> 9; matrix products, arithmetic and copies ran while one was open for 0% -> 1% of each run, Pallas kernels for 7% -> 9%
where the time goes in v5:
time: 81 us; the launch traced here: 80.7 us
  starting transfers between devices  36.6 us (45%)
  waiting for transfers between devices  24.3 us (30%)
  Pallas kernels  10.8 us (13%)
  local copies, waits for them, and re-layouts  7.92 us (10%)
  between operations  0.84 us (1%)
    ppermute x20, starting transfers between devices, swap(): return lax.ppermute(value, axis, [(i, i ^ offset) for i in range(count)])  27.9 us
    ppermute x20, waiting for transfers between devices, swap(): return lax.ppermute(value, axis, [(i, i ^ offset) for i in range(count)])  24.3 us
    ppermute x1, starting transfers between devices, on_device(): lax.ppermute(value, 'dp', [(0, 2), (1, 0), (2, 3), (3, 1)])  8.7 us
    unnamed x22, local copies, waits for them, and re-layouts  7.2 us
    pallas_call x2, Pallas kernels, forward(): pl.pallas_call(functools.partial(forward_kernel, (len(blocks), width, inn...  2.67 us
    pallas_call x1, Pallas kernels, on_device(): pl.pallas_call(functools.partial(grad_kernel, 2), out_shape=jax.ShapeDtyp...  2.26 us
  transfers between devices with their start and end apart: 21, of which 9 were waited for; matrix products, arithmetic and copies ran while one was open for 1% of the time, Pallas kernels for 9%

profile of v5, /device:TPU:0, one launch (start us, length us, event | category | flops | bytes accessed | tf_op | source)
XLA Modules:
  0.0 80.7 jit_solution(12543744118284679463)
XLA Ops:
  0.6 1.2 %copy-done.2 = bf16[128,3584]{1,0:T(8,128)(2,1)S(1)} copy-done((bf16[128,3584]{1,0:T(8,128)(2,1)S(1)}, bf16[128,3584]{1,0:T(8,128)(2,1)}, u32[]{:S(2)}) %copy-start.2) | copy-done | bytes 917528
  1.8 0.9 %copy-done.3 = bf16[128,1024]{1,0:T(8,128)(2,1)S(1)} copy-done((bf16[128,1024]{1,0:T(8,128)(2,1)S(1)}, bf16[128,1024]{1,0:T(8,128)(2,1)}, u32[]{:S(2)}) %copy-start.3) | copy-done | bytes 262168
  2.8 0.7 copy-done.8
  3.4 0.7 copy-done.10
  4.1 1.2 %place.1 = (bf16[32,4736]{1,0:T(8,128)(2,1)S(1)}, bf16[32,4736]{1,0:T(8,128)(2,1)S(1)}, bf16[32,4736]{1,0:T(8,128)(2,1)S(1)}, bf16[32,4736]{1,0:T(8,128)(2,1)S(1...) custom-call(s32[1,128]{1,0:T(1,128)S(1)} %bitcast.3, ...), custom_call_target="tpu_custom_call" | custom-call | tf_op jit(solution)/shard_map/place/pallas_call | solution.py:241
  5.3 3.0 %collective-permute-start.6 = (bf16[32,4736]{1,0:T(8,128)(2,1)S(1)}, bf16[32,4736]{1,0:T(8,128)(2,1)S(1)}, u32[]{:S(2)}, u32[]{:S(2)}) collective-permute-start(bf16[32,4736]{1,0:T(8,128)(2,1)S(1)} %get-tuple-element.27), channel_id=1, source_target_pairs={{0,2},{1,3},{2,0},{3,1},{4,6},{5,7},{6,4},{7,5},{8,10},{9,11},{10,... | collective-permute-start | bytes 909320 | tf_op jit(solution)/shard_map/ppermute | solution.py:28
  8.3 1.5 %collective-permute-start.7 = (bf16[32,4736]{1,0:T(8,128)(2,1)S(1)}, bf16[32,4736]{1,0:T(8,128)(2,1)S(1)}, u32[]{:S(2)}, u32[]{:S(2)}) collective-permute-start(bf16[32,4736]{1,0:T(8,128)(2,1)S(1)} %get-tuple-element.28), channel_id=1, source_target_pairs={{0,4},{1,5},{2,6},{3,7},{4,0},{5,1},{6,2},{7,3},{8,12},{9,13},{10,... | collective-permute-start | bytes 909320 | tf_op jit(solution)/shard_map/ppermute | solution.py:28
  9.8 0.0 collective-permute-start.8
  9.8 2.0 %collective-permute-start = (bf16[144,896]{1,0:T(8,128)(2,1)S(1)}, bf16[144,896]{1,0:T(8,128)(2,1)S(1)}, u32[]{:S(2)}, u32[]{:S(2)}) collective-permute-start(bf16[144,896]{1,0:T(8,128)(2,1)S(1)} %get-tuple-element.23), channel_id=1, source_target_pairs={{0,8},{8,0},{16,24},{24,16},{1,9},{9,1},{17,25},{25,17},{2,10},{10... | collective-permute-start | bytes 774152 | tf_op jit(solution)/shard_map/ppermute | solution.py:28
  11.8 2.6 %collective-permute-start.1 = (bf16[144,896]{1,0:T(8,128)(2,1)S(1)}, bf16[144,896]{1,0:T(8,128)(2,1)S(1)}, u32[]{:S(2)}, u32[]{:S(2)}) collective-permute-start(bf16[144,896]{1,0:T(8,128)(2,1)S(1)} %get-tuple-element.24), channel_id=1, source_target_pairs={{0,16},{8,24},{16,0},{24,8},{1,17},{9,25},{17,1},{25,9},{2,18},{10... | collective-permute-start | bytes 774152 | tf_op jit(solution)/shard_map/ppermute | solution.py:28
  14.4 1.8 %collective-permute-done.6.rest_1_.refs_1_ = bf16[32,4736]{1,0:T(8,128)(2,1)S(1)} collective-permute-done((bf16[32,4736]{1,0:T(8,128)(2,1)S(1)}, bf16[32,4736]{1,0:T(8,128)(2,1)S(1)}, u32[]{:S(2)}, u32[]{:S(2)}) %collective-permute-start.6) | collective-permute-done | bytes 303136 | tf_op jit(solution)/shard_map/ppermute | solution.py:28
  16.3 4.2 %collective-permute-start.2 = (bf16[144,896]{1,0:T(8,128)(2,1)S(1)}, bf16[144,896]{1,0:T(8,128)(2,1)S(1)}, u32[]{:S(2)}, u32[]{:S(2)}) collective-permute-start(bf16[144,896]{1,0:T(8,128)(2,1)S(1)} %get-tuple-element.25), channel_id=1, source_target_pairs={{0,24},{8,16},{16,8},{24,0},{1,25},{9,17},{17,9},{25,1},{2,26},{10... | collective-permute-start | bytes 774152 | tf_op jit(solution)/shard_map/ppermute | solution.py:28
  20.4 3.1 %copy-done = bf16[1,3584,1024]{2,1,0:T(8,128)(2,1)S(1)} copy-done((bf16[1,3584,1024]{2,1,0:T(8,128)(2,1)S(1)}, bf16[1,3584,1024]{2,1,0:T(8,128)(2,1)}, u32[]{:S(2)}) %copy-start) | copy-done | bytes 7340056
  23.5 0.0 collective-permute-done.7.rest_2_.refs_1_
  23.5 0.1 collective-permute-start.9
  23.6 0.0 collective-permute-done.8.rest_3_.refs_1_
  23.6 2.6 %collective-permute-start.12 = (bf16[32,4736]{1,0:T(8,128)(2,1)S(1)}, bf16[32,4736]{1,0:T(8,128)(2,1)S(1)}, u32[]{:S(2)}, u32[]{:S(2)}) collective-permute-start(bf16[32,4736]{1,0:T(8,128)(2,1)S(1)} %hold.7), channel_id=1, source_target_pairs={{0,7},{1,6},{2,5},{3,4},{4,3},{5,2},{6,1},{7,0},{8,15},{9,14},{10,... | collective-permute-start | bytes 909320 | tf_op jit(solution)/shard_map/ppermute | solution.py:28
  26.2 0.2 collective-permute-start.11
  26.4 6.0 %collective-permute-done.1.rest_6_.refs_1_ = bf16[144,896]{1,0:T(8,128)(2,1)S(1)} collective-permute-done((bf16[144,896]{1,0:T(8,128)(2,1)S(1)}, bf16[144,896]{1,0:T(8,128)(2,1)S(1)}, u32[]{:S(2)}, u32[]{:S(2)}) %collective-permute-start.1) | collective-permute-done | bytes 258080 | tf_op jit(solution)/shard_map/ppermute | solution.py:28
  32.4 0.0 collective-permute-start.10
  32.4 1.6 %collective-permute-start.3 = (bf16[144,896]{1,0:T(8,128)(2,1)S(1)}, bf16[144,896]{1,0:T(8,128)(2,1)S(1)}, u32[]{:S(2)}, u32[]{:S(2)}) collective-permute-start(bf16[144,896]{1,0:T(8,128)(2,1)S(1)} %collective-permute-done.rest_4_.rest_5_.refs_0_), channel_id=1, source_target_pairs={{0,1},{1,0},{2,3},{3,2},{4,5},{5,4},{6,7},{7,6},{8,9},{9,8},{10,11... | collective-permute-start | bytes 774152 | tf_op jit(solution)/shard_map/ppermute | solution.py:28
  34.0 1.3 %forward.2 = (bf16[128,1024]{1,0:T(8,128)(2,1)S(1)}, bf16[128,1024]{1,0:T(8,128)(2,1)S(1)}, bf16[128,896]{1,0:T(8,128)(2,1)S(1)}) custom-call(bf16[1,3584,1024]{2,1,0:T(8,128)(2,1)S(1)} %copy-done.1, bf16[32,4736]{1,0:T(8,128)(2,1)S(1)} %get-tuple-element.26.rest_0_.tie, bf16[32,4736]{1,0:T(8,128)(2,1)S(1)} %collective-permute-done.6.rest_1_.refs_1_, ...), custom_call_target="tpu_custom_call" | custom-call | tf_op jit(solution)/shard_map/forward/pallas_call | solution.py:271
  35.4 0.0 copy-start.4
  35.4 3.1 %collective-permute-start.18 = (bf16[128,1024]{1,0:T(8,128)(2,1)S(1)}, bf16[128,1024]{1,0:T(8,128)(2,1)S(1)}, u32[]{:S(2)}, u32[]{:S(2)}) collective-permute-start(bf16[128,1024]{1,0:T(8,128)(2,1)S(1)} %get-tuple-element.35.rest_4_), channel_id=1, source_target_pairs={{0,24},{8,16},{16,8},{24,0},{1,25},{9,17},{17,9},{25,1},{2,26},{10... | collective-permute-start | bytes 786440 | tf_op jit(solution)/shard_map/ppermute | solution.py:28
  38.5 2.1 %collective-permute-done.11.rest_2_ = bf16[32,4736]{1,0:T(8,128)(2,1)S(1)} collective-permute-done((bf16[32,4736]{1,0:T(8,128)(2,1)S(1)}, bf16[32,4736]{1,0:T(8,128)(2,1)S(1)}, u32[]{:S(2)}, u32[]{:S(2)}) %collective-permute-start.11) | collective-permute-done | bytes 303136 | tf_op jit(solution)/shard_map/ppermute | solution.py:28
  40.6 1.3 %collective-permute-done.10.rest_1_ = bf16[32,4736]{1,0:T(8,128)(2,1)S(1)} collective-permute-done((bf16[32,4736]{1,0:T(8,128)(2,1)S(1)}, bf16[32,4736]{1,0:T(8,128)(2,1)S(1)}, u32[]{:S(2)}, u32[]{:S(2)}) %collective-permute-start.10) | collective-permute-done | bytes 303136 | tf_op jit(solution)/shard_map/ppermute | solution.py:28
  41.9 1.3 %forward.3 = (bf16[128,1024]{1,0:T(8,128)(2,1)S(1)}, bf16[256,1024]{1,0:T(8,128)(2,1)S(1)}, bf16[128,896]{1,0:T(8,128)(2,1)S(1)}) custom-call(bf16[1,3584,1024]{2,1,0:T(8,128)(2,1)S(1)} %copy-done.1, bf16[32,4736]{1,0:T(8,128)(2,1)S(1)} %collective-permute-done.9.rest_0_, bf16[32,4736]{1,0:T(8,128)(2,1)S(1)} %collective-permute-done.10.rest_1_, ...), custom_call_target="tpu_custom_call" | custom-call | tf_op jit(solution)/shard_map/forward/pallas_call | solution.py:271
  43.2 0.7 copy-done.6
  43.9 0.7 slice.3
  44.6 3.0 %collective-permute-start.19 = (bf16[128,1024]{1,0:T(8,128)(2,1)}, bf16[128,1024]{1,0:T(8,128)(2,1)S(1)}, u32[]{:S(2)}, u32[]{:S(2)}) collective-permute-start(bf16[128,1024]{1,0:T(8,128)(2,1)} %slice.3), channel_id=1, source_target_pairs={{0,24},{8,16},{16,8},{24,0},{1,25},{9,17},{17,9},{25,1},{2,26},{10... | collective-permute-start | bytes 786440 | tf_op jit(solution)/shard_map/ppermute | solution.py:28
  47.6 0.5 collective-permute-start.5
  48.1 1.0 %collective-permute-done.4.refs_4_ = bf16[144,896]{1,0:T(8,128)(2,1)S(1)} collective-permute-done((bf16[144,896]{1,0:T(8,128)(2,1)S(1)}, bf16[144,896]{1,0:T(8,128)(2,1)S(1)}, u32[]{:S(2)}, u32[]{:S(2)}) %collective-permute-start.4) | collective-permute-done | bytes 258080 | tf_op jit(solution)/shard_map/ppermute | solution.py:28
  49.1 0.4 collective-permute-done.5.refs_5_
  49.5 1.3 %place_shares.1 = (bf16[64,3712]{1,0:T(8,128)(2,1)S(1)}, bf16[64,3712]{1,0:T(8,128)(2,1)S(1)}, bf16[64,3712]{1,0:T(8,128)(2,1)S(1)}, bf16[64,3712]{1,0:T(8,128)(2,1)S(1)}) custom-call(bf16[144,896]{1,0:T(8,128)(2,1)S(1)} %collective-permute-done.rest_4_.rest_5_.refs_0_, bf16[144,896]{1,0:T(8,128)(2,1)S(1)} %collective-permute-done.1.rest_6_.refs_1_, ...), custom_call_target="tpu_custom_call" | custom-call | tf_op jit(solution)/shard_map/place_shares/pallas_call | solution.py:298
  50.8 0.7 collective-permute-start.13
  51.5 1.5 %collective-permute-start.14 = (bf16[64,3712]{1,0:T(8,128)(2,1)S(1)}, bf16[64,3712]{1,0:T(8,128)(2,1)S(1)}, u32[]{:S(2)}, u32[]{:S(2)}) collective-permute-start(bf16[64,3712]{1,0:T(8,128)(2,1)S(1)} %get-tuple-element.39), channel_id=1, source_target_pairs={{0,4},{1,5},{2,6},{3,7},{4,0},{5,1},{6,2},{7,3},{8,12},{9,13},{10,... | collective-permute-start | bytes 1425416 | tf_op jit(solution)/shard_map/ppermute | solution.py:28
  53.0 1.3 %collective-permute-start.15 = (bf16[64,3712]{1,0:T(8,128)(2,1)S(1)}, bf16[64,3712]{1,0:T(8,128)(2,1)S(1)}, u32[]{:S(2)}, u32[]{:S(2)}) collective-permute-start(bf16[64,3712]{1,0:T(8,128)(2,1)S(1)} %get-tuple-element.40), channel_id=1, source_target_pairs={{0,6},{1,7},{2,4},{3,5},{4,2},{5,3},{6,0},{7,1},{8,14},{9,15},{10,... | collective-permute-start | bytes 1425416 | tf_op jit(solution)/shard_map/ppermute | solution.py:28
  54.4 1.5 %collective-permute-done.19.refs_3_ = bf16[128,1024]{1,0:T(8,128)(2,1)S(1)} collective-permute-done((bf16[128,1024]{1,0:T(8,128)(2,1)}, bf16[128,1024]{1,0:T(8,128)(2,1)S(1)}, u32[]{:S(2)}, u32[]{:S(2)}) %collective-permute-start.19) | collective-permute-done | bytes 262176 | tf_op jit(solution)/shard_map/ppermute | solution.py:28
  55.9 0.2 maximum_select_fusion
  56.1 8.7 %collective-permute-start.20 = (bf16[256,1024]{1,0:T(8,128)(2,1)S(1)}, bf16[256,1024]{1,0:T(8,128)(2,1)S(1)}, u32[]{:S(2)}, u32[]{:S(2)}) collective-permute-start(bf16[256,1024]{1,0:T(8,128)(2,1)S(1)} %maximum_select_fusion), channel_id=1, source_target_pairs={{0,16},{8,0},{16,24},{24,8},{1,17},{9,1},{17,25},{25,9},{2,18},{10... | collective-permute-start | bytes 1572872 | tf_op jit(solution)/shard_map/ppermute | solution.py:296
  64.8 8.7 %collective-permute-done.14.refs_2_.refs_4_ = bf16[64,3712]{1,0:T(8,128)(2,1)S(1)} collective-permute-done((bf16[64,3712]{1,0:T(8,128)(2,1)S(1)}, bf16[64,3712]{1,0:T(8,128)(2,1)S(1)}, u32[]{:S(2)}, u32[]{:S(2)}) %collective-permute-start.14) | collective-permute-done | bytes 475168 | tf_op jit(solution)/shard_map/ppermute | solution.py:28
  73.4 1.5 %collective-permute-done.15.refs_3_.refs_5_ = bf16[64,3712]{1,0:T(8,128)(2,1)S(1)} collective-permute-done((bf16[64,3712]{1,0:T(8,128)(2,1)S(1)}, bf16[64,3712]{1,0:T(8,128)(2,1)S(1)}, u32[]{:S(2)}, u32[]{:S(2)}) %collective-permute-start.15) | collective-permute-done | bytes 475168 | tf_op jit(solution)/shard_map/ppermute | solution.py:28
  75.0 0.1 collective-permute-start.16
  75.1 0.6 turn.1.left_ref
  75.7 0.0 copy-start.9
  75.7 1.6 %sum.1.before_ref = f32[896,1024]{1,0:T(8,128)S(1)} custom-call(bf16[896,1024]{1,0:T(8,128)(2,1)S(1)} %turn.1.left_ref, bf16[256,1024]{1,0:T(8,128)(2,1)S(1)} %get-tuple-element.43.refs_0_, bf16[256,1024]{1,0:T(8,128)(2,1)S(1)} %collective-permute-done.17.refs_1_, bf16[128,1024]{1,0:T(8,128)(2,1)S(1)} %collective-permute-done.18.refs_2_, ...), custom_call_target="tpu_custom_call" | custom-call | tf_op jit(solution)/shard_map/sum/pallas_call | solution.py:334
  77.3 1.2 %unplace.1 = bf16[128,1024]{1,0:T(8,128)(2,1)} custom-call(s32[1,128]{1,0:T(1,128)S(1)} %bitcast.4, bf16[128,1024]{1,0:T(8,128)(2,1)S(1)} %collective-permute-done.16.theirs_ref, bf16[64,3712]{1,0:T(8,128)(2,1)S(1)} %get-tuple-element.37.refs_0_.refs_2_, bf16[64,3712]{1,0:T(8,128)(2,1)S(1)} %collective-permute-done.13.refs_1_.refs_3_, ...), custom_call_target="tpu_custom_call" | custom-call | tf_op jit(solution)/shard_map/unplace/pallas_call | solution.py:315
  78.5 2.3 %grad.1 = f32[896,1024]{1,0:T(8,128)} custom-call(bf16[896,1024]{1,0:T(8,128)(2,1)S(1)} %turn.1.left_ref, f32[896,1024]{1,0:T(8,128)S(1)} %sum.1.before_ref, bf16[256,1024]{1,0:T(8,128)(2,1)S(1)} %collective-permute-done.20.refs_0_), custom_call_target="tpu_custom_call" | custom-call | tf_op jit(solution)/shard_map/grad/pallas_call | solution.py:344
  (32 shorter events, 0.1 us)
Async XLA Ops:
  0.6 1.2 %copy-start.2 = (bf16[128,3584]{1,0:T(8,128)(2,1)S(1)}, bf16[128,3584]{1,0:T(8,128)(2,1)}, u32[]{:S(2)}) copy-start(bf16[128,3584]{1,0:T(8,128)(2,1)} %refs_3_.1) | copy-start | bytes 2752516
  1.8 0.9 %copy-start.3 = (bf16[128,1024]{1,0:T(8,128)(2,1)S(1)}, bf16[128,1024]{1,0:T(8,128)(2,1)}, u32[]{:S(2)}) copy-start(bf16[128,1024]{1,0:T(8,128)(2,1)} %refs_2_.1) | copy-start | bytes 786436
  2.8 0.7 copy-start.8
  3.4 0.7 copy-start.10
  5.3 11.0 %collective-permute-start.6 = (bf16[32,4736]{1,0:T(8,128)(2,1)S(1)}, bf16[32,4736]{1,0:T(8,128)(2,1)S(1)}, u32[]{:S(2)}, u32[]{:S(2)}) collective-permute-start(bf16[32,4736]{1,0:T(8,128)(2,1)S(1)} %get-tuple-element.27), channel_id=1, source_target_pairs={{0,2},{1,3},{2,0},{3,1},{4,6},{5,7},{6,4},{7,5},{8,10},{9,11},{10,... | collective-permute-start | bytes 909320 | tf_op jit(solution)/shard_map/ppermute | solution.py:28
  8.3 15.3 %collective-permute-start.7 = (bf16[32,4736]{1,0:T(8,128)(2,1)S(1)}, bf16[32,4736]{1,0:T(8,128)(2,1)S(1)}, u32[]{:S(2)}, u32[]{:S(2)}) collective-permute-start(bf16[32,4736]{1,0:T(8,128)(2,1)S(1)} %get-tuple-element.28), channel_id=1, source_target_pairs={{0,4},{1,5},{2,6},{3,7},{4,0},{5,1},{6,2},{7,3},{8,12},{9,13},{10,... | collective-permute-start | bytes 909320 | tf_op jit(solution)/shard_map/ppermute | solution.py:28
  9.8 13.8 %collective-permute-start.8 = (bf16[32,4736]{1,0:T(8,128)(2,1)S(1)}, bf16[32,4736]{1,0:T(8,128)(2,1)S(1)}, u32[]{:S(2)}, u32[]{:S(2)}) collective-permute-start(bf16[32,4736]{1,0:T(8,128)(2,1)S(1)} %get-tuple-element.29), channel_id=1, source_target_pairs={{0,6},{1,7},{2,4},{3,5},{4,2},{5,3},{6,0},{7,1},{8,14},{9,15},{10,... | collective-permute-start | bytes 909320 | tf_op jit(solution)/shard_map/ppermute | solution.py:28
  9.8 16.4 %collective-permute-start = (bf16[144,896]{1,0:T(8,128)(2,1)S(1)}, bf16[144,896]{1,0:T(8,128)(2,1)S(1)}, u32[]{:S(2)}, u32[]{:S(2)}) collective-permute-start(bf16[144,896]{1,0:T(8,128)(2,1)S(1)} %get-tuple-element.23), channel_id=1, source_target_pairs={{0,8},{8,0},{16,24},{24,16},{1,9},{9,1},{17,25},{25,17},{2,10},{10... | collective-permute-start | bytes 774152 | tf_op jit(solution)/shard_map/ppermute | solution.py:28
  11.8 20.6 %collective-permute-start.1 = (bf16[144,896]{1,0:T(8,128)(2,1)S(1)}, bf16[144,896]{1,0:T(8,128)(2,1)S(1)}, u32[]{:S(2)}, u32[]{:S(2)}) collective-permute-start(bf16[144,896]{1,0:T(8,128)(2,1)S(1)} %get-tuple-element.24), channel_id=1, source_target_pairs={{0,16},{8,24},{16,0},{24,8},{1,17},{9,25},{17,1},{25,9},{2,18},{10... | collective-permute-start | bytes 774152 | tf_op jit(solution)/shard_map/ppermute | solution.py:28
  16.3 16.1 %collective-permute-start.2 = (bf16[144,896]{1,0:T(8,128)(2,1)S(1)}, bf16[144,896]{1,0:T(8,128)(2,1)S(1)}, u32[]{:S(2)}, u32[]{:S(2)}) collective-permute-start(bf16[144,896]{1,0:T(8,128)(2,1)S(1)} %get-tuple-element.25), channel_id=1, source_target_pairs={{0,24},{8,16},{16,8},{24,0},{1,25},{9,17},{17,9},{25,1},{2,26},{10... | collective-permute-start | bytes 774152 | tf_op jit(solution)/shard_map/ppermute | solution.py:28
  20.4 3.1 %copy-start = (bf16[1,3584,1024]{2,1,0:T(8,128)(2,1)S(1)}, bf16[1,3584,1024]{2,1,0:T(8,128)(2,1)}, u32[]{:S(2)}) copy-start(bf16[1,3584,1024]{2,1,0:T(8,128)(2,1)} %weight_ref.5) | copy-start | bytes 22020100
  23.5 10.5 %copy-start.1 = (bf16[1,3584,1024]{2,1,0:T(8,128)(2,1)S(1)}, bf16[1,3584,1024]{2,1,0:T(8,128)(2,1)}, u32[]{:S(2)}) copy-start(bf16[1,3584,1024]{2,1,0:T(8,128)(2,1)} %weight_ref.5) | copy-start | bytes 22020100
  23.5 14.9 %collective-permute-start.9 = (bf16[32,4736]{1,0:T(8,128)(2,1)S(1)}, bf16[32,4736]{1,0:T(8,128)(2,1)S(1)}, u32[]{:S(2)}, u32[]{:S(2)}) collective-permute-start(bf16[32,4736]{1,0:T(8,128)(2,1)S(1)} %hold.4), channel_id=1, source_target_pairs={{0,1},{1,0},{2,3},{3,2},{4,5},{5,4},{6,7},{7,6},{8,9},{9,8},{10,11... | collective-permute-start | bytes 909320 | tf_op jit(solution)/shard_map/ppermute | solution.py:28
  23.6 14.8 %collective-permute-start.12 = (bf16[32,4736]{1,0:T(8,128)(2,1)S(1)}, bf16[32,4736]{1,0:T(8,128)(2,1)S(1)}, u32[]{:S(2)}, u32[]{:S(2)}) collective-permute-start(bf16[32,4736]{1,0:T(8,128)(2,1)S(1)} %hold.7), channel_id=1, source_target_pairs={{0,7},{1,6},{2,5},{3,4},{4,3},{5,2},{6,1},{7,0},{8,15},{9,14},{10,... | collective-permute-start | bytes 909320 | tf_op jit(solution)/shard_map/ppermute | solution.py:28
  26.2 14.4 %collective-permute-start.11 = (bf16[32,4736]{1,0:T(8,128)(2,1)S(1)}, bf16[32,4736]{1,0:T(8,128)(2,1)S(1)}, u32[]{:S(2)}, u32[]{:S(2)}) collective-permute-start(bf16[32,4736]{1,0:T(8,128)(2,1)S(1)} %hold.6), channel_id=1, source_target_pairs={{0,5},{1,4},{2,7},{3,6},{4,1},{5,0},{6,3},{7,2},{8,13},{9,12},{10,... | collective-permute-start | bytes 909320 | tf_op jit(solution)/shard_map/ppermute | solution.py:28
  32.4 9.4 %collective-permute-start.10 = (bf16[32,4736]{1,0:T(8,128)(2,1)S(1)}, bf16[32,4736]{1,0:T(8,128)(2,1)S(1)}, u32[]{:S(2)}, u32[]{:S(2)}) collective-permute-start(bf16[32,4736]{1,0:T(8,128)(2,1)S(1)} %hold.5), channel_id=1, source_target_pairs={{0,3},{1,2},{2,1},{3,0},{4,7},{5,6},{6,5},{7,4},{8,11},{9,10},{10,... | collective-permute-start | bytes 909320 | tf_op jit(solution)/shard_map/ppermute | solution.py:28
  32.4 3.0 %collective-permute-start.3 = (bf16[144,896]{1,0:T(8,128)(2,1)S(1)}, bf16[144,896]{1,0:T(8,128)(2,1)S(1)}, u32[]{:S(2)}, u32[]{:S(2)}) collective-permute-start(bf16[144,896]{1,0:T(8,128)(2,1)S(1)} %collective-permute-done.rest_4_.rest_5_.refs_0_), channel_id=1, source_target_pairs={{0,1},{1,0},{2,3},{3,2},{4,5},{5,4},{6,7},{7,6},{8,9},{9,8},{10,11... | collective-permute-start | bytes 774152 | tf_op jit(solution)/shard_map/ppermute | solution.py:28
  35.4 7.8 %copy-start.4 = (bf16[128,896]{1,0:T(8,128)(2,1)}, bf16[128,896]{1,0:T(8,128)(2,1)S(1)}, u32[]{:S(2)}) copy-start(bf16[128,896]{1,0:T(8,128)(2,1)S(1)} %get-tuple-element.41.refs_0_) | copy-start | bytes 688132
  35.4 17.6 %collective-permute-start.18 = (bf16[128,1024]{1,0:T(8,128)(2,1)S(1)}, bf16[128,1024]{1,0:T(8,128)(2,1)S(1)}, u32[]{:S(2)}, u32[]{:S(2)}) collective-permute-start(bf16[128,1024]{1,0:T(8,128)(2,1)S(1)} %get-tuple-element.35.rest_4_), channel_id=1, source_target_pairs={{0,24},{8,16},{16,8},{24,0},{1,25},{9,17},{17,9},{25,1},{2,26},{10... | collective-permute-start | bytes 786440 | tf_op jit(solution)/shard_map/ppermute | solution.py:28
  43.2 0.7 copy-start.6
  44.6 11.2 %collective-permute-start.19 = (bf16[128,1024]{1,0:T(8,128)(2,1)}, bf16[128,1024]{1,0:T(8,128)(2,1)S(1)}, u32[]{:S(2)}, u32[]{:S(2)}) collective-permute-start(bf16[128,1024]{1,0:T(8,128)(2,1)} %slice.3), channel_id=1, source_target_pairs={{0,24},{8,16},{16,8},{24,0},{1,25},{9,17},{17,9},{25,1},{2,26},{10... | collective-permute-start | bytes 786440 | tf_op jit(solution)/shard_map/ppermute | solution.py:28
  47.6 1.5 %collective-permute-start.4 = (bf16[144,896]{1,0:T(8,128)(2,1)S(1)}, bf16[144,896]{1,0:T(8,128)(2,1)S(1)}, u32[]{:S(2)}, u32[]{:S(2)}) collective-permute-start(bf16[144,896]{1,0:T(8,128)(2,1)S(1)} %collective-permute-done.1.rest_6_.refs_1_), channel_id=1, source_target_pairs={{0,1},{1,0},{2,3},{3,2},{4,5},{5,4},{6,7},{7,6},{8,9},{9,8},{10,11... | collective-permute-start | bytes 774152 | tf_op jit(solution)/shard_map/ppermute | solution.py:28
  47.6 1.9 %collective-permute-start.5 = (bf16[144,896]{1,0:T(8,128)(2,1)S(1)}, bf16[144,896]{1,0:T(8,128)(2,1)S(1)}, u32[]{:S(2)}, u32[]{:S(2)}) collective-permute-start(bf16[144,896]{1,0:T(8,128)(2,1)S(1)} %collective-permute-done.2.rest_7_.refs_2_), channel_id=1, source_target_pairs={{0,1},{1,0},{2,3},{3,2},{4,5},{5,4},{6,7},{7,6},{8,9},{9,8},{10,11... | collective-permute-start | bytes 774152 | tf_op jit(solution)/shard_map/ppermute | solution.py:28
  48.1 26.9 %copy-start.5 = (bf16[128,896]{1,0:T(8,128)(2,1)S(1)}, bf16[128,896]{1,0:T(8,128)(2,1)}, u32[]{:S(2)}) copy-start(bf16[128,896]{1,0:T(8,128)(2,1)} %copy-done.4) | copy-start | bytes 688132
  48.1 26.9 %copy-start.7 = (bf16[128,896]{1,0:T(8,128)(2,1)S(1)}, bf16[128,896]{1,0:T(8,128)(2,1)}, u32[]{:S(2)}) copy-start(bf16[128,896]{1,0:T(8,128)(2,1)} %copy-done.6) | copy-start | bytes 688132
  48.1 27.6 %collective-permute-start.17 = (bf16[256,1024]{1,0:T(8,128)(2,1)S(1)}, bf16[256,1024]{1,0:T(8,128)(2,1)S(1)}, u32[]{:S(2)}, u32[]{:S(2)}) collective-permute-start(bf16[256,1024]{1,0:T(8,128)(2,1)S(1)} %get-tuple-element.43.refs_0_), channel_id=1, source_target_pairs={{0,8},{8,0},{16,24},{24,16},{1,9},{9,1},{17,25},{25,17},{2,10},{10... | collective-permute-start | bytes 1572872 | tf_op jit(solution)/shard_map/ppermute | solution.py:28
  50.8 13.9 %collective-permute-start.13 = (bf16[64,3712]{1,0:T(8,128)(2,1)S(1)}, bf16[64,3712]{1,0:T(8,128)(2,1)S(1)}, u32[]{:S(2)}, u32[]{:S(2)}) collective-permute-start(bf16[64,3712]{1,0:T(8,128)(2,1)S(1)} %get-tuple-element.38), channel_id=1, source_target_pairs={{0,2},{1,3},{2,0},{3,1},{4,6},{5,7},{6,4},{7,5},{8,10},{9,11},{10,... | collective-permute-start | bytes 1425416 | tf_op jit(solution)/shard_map/ppermute | solution.py:28
  51.5 21.9 %collective-permute-start.14 = (bf16[64,3712]{1,0:T(8,128)(2,1)S(1)}, bf16[64,3712]{1,0:T(8,128)(2,1)S(1)}, u32[]{:S(2)}, u32[]{:S(2)}) collective-permute-start(bf16[64,3712]{1,0:T(8,128)(2,1)S(1)} %get-tuple-element.39), channel_id=1, source_target_pairs={{0,4},{1,5},{2,6},{3,7},{4,0},{5,1},{6,2},{7,3},{8,12},{9,13},{10,... | collective-permute-start | bytes 1425416 | tf_op jit(solution)/shard_map/ppermute | solution.py:28
  53.0 21.9 %collective-permute-start.15 = (bf16[64,3712]{1,0:T(8,128)(2,1)S(1)}, bf16[64,3712]{1,0:T(8,128)(2,1)S(1)}, u32[]{:S(2)}, u32[]{:S(2)}) collective-permute-start(bf16[64,3712]{1,0:T(8,128)(2,1)S(1)} %get-tuple-element.40), channel_id=1, source_target_pairs={{0,6},{1,7},{2,4},{3,5},{4,2},{5,3},{6,0},{7,1},{8,14},{9,15},{10,... | collective-permute-start | bytes 1425416 | tf_op jit(solution)/shard_map/ppermute | solution.py:28
  56.1 22.4 %collective-permute-start.20 = (bf16[256,1024]{1,0:T(8,128)(2,1)S(1)}, bf16[256,1024]{1,0:T(8,128)(2,1)S(1)}, u32[]{:S(2)}, u32[]{:S(2)}) collective-permute-start(bf16[256,1024]{1,0:T(8,128)(2,1)S(1)} %maximum_select_fusion), channel_id=1, source_target_pairs={{0,16},{8,0},{16,24},{24,8},{1,17},{9,1},{17,25},{25,9},{2,18},{10... | collective-permute-start | bytes 1572872 | tf_op jit(solution)/shard_map/ppermute | solution.py:296
  75.0 2.3 %collective-permute-start.16 = (bf16[128,1024]{1,0:T(8,128)(2,1)S(1)}, bf16[128,1024]{1,0:T(8,128)(2,1)S(1)}, u32[]{:S(2)}, u32[]{:S(2)}) collective-permute-start(bf16[128,1024]{1,0:T(8,128)(2,1)S(1)} %split.1), channel_id=1, source_target_pairs={{0,1},{1,0},{2,3},{3,2},{4,5},{5,4},{6,7},{7,6},{8,9},{9,8},{10,11... | collective-permute-start | bytes 786440 | tf_op jit(solution)/shard_map/ppermute | solution.py:28
  75.7 1.6 %copy-start.9 = (s32[128,1]{0,1:T(1,128)S(1)}, s32[128,1]{0,1:T(1,128)}, u32[]{:S(2)}) copy-start(s32[128,1]{0,1:T(1,128)} %param.6) | copy-start | bytes 1540

commit v6 on v5

--- a/solution.py
+++ b/solution.py
@@ -285,7 +285,7 @@
     act, dpre, own = forward(got[1::2], [half], *cuts, crossed[0])
     acts, owns, dpres = acts + [act], owns + [own], [dpre]
     gathered = [[] for _ in range(groups)]
-    for k in range(1, members):
+    for k in reversed(range(1, members)):
         if chain and k == 3:
             gathered[2] = [*early, swap(dpre[rows // 2 :], "dp", 3)]
         elif not (chain and k == 2):

time: 81 us -> 81 us (level)
  no operation moved by 1% of the time
where the time goes in v6:
time: 81 us; the launch traced here: 80.7 us
  starting transfers between devices  36.6 us (45%)
  waiting for transfers between devices  24.3 us (30%)
  Pallas kernels  10.8 us (13%)
  local copies, waits for them, and re-layouts  7.92 us (10%)
  between operations  0.84 us (1%)
    ppermute x20, starting transfers between devices, swap(): return lax.ppermute(value, axis, [(i, i ^ offset) for i in range(count)])  27.9 us
    ppermute x20, waiting for transfers between devices, swap(): return lax.ppermute(value, axis, [(i, i ^ offset) for i in range(count)])  24.3 us
    ppermute x1, starting transfers between devices, on_device(): lax.ppermute(value, 'dp', [(0, 2), (1, 0), (2, 3), (3, 1)])  8.7 us
    unnamed x22, local copies, waits for them, and re-layouts  7.2 us
    pallas_call x2, Pallas kernels, forward(): pl.pallas_call(functools.partial(forward_kernel, (len(blocks), width, inn...  2.67 us
    pallas_call x1, Pallas kernels, on_device(): pl.pallas_call(functools.partial(grad_kernel, 2), out_shape=jax.ShapeDtyp...  2.26 us
  transfers between devices with their start and end apart: 21, of which 9 were waited for; matrix products, arithmetic and copies ran while one was open for 1% of the time, Pallas kernels for 9%

profile of v6, /device:TPU:0, one launch (start us, length us, event | category | flops | bytes accessed | tf_op | source)
XLA Modules:
  0.0 80.7 jit_solution(12543744118284679463)
XLA Ops:
  0.6 1.2 %copy-done.2 = bf16[128,3584]{1,0:T(8,128)(2,1)S(1)} copy-done((bf16[128,3584]{1,0:T(8,128)(2,1)S(1)}, bf16[128,3584]{1,0:T(8,128)(2,1)}, u32[]{:S(2)}) %copy-start.2) | copy-done | bytes 917528
  1.8 0.9 %copy-done.3 = bf16[128,1024]{1,0:T(8,128)(2,1)S(1)} copy-done((bf16[128,1024]{1,0:T(8,128)(2,1)S(1)}, bf16[128,1024]{1,0:T(8,128)(2,1)}, u32[]{:S(2)}) %copy-start.3) | copy-done | bytes 262168
  2.8 0.7 copy-done.8
  3.4 0.7 copy-done.10
  4.1 1.2 %place.1 = (bf16[32,4736]{1,0:T(8,128)(2,1)S(1)}, bf16[32,4736]{1,0:T(8,128)(2,1)S(1)}, bf16[32,4736]{1,0:T(8,128)(2,1)S(1)}, bf16[32,4736]{1,0:T(8,128)(2,1)S(1...) custom-call(s32[1,128]{1,0:T(1,128)S(1)} %bitcast.3, ...), custom_call_target="tpu_custom_call" | custom-call | tf_op jit(solution)/shard_map/place/pallas_call | solution.py:241
  5.3 3.0 %collective-permute-start.6 = (bf16[32,4736]{1,0:T(8,128)(2,1)S(1)}, bf16[32,4736]{1,0:T(8,128)(2,1)S(1)}, u32[]{:S(2)}, u32[]{:S(2)}) collective-permute-start(bf16[32,4736]{1,0:T(8,128)(2,1)S(1)} %get-tuple-element.27), channel_id=1, source_target_pairs={{0,2},{1,3},{2,0},{3,1},{4,6},{5,7},{6,4},{7,5},{8,10},{9,11},{10,... | collective-permute-start | bytes 909320 | tf_op jit(solution)/shard_map/ppermute | solution.py:28
  8.3 1.5 %collective-permute-start.7 = (bf16[32,4736]{1,0:T(8,128)(2,1)S(1)}, bf16[32,4736]{1,0:T(8,128)(2,1)S(1)}, u32[]{:S(2)}, u32[]{:S(2)}) collective-permute-start(bf16[32,4736]{1,0:T(8,128)(2,1)S(1)} %get-tuple-element.28), channel_id=1, source_target_pairs={{0,4},{1,5},{2,6},{3,7},{4,0},{5,1},{6,2},{7,3},{8,12},{9,13},{10,... | collective-permute-start | bytes 909320 | tf_op jit(solution)/shard_map/ppermute | solution.py:28
  9.8 0.0 collective-permute-start.8
  9.8 2.0 %collective-permute-start = (bf16[144,896]{1,0:T(8,128)(2,1)S(1)}, bf16[144,896]{1,0:T(8,128)(2,1)S(1)}, u32[]{:S(2)}, u32[]{:S(2)}) collective-permute-start(bf16[144,896]{1,0:T(8,128)(2,1)S(1)} %get-tuple-element.23), channel_id=1, source_target_pairs={{0,8},{8,0},{16,24},{24,16},{1,9},{9,1},{17,25},{25,17},{2,10},{10... | collective-permute-start | bytes 774152 | tf_op jit(solution)/shard_map/ppermute | solution.py:28
  11.8 2.6 %collective-permute-start.1 = (bf16[144,896]{1,0:T(8,128)(2,1)S(1)}, bf16[144,896]{1,0:T(8,128)(2,1)S(1)}, u32[]{:S(2)}, u32[]{:S(2)}) collective-permute-start(bf16[144,896]{1,0:T(8,128)(2,1)S(1)} %get-tuple-element.24), channel_id=1, source_target_pairs={{0,16},{8,24},{16,0},{24,8},{1,17},{9,25},{17,1},{25,9},{2,18},{10... | collective-permute-start | bytes 774152 | tf_op jit(solution)/shard_map/ppermute | solution.py:28
  14.4 1.8 %collective-permute-done.6.rest_1_.refs_1_ = bf16[32,4736]{1,0:T(8,128)(2,1)S(1)} collective-permute-done((bf16[32,4736]{1,0:T(8,128)(2,1)S(1)}, bf16[32,4736]{1,0:T(8,128)(2,1)S(1)}, u32[]{:S(2)}, u32[]{:S(2)}) %collective-permute-start.6) | collective-permute-done | bytes 303136 | tf_op jit(solution)/shard_map/ppermute | solution.py:28
  16.3 4.2 %collective-permute-start.2 = (bf16[144,896]{1,0:T(8,128)(2,1)S(1)}, bf16[144,896]{1,0:T(8,128)(2,1)S(1)}, u32[]{:S(2)}, u32[]{:S(2)}) collective-permute-start(bf16[144,896]{1,0:T(8,128)(2,1)S(1)} %get-tuple-element.25), channel_id=1, source_target_pairs={{0,24},{8,16},{16,8},{24,0},{1,25},{9,17},{17,9},{25,1},{2,26},{10... | collective-permute-start | bytes 774152 | tf_op jit(solution)/shard_map/ppermute | solution.py:28
  20.4 3.1 %copy-done = bf16[1,3584,1024]{2,1,0:T(8,128)(2,1)S(1)} copy-done((bf16[1,3584,1024]{2,1,0:T(8,128)(2,1)S(1)}, bf16[1,3584,1024]{2,1,0:T(8,128)(2,1)}, u32[]{:S(2)}) %copy-start) | copy-done | bytes 7340056
  23.5 0.0 collective-permute-done.7.rest_2_.refs_1_
  23.5 0.1 collective-permute-start.9
  23.6 0.0 collective-permute-done.8.rest_3_.refs_1_
  23.6 2.6 %collective-permute-start.12 = (bf16[32,4736]{1,0:T(8,128)(2,1)S(1)}, bf16[32,4736]{1,0:T(8,128)(2,1)S(1)}, u32[]{:S(2)}, u32[]{:S(2)}) collective-permute-start(bf16[32,4736]{1,0:T(8,128)(2,1)S(1)} %hold.7), channel_id=1, source_target_pairs={{0,7},{1,6},{2,5},{3,4},{4,3},{5,2},{6,1},{7,0},{8,15},{9,14},{10,... | collective-permute-start | bytes 909320 | tf_op jit(solution)/shard_map/ppermute | solution.py:28
  26.2 0.2 collective-permute-start.11
  26.4 6.0 %collective-permute-done.1.rest_6_.refs_1_ = bf16[144,896]{1,0:T(8,128)(2,1)S(1)} collective-permute-done((bf16[144,896]{1,0:T(8,128)(2,1)S(1)}, bf16[144,896]{1,0:T(8,128)(2,1)S(1)}, u32[]{:S(2)}, u32[]{:S(2)}) %collective-permute-start.1) | collective-permute-done | bytes 258080 | tf_op jit(solution)/shard_map/ppermute | solution.py:28
  32.4 0.0 collective-permute-start.10
  32.4 1.6 %collective-permute-start.3 = (bf16[144,896]{1,0:T(8,128)(2,1)S(1)}, bf16[144,896]{1,0:T(8,128)(2,1)S(1)}, u32[]{:S(2)}, u32[]{:S(2)}) collective-permute-start(bf16[144,896]{1,0:T(8,128)(2,1)S(1)} %collective-permute-done.rest_4_.rest_5_.refs_0_), channel_id=1, source_target_pairs={{0,1},{1,0},{2,3},{3,2},{4,5},{5,4},{6,7},{7,6},{8,9},{9,8},{10,11... | collective-permute-start | bytes 774152 | tf_op jit(solution)/shard_map/ppermute | solution.py:28
  34.0 1.3 %forward.2 = (bf16[128,1024]{1,0:T(8,128)(2,1)S(1)}, bf16[128,1024]{1,0:T(8,128)(2,1)S(1)}, bf16[128,896]{1,0:T(8,128)(2,1)S(1)}) custom-call(bf16[1,3584,1024]{2,1,0:T(8,128)(2,1)S(1)} %copy-done.1, bf16[32,4736]{1,0:T(8,128)(2,1)S(1)} %get-tuple-element.26.rest_0_.tie, bf16[32,4736]{1,0:T(8,128)(2,1)S(1)} %collective-permute-done.6.rest_1_.refs_1_, ...), custom_call_target="tpu_custom_call" | custom-call | tf_op jit(solution)/shard_map/forward/pallas_call | solution.py:271
  35.4 0.0 copy-start.4
  35.4 3.1 %collective-permute-start.18 = (bf16[128,1024]{1,0:T(8,128)(2,1)S(1)}, bf16[128,1024]{1,0:T(8,128)(2,1)S(1)}, u32[]{:S(2)}, u32[]{:S(2)}) collective-permute-start(bf16[128,1024]{1,0:T(8,128)(2,1)S(1)} %get-tuple-element.35.rest_4_), channel_id=1, source_target_pairs={{0,24},{8,16},{16,8},{24,0},{1,25},{9,17},{17,9},{25,1},{2,26},{10... | collective-permute-start | bytes 786440 | tf_op jit(solution)/shard_map/ppermute | solution.py:28
  38.5 2.1 %collective-permute-done.11.rest_2_ = bf16[32,4736]{1,0:T(8,128)(2,1)S(1)} collective-permute-done((bf16[32,4736]{1,0:T(8,128)(2,1)S(1)}, bf16[32,4736]{1,0:T(8,128)(2,1)S(1)}, u32[]{:S(2)}, u32[]{:S(2)}) %collective-permute-start.11) | collective-permute-done | bytes 303136 | tf_op jit(solution)/shard_map/ppermute | solution.py:28
  40.6 1.3 %collective-permute-done.10.rest_1_ = bf16[32,4736]{1,0:T(8,128)(2,1)S(1)} collective-permute-done((bf16[32,4736]{1,0:T(8,128)(2,1)S(1)}, bf16[32,4736]{1,0:T(8,128)(2,1)S(1)}, u32[]{:S(2)}, u32[]{:S(2)}) %collective-permute-start.10) | collective-permute-done | bytes 303136 | tf_op jit(solution)/shard_map/ppermute | solution.py:28
  41.9 1.3 %forward.3 = (bf16[128,1024]{1,0:T(8,128)(2,1)S(1)}, bf16[256,1024]{1,0:T(8,128)(2,1)S(1)}, bf16[128,896]{1,0:T(8,128)(2,1)S(1)}) custom-call(bf16[1,3584,1024]{2,1,0:T(8,128)(2,1)S(1)} %copy-done.1, bf16[32,4736]{1,0:T(8,128)(2,1)S(1)} %collective-permute-done.9.rest_0_, bf16[32,4736]{1,0:T(8,128)(2,1)S(1)} %collective-permute-done.10.rest_1_, ...), custom_call_target="tpu_custom_call" | custom-call | tf_op jit(solution)/shard_map/forward/pallas_call | solution.py:271
  43.2 0.7 copy-done.6
  43.9 0.7 slice.3
  44.6 3.0 %collective-permute-start.19 = (bf16[128,1024]{1,0:T(8,128)(2,1)}, bf16[128,1024]{1,0:T(8,128)(2,1)S(1)}, u32[]{:S(2)}, u32[]{:S(2)}) collective-permute-start(bf16[128,1024]{1,0:T(8,128)(2,1)} %slice.3), channel_id=1, source_target_pairs={{0,24},{8,16},{16,8},{24,0},{1,25},{9,17},{17,9},{25,1},{2,26},{10... | collective-permute-start | bytes 786440 | tf_op jit(solution)/shard_map/ppermute | solution.py:28
  47.6 0.5 collective-permute-start.5
  48.1 1.0 %collective-permute-done.4.refs_4_ = bf16[144,896]{1,0:T(8,128)(2,1)S(1)} collective-permute-done((bf16[144,896]{1,0:T(8,128)(2,1)S(1)}, bf16[144,896]{1,0:T(8,128)(2,1)S(1)}, u32[]{:S(2)}, u32[]{:S(2)}) %collective-permute-start.4) | collective-permute-done | bytes 258080 | tf_op jit(solution)/shard_map/ppermute | solution.py:28
  49.1 0.4 collective-permute-done.5.refs_5_
  49.5 1.3 %place_shares.1 = (bf16[64,3712]{1,0:T(8,128)(2,1)S(1)}, bf16[64,3712]{1,0:T(8,128)(2,1)S(1)}, bf16[64,3712]{1,0:T(8,128)(2,1)S(1)}, bf16[64,3712]{1,0:T(8,128)(2,1)S(1)}) custom-call(bf16[144,896]{1,0:T(8,128)(2,1)S(1)} %collective-permute-done.rest_4_.rest_5_.refs_0_, bf16[144,896]{1,0:T(8,128)(2,1)S(1)} %collective-permute-done.1.rest_6_.refs_1_, ...), custom_call_target="tpu_custom_call" | custom-call | tf_op jit(solution)/shard_map/place_shares/pallas_call | solution.py:298
  50.8 0.7 collective-permute-start.13
  51.5 1.5 %collective-permute-start.14 = (bf16[64,3712]{1,0:T(8,128)(2,1)S(1)}, bf16[64,3712]{1,0:T(8,128)(2,1)S(1)}, u32[]{:S(2)}, u32[]{:S(2)}) collective-permute-start(bf16[64,3712]{1,0:T(8,128)(2,1)S(1)} %get-tuple-element.39), channel_id=1, source_target_pairs={{0,4},{1,5},{2,6},{3,7},{4,0},{5,1},{6,2},{7,3},{8,12},{9,13},{10,... | collective-permute-start | bytes 1425416 | tf_op jit(solution)/shard_map/ppermute | solution.py:28
  53.0 1.3 %collective-permute-start.15 = (bf16[64,3712]{1,0:T(8,128)(2,1)S(1)}, bf16[64,3712]{1,0:T(8,128)(2,1)S(1)}, u32[]{:S(2)}, u32[]{:S(2)}) collective-permute-start(bf16[64,3712]{1,0:T(8,128)(2,1)S(1)} %get-tuple-element.40), channel_id=1, source_target_pairs={{0,6},{1,7},{2,4},{3,5},{4,2},{5,3},{6,0},{7,1},{8,14},{9,15},{10,... | collective-permute-start | bytes 1425416 | tf_op jit(solution)/shard_map/ppermute | solution.py:28
  54.4 1.5 %collective-permute-done.19.refs_3_ = bf16[128,1024]{1,0:T(8,128)(2,1)S(1)} collective-permute-done((bf16[128,1024]{1,0:T(8,128)(2,1)}, bf16[128,1024]{1,0:T(8,128)(2,1)S(1)}, u32[]{:S(2)}, u32[]{:S(2)}) %collective-permute-start.19) | collective-permute-done | bytes 262176 | tf_op jit(solution)/shard_map/ppermute | solution.py:28
  55.9 0.2 maximum_select_fusion
  56.1 8.7 %collective-permute-start.20 = (bf16[256,1024]{1,0:T(8,128)(2,1)S(1)}, bf16[256,1024]{1,0:T(8,128)(2,1)S(1)}, u32[]{:S(2)}, u32[]{:S(2)}) collective-permute-start(bf16[256,1024]{1,0:T(8,128)(2,1)S(1)} %maximum_select_fusion), channel_id=1, source_target_pairs={{0,16},{8,0},{16,24},{24,8},{1,17},{9,1},{17,25},{25,9},{2,18},{10... | collective-permute-start | bytes 1572872 | tf_op jit(solution)/shard_map/ppermute | solution.py:296
  64.8 8.7 %collective-permute-done.14.refs_2_.refs_4_ = bf16[64,3712]{1,0:T(8,128)(2,1)S(1)} collective-permute-done((bf16[64,3712]{1,0:T(8,128)(2,1)S(1)}, bf16[64,3712]{1,0:T(8,128)(2,1)S(1)}, u32[]{:S(2)}, u32[]{:S(2)}) %collective-permute-start.14) | collective-permute-done | bytes 475168 | tf_op jit(solution)/shard_map/ppermute | solution.py:28
  73.4 1.5 %collective-permute-done.15.refs_3_.refs_5_ = bf16[64,3712]{1,0:T(8,128)(2,1)S(1)} collective-permute-done((bf16[64,3712]{1,0:T(8,128)(2,1)S(1)}, bf16[64,3712]{1,0:T(8,128)(2,1)S(1)}, u32[]{:S(2)}, u32[]{:S(2)}) %collective-permute-start.15) | collective-permute-done | bytes 475168 | tf_op jit(solution)/shard_map/ppermute | solution.py:28
  75.0 0.1 collective-permute-start.16
  75.1 0.6 turn.1.left_ref
  75.7 0.0 copy-start.9
  75.7 1.6 %sum.1.before_ref = f32[896,1024]{1,0:T(8,128)S(1)} custom-call(bf16[896,1024]{1,0:T(8,128)(2,1)S(1)} %turn.1.left_ref, bf16[256,1024]{1,0:T(8,128)(2,1)S(1)} %get-tuple-element.43.refs_0_, bf16[256,1024]{1,0:T(8,128)(2,1)S(1)} %collective-permute-done.17.refs_1_, bf16[128,1024]{1,0:T(8,128)(2,1)S(1)} %collective-permute-done.18.refs_2_, ...), custom_call_target="tpu_custom_call" | custom-call | tf_op jit(solution)/shard_map/sum/pallas_call | solution.py:334
  77.3 1.2 %unplace.1 = bf16[128,1024]{1,0:T(8,128)(2,1)} custom-call(s32[1,128]{1,0:T(1,128)S(1)} %bitcast.4, bf16[128,1024]{1,0:T(8,128)(2,1)S(1)} %collective-permute-done.16.theirs_ref, bf16[64,3712]{1,0:T(8,128)(2,1)S(1)} %get-tuple-element.37.refs_0_.refs_2_, bf16[64,3712]{1,0:T(8,128)(2,1)S(1)} %collective-permute-done.13.refs_1_.refs_3_, ...), custom_call_target="tpu_custom_call" | custom-call | tf_op jit(solution)/shard_map/unplace/pallas_call | solution.py:315
  78.5 2.3 %grad.1 = f32[896,1024]{1,0:T(8,128)} custom-call(bf16[896,1024]{1,0:T(8,128)(2,1)S(1)} %turn.1.left_ref, f32[896,1024]{1,0:T(8,128)S(1)} %sum.1.before_ref, bf16[256,1024]{1,0:T(8,128)(2,1)S(1)} %collective-permute-done.20.refs_0_), custom_call_target="tpu_custom_call" | custom-call | tf_op jit(solution)/shard_map/grad/pallas_call | solution.py:344
  (32 shorter events, 0.1 us)
Async XLA Ops:
  0.6 1.2 %copy-start.2 = (bf16[128,3584]{1,0:T(8,128)(2,1)S(1)}, bf16[128,3584]{1,0:T(8,128)(2,1)}, u32[]{:S(2)}) copy-start(bf16[128,3584]{1,0:T(8,128)(2,1)} %refs_3_.1) | copy-start | bytes 2752516
  1.8 0.9 %copy-start.3 = (bf16[128,1024]{1,0:T(8,128)(2,1)S(1)}, bf16[128,1024]{1,0:T(8,128)(2,1)}, u32[]{:S(2)}) copy-start(bf16[128,1024]{1,0:T(8,128)(2,1)} %refs_2_.1) | copy-start | bytes 786436
  2.8 0.7 copy-start.8
  3.4 0.7 copy-start.10
  5.3 11.0 %collective-permute-start.6 = (bf16[32,4736]{1,0:T(8,128)(2,1)S(1)}, bf16[32,4736]{1,0:T(8,128)(2,1)S(1)}, u32[]{:S(2)}, u32[]{:S(2)}) collective-permute-start(bf16[32,4736]{1,0:T(8,128)(2,1)S(1)} %get-tuple-element.27), channel_id=1, source_target_pairs={{0,2},{1,3},{2,0},{3,1},{4,6},{5,7},{6,4},{7,5},{8,10},{9,11},{10,... | collective-permute-start | bytes 909320 | tf_op jit(solution)/shard_map/ppermute | solution.py:28
  8.3 15.3 %collective-permute-start.7 = (bf16[32,4736]{1,0:T(8,128)(2,1)S(1)}, bf16[32,4736]{1,0:T(8,128)(2,1)S(1)}, u32[]{:S(2)}, u32[]{:S(2)}) collective-permute-start(bf16[32,4736]{1,0:T(8,128)(2,1)S(1)} %get-tuple-element.28), channel_id=1, source_target_pairs={{0,4},{1,5},{2,6},{3,7},{4,0},{5,1},{6,2},{7,3},{8,12},{9,13},{10,... | collective-permute-start | bytes 909320 | tf_op jit(solution)/shard_map/ppermute | solution.py:28
  9.8 13.8 %collective-permute-start.8 = (bf16[32,4736]{1,0:T(8,128)(2,1)S(1)}, bf16[32,4736]{1,0:T(8,128)(2,1)S(1)}, u32[]{:S(2)}, u32[]{:S(2)}) collective-permute-start(bf16[32,4736]{1,0:T(8,128)(2,1)S(1)} %get-tuple-element.29), channel_id=1, source_target_pairs={{0,6},{1,7},{2,4},{3,5},{4,2},{5,3},{6,0},{7,1},{8,14},{9,15},{10,... | collective-permute-start | bytes 909320 | tf_op jit(solution)/shard_map/ppermute | solution.py:28
  9.8 16.4 %collective-permute-start = (bf16[144,896]{1,0:T(8,128)(2,1)S(1)}, bf16[144,896]{1,0:T(8,128)(2,1)S(1)}, u32[]{:S(2)}, u32[]{:S(2)}) collective-permute-start(bf16[144,896]{1,0:T(8,128)(2,1)S(1)} %get-tuple-element.23), channel_id=1, source_target_pairs={{0,8},{8,0},{16,24},{24,16},{1,9},{9,1},{17,25},{25,17},{2,10},{10... | collective-permute-start | bytes 774152 | tf_op jit(solution)/shard_map/ppermute | solution.py:28
  11.8 20.6 %collective-permute-start.1 = (bf16[144,896]{1,0:T(8,128)(2,1)S(1)}, bf16[144,896]{1,0:T(8,128)(2,1)S(1)}, u32[]{:S(2)}, u32[]{:S(2)}) collective-permute-start(bf16[144,896]{1,0:T(8,128)(2,1)S(1)} %get-tuple-element.24), channel_id=1, source_target_pairs={{0,16},{8,24},{16,0},{24,8},{1,17},{9,25},{17,1},{25,9},{2,18},{10... | collective-permute-start | bytes 774152 | tf_op jit(solution)/shard_map/ppermute | solution.py:28
  16.3 16.1 %collective-permute-start.2 = (bf16[144,896]{1,0:T(8,128)(2,1)S(1)}, bf16[144,896]{1,0:T(8,128)(2,1)S(1)}, u32[]{:S(2)}, u32[]{:S(2)}) collective-permute-start(bf16[144,896]{1,0:T(8,128)(2,1)S(1)} %get-tuple-element.25), channel_id=1, source_target_pairs={{0,24},{8,16},{16,8},{24,0},{1,25},{9,17},{17,9},{25,1},{2,26},{10... | collective-permute-start | bytes 774152 | tf_op jit(solution)/shard_map/ppermute | solution.py:28
  20.4 3.1 %copy-start = (bf16[1,3584,1024]{2,1,0:T(8,128)(2,1)S(1)}, bf16[1,3584,1024]{2,1,0:T(8,128)(2,1)}, u32[]{:S(2)}) copy-start(bf16[1,3584,1024]{2,1,0:T(8,128)(2,1)} %weight_ref.5) | copy-start | bytes 22020100
  23.5 10.5 %copy-start.1 = (bf16[1,3584,1024]{2,1,0:T(8,128)(2,1)S(1)}, bf16[1,3584,1024]{2,1,0:T(8,128)(2,1)}, u32[]{:S(2)}) copy-start(bf16[1,3584,1024]{2,1,0:T(8,128)(2,1)} %weight_ref.5) | copy-start | bytes 22020100
  23.5 14.9 %collective-permute-start.9 = (bf16[32,4736]{1,0:T(8,128)(2,1)S(1)}, bf16[32,4736]{1,0:T(8,128)(2,1)S(1)}, u32[]{:S(2)}, u32[]{:S(2)}) collective-permute-start(bf16[32,4736]{1,0:T(8,128)(2,1)S(1)} %hold.4), channel_id=1, source_target_pairs={{0,1},{1,0},{2,3},{3,2},{4,5},{5,4},{6,7},{7,6},{8,9},{9,8},{10,11... | collective-permute-start | bytes 909320 | tf_op jit(solution)/shard_map/ppermute | solution.py:28
  23.6 14.8 %collective-permute-start.12 = (bf16[32,4736]{1,0:T(8,128)(2,1)S(1)}, bf16[32,4736]{1,0:T(8,128)(2,1)S(1)}, u32[]{:S(2)}, u32[]{:S(2)}) collective-permute-start(bf16[32,4736]{1,0:T(8,128)(2,1)S(1)} %hold.7), channel_id=1, source_target_pairs={{0,7},{1,6},{2,5},{3,4},{4,3},{5,2},{6,1},{7,0},{8,15},{9,14},{10,... | collective-permute-start | bytes 909320 | tf_op jit(solution)/shard_map/ppermute | solution.py:28
  26.2 14.4 %collective-permute-start.11 = (bf16[32,4736]{1,0:T(8,128)(2,1)S(1)}, bf16[32,4736]{1,0:T(8,128)(2,1)S(1)}, u32[]{:S(2)}, u32[]{:S(2)}) collective-permute-start(bf16[32,4736]{1,0:T(8,128)(2,1)S(1)} %hold.6), channel_id=1, source_target_pairs={{0,5},{1,4},{2,7},{3,6},{4,1},{5,0},{6,3},{7,2},{8,13},{9,12},{10,... | collective-permute-start | bytes 909320 | tf_op jit(solution)/shard_map/ppermute | solution.py:28
  32.4 9.4 %collective-permute-start.10 = (bf16[32,4736]{1,0:T(8,128)(2,1)S(1)}, bf16[32,4736]{1,0:T(8,128)(2,1)S(1)}, u32[]{:S(2)}, u32[]{:S(2)}) collective-permute-start(bf16[32,4736]{1,0:T(8,128)(2,1)S(1)} %hold.5), channel_id=1, source_target_pairs={{0,3},{1,2},{2,1},{3,0},{4,7},{5,6},{6,5},{7,4},{8,11},{9,10},{10,... | collective-permute-start | bytes 909320 | tf_op jit(solution)/shard_map/ppermute | solution.py:28
  32.4 3.0 %collective-permute-start.3 = (bf16[144,896]{1,0:T(8,128)(2,1)S(1)}, bf16[144,896]{1,0:T(8,128)(2,1)S(1)}, u32[]{:S(2)}, u32[]{:S(2)}) collective-permute-start(bf16[144,896]{1,0:T(8,128)(2,1)S(1)} %collective-permute-done.rest_4_.rest_5_.refs_0_), channel_id=1, source_target_pairs={{0,1},{1,0},{2,3},{3,2},{4,5},{5,4},{6,7},{7,6},{8,9},{9,8},{10,11... | collective-permute-start | bytes 774152 | tf_op jit(solution)/shard_map/ppermute | solution.py:28
  35.4 7.8 %copy-start.4 = (bf16[128,896]{1,0:T(8,128)(2,1)}, bf16[128,896]{1,0:T(8,128)(2,1)S(1)}, u32[]{:S(2)}) copy-start(bf16[128,896]{1,0:T(8,128)(2,1)S(1)} %get-tuple-element.41.refs_0_) | copy-start | bytes 688132
  35.4 17.6 %collective-permute-start.18 = (bf16[128,1024]{1,0:T(8,128)(2,1)S(1)}, bf16[128,1024]{1,0:T(8,128)(2,1)S(1)}, u32[]{:S(2)}, u32[]{:S(2)}) collective-permute-start(bf16[128,1024]{1,0:T(8,128)(2,1)S(1)} %get-tuple-element.35.rest_4_), channel_id=1, source_target_pairs={{0,24},{8,16},{16,8},{24,0},{1,25},{9,17},{17,9},{25,1},{2,26},{10... | collective-permute-start | bytes 786440 | tf_op jit(solution)/shard_map/ppermute | solution.py:28
  43.2 0.7 copy-start.6
  44.6 11.2 %collective-permute-start.19 = (bf16[128,1024]{1,0:T(8,128)(2,1)}, bf16[128,1024]{1,0:T(8,128)(2,1)S(1)}, u32[]{:S(2)}, u32[]{:S(2)}) collective-permute-start(bf16[128,1024]{1,0:T(8,128)(2,1)} %slice.3), channel_id=1, source_target_pairs={{0,24},{8,16},{16,8},{24,0},{1,25},{9,17},{17,9},{25,1},{2,26},{10... | collective-permute-start | bytes 786440 | tf_op jit(solution)/shard_map/ppermute | solution.py:28
  47.6 1.5 %collective-permute-start.4 = (bf16[144,896]{1,0:T(8,128)(2,1)S(1)}, bf16[144,896]{1,0:T(8,128)(2,1)S(1)}, u32[]{:S(2)}, u32[]{:S(2)}) collective-permute-start(bf16[144,896]{1,0:T(8,128)(2,1)S(1)} %collective-permute-done.1.rest_6_.refs_1_), channel_id=1, source_target_pairs={{0,1},{1,0},{2,3},{3,2},{4,5},{5,4},{6,7},{7,6},{8,9},{9,8},{10,11... | collective-permute-start | bytes 774152 | tf_op jit(solution)/shard_map/ppermute | solution.py:28
  47.6 1.9 %collective-permute-start.5 = (bf16[144,896]{1,0:T(8,128)(2,1)S(1)}, bf16[144,896]{1,0:T(8,128)(2,1)S(1)}, u32[]{:S(2)}, u32[]{:S(2)}) collective-permute-start(bf16[144,896]{1,0:T(8,128)(2,1)S(1)} %collective-permute-done.2.rest_7_.refs_2_), channel_id=1, source_target_pairs={{0,1},{1,0},{2,3},{3,2},{4,5},{5,4},{6,7},{7,6},{8,9},{9,8},{10,11... | collective-permute-start | bytes 774152 | tf_op jit(solution)/shard_map/ppermute | solution.py:28
  48.1 26.9 %copy-start.5 = (bf16[128,896]{1,0:T(8,128)(2,1)S(1)}, bf16[128,896]{1,0:T(8,128)(2,1)}, u32[]{:S(2)}) copy-start(bf16[128,896]{1,0:T(8,128)(2,1)} %copy-done.4) | copy-start | bytes 688132
  48.1 26.9 %copy-start.7 = (bf16[128,896]{1,0:T(8,128)(2,1)S(1)}, bf16[128,896]{1,0:T(8,128)(2,1)}, u32[]{:S(2)}) copy-start(bf16[128,896]{1,0:T(8,128)(2,1)} %copy-done.6) | copy-start | bytes 688132
  48.1 27.6 %collective-permute-start.17 = (bf16[256,1024]{1,0:T(8,128)(2,1)S(1)}, bf16[256,1024]{1,0:T(8,128)(2,1)S(1)}, u32[]{:S(2)}, u32[]{:S(2)}) collective-permute-start(bf16[256,1024]{1,0:T(8,128)(2,1)S(1)} %get-tuple-element.43.refs_0_), channel_id=1, source_target_pairs={{0,8},{8,0},{16,24},{24,16},{1,9},{9,1},{17,25},{25,17},{2,10},{10... | collective-permute-start | bytes 1572872 | tf_op jit(solution)/shard_map/ppermute | solution.py:28
  50.8 13.9 %collective-permute-start.13 = (bf16[64,3712]{1,0:T(8,128)(2,1)S(1)}, bf16[64,3712]{1,0:T(8,128)(2,1)S(1)}, u32[]{:S(2)}, u32[]{:S(2)}) collective-permute-start(bf16[64,3712]{1,0:T(8,128)(2,1)S(1)} %get-tuple-element.38), channel_id=1, source_target_pairs={{0,2},{1,3},{2,0},{3,1},{4,6},{5,7},{6,4},{7,5},{8,10},{9,11},{10,... | collective-permute-start | bytes 1425416 | tf_op jit(solution)/shard_map/ppermute | solution.py:28
  51.5 21.9 %collective-permute-start.14 = (bf16[64,3712]{1,0:T(8,128)(2,1)S(1)}, bf16[64,3712]{1,0:T(8,128)(2,1)S(1)}, u32[]{:S(2)}, u32[]{:S(2)}) collective-permute-start(bf16[64,3712]{1,0:T(8,128)(2,1)S(1)} %get-tuple-element.39), channel_id=1, source_target_pairs={{0,4},{1,5},{2,6},{3,7},{4,0},{5,1},{6,2},{7,3},{8,12},{9,13},{10,... | collective-permute-start | bytes 1425416 | tf_op jit(solution)/shard_map/ppermute | solution.py:28
  53.0 21.9 %collective-permute-start.15 = (bf16[64,3712]{1,0:T(8,128)(2,1)S(1)}, bf16[64,3712]{1,0:T(8,128)(2,1)S(1)}, u32[]{:S(2)}, u32[]{:S(2)}) collective-permute-start(bf16[64,3712]{1,0:T(8,128)(2,1)S(1)} %get-tuple-element.40), channel_id=1, source_target_pairs={{0,6},{1,7},{2,4},{3,5},{4,2},{5,3},{6,0},{7,1},{8,14},{9,15},{10,... | collective-permute-start | bytes 1425416 | tf_op jit(solution)/shard_map/ppermute | solution.py:28
  56.1 22.4 %collective-permute-start.20 = (bf16[256,1024]{1,0:T(8,128)(2,1)S(1)}, bf16[256,1024]{1,0:T(8,128)(2,1)S(1)}, u32[]{:S(2)}, u32[]{:S(2)}) collective-permute-start(bf16[256,1024]{1,0:T(8,128)(2,1)S(1)} %maximum_select_fusion), channel_id=1, source_target_pairs={{0,16},{8,0},{16,24},{24,8},{1,17},{9,1},{17,25},{25,9},{2,18},{10... | collective-permute-start | bytes 1572872 | tf_op jit(solution)/shard_map/ppermute | solution.py:296
  75.0 2.3 %collective-permute-start.16 = (bf16[128,1024]{1,0:T(8,128)(2,1)S(1)}, bf16[128,1024]{1,0:T(8,128)(2,1)S(1)}, u32[]{:S(2)}, u32[]{:S(2)}) collective-permute-start(bf16[128,1024]{1,0:T(8,128)(2,1)S(1)} %split.1), channel_id=1, source_target_pairs={{0,1},{1,0},{2,3},{3,2},{4,5},{5,4},{6,7},{7,6},{8,9},{9,8},{10,11... | collective-permute-start | bytes 786440 | tf_op jit(solution)/shard_map/ppermute | solution.py:28
  75.7 1.6 %copy-start.9 = (s32[128,1]{0,1:T(1,128)S(1)}, s32[128,1]{0,1:T(1,128)}, u32[]{:S(2)}) copy-start(s32[128,1]{0,1:T(1,128)} %param.6) | copy-start | bytes 1540

commit v7 on v6

--- a/solution.py
+++ b/solution.py
@@ -261,7 +261,7 @@
     for k in range(2, experts, 2):
         got[k] = swap(placed[k], "expert", k)
     for k in range(3, experts, 2):
-        got[k] = swap(after([placed[k]], got[experts - k + 1 if k > 1 else 2], *([touched] if k == 3 else []))[0], "expert", k)
+        got[k] = swap(after([placed[k]], got[{3: experts - 2, 5: 2, 7: 4}.get(k, 2)], *([touched] if k == 3 else []))[0], "expert", k)
     got[1] = swap(after([placed[1]], got[2])[0], "expert", 1)
     cuts = [swap(cut, "dp", k + 1) for k, cut in enumerate(cuts)]
 

time: 81 us -> 81 us (level)
  no operation moved by 1% of the time
where the time goes in v7:
time: 81 us; the launch traced here: 80.7 us
  starting transfers between devices  36.6 us (45%)
  waiting for transfers between devices  24.3 us (30%)
  Pallas kernels  10.9 us (13%)
  local copies, waits for them, and re-layouts  7.92 us (10%)
  between operations  0.84 us (1%)
    ppermute x20, starting transfers between devices, swap(): return lax.ppermute(value, axis, [(i, i ^ offset) for i in range(count)])  27.9 us
    ppermute x20, waiting for transfers between devices, swap(): return lax.ppermute(value, axis, [(i, i ^ offset) for i in range(count)])  24.3 us
    ppermute x1, starting transfers between devices, on_device(): lax.ppermute(value, 'dp', [(0, 2), (1, 0), (2, 3), (3, 1)])  8.68 us
    unnamed x22, local copies, waits for them, and re-layouts  7.2 us
    pallas_call x2, Pallas kernels, forward(): pl.pallas_call(functools.partial(forward_kernel, (len(blocks), width, inn...  2.7 us
    pallas_call x1, Pallas kernels, on_device(): pl.pallas_call(functools.partial(grad_kernel, 2), out_shape=jax.ShapeDtyp...  2.26 us
  transfers between devices with their start and end apart: 21, of which 9 were waited for; matrix products, arithmetic and copies ran while one was open for 1% of the time, Pallas kernels for 9%

profile of v7, /device:TPU:0, one launch (start us, length us, event | category | flops | bytes accessed | tf_op | source)
XLA Modules:
  0.0 80.7 jit_solution(16095362110799079528)
XLA Ops:
  0.6 1.2 %copy-done.2 = bf16[128,3584]{1,0:T(8,128)(2,1)S(1)} copy-done((bf16[128,3584]{1,0:T(8,128)(2,1)S(1)}, bf16[128,3584]{1,0:T(8,128)(2,1)}, u32[]{:S(2)}) %copy-start.2) | copy-done | bytes 917528
  1.8 0.9 %copy-done.3 = bf16[128,1024]{1,0:T(8,128)(2,1)S(1)} copy-done((bf16[128,1024]{1,0:T(8,128)(2,1)S(1)}, bf16[128,1024]{1,0:T(8,128)(2,1)}, u32[]{:S(2)}) %copy-start.3) | copy-done | bytes 262168
  2.8 0.7 copy-done.8
  3.4 0.7 copy-done.10
  4.1 1.2 %place.1 = (bf16[32,4736]{1,0:T(8,128)(2,1)S(1)}, bf16[32,4736]{1,0:T(8,128)(2,1)S(1)}, bf16[32,4736]{1,0:T(8,128)(2,1)S(1)}, bf16[32,4736]{1,0:T(8,128)(2,1)S(1...) custom-call(s32[1,128]{1,0:T(1,128)S(1)} %bitcast.3, ...), custom_call_target="tpu_custom_call" | custom-call | tf_op jit(solution)/shard_map/place/pallas_call | solution.py:241
  5.3 3.0 %collective-permute-start.6 = (bf16[32,4736]{1,0:T(8,128)(2,1)S(1)}, bf16[32,4736]{1,0:T(8,128)(2,1)S(1)}, u32[]{:S(2)}, u32[]{:S(2)}) collective-permute-start(bf16[32,4736]{1,0:T(8,128)(2,1)S(1)} %get-tuple-element.27), channel_id=1, source_target_pairs={{0,2},{1,3},{2,0},{3,1},{4,6},{5,7},{6,4},{7,5},{8,10},{9,11},{10,... | collective-permute-start | bytes 909320 | tf_op jit(solution)/shard_map/ppermute | solution.py:28
  8.3 1.5 %collective-permute-start.7 = (bf16[32,4736]{1,0:T(8,128)(2,1)S(1)}, bf16[32,4736]{1,0:T(8,128)(2,1)S(1)}, u32[]{:S(2)}, u32[]{:S(2)}) collective-permute-start(bf16[32,4736]{1,0:T(8,128)(2,1)S(1)} %get-tuple-element.28), channel_id=1, source_target_pairs={{0,4},{1,5},{2,6},{3,7},{4,0},{5,1},{6,2},{7,3},{8,12},{9,13},{10,... | collective-permute-start | bytes 909320 | tf_op jit(solution)/shard_map/ppermute | solution.py:28
  9.8 0.0 collective-permute-start.8
  9.8 2.0 %collective-permute-start = (bf16[144,896]{1,0:T(8,128)(2,1)S(1)}, bf16[144,896]{1,0:T(8,128)(2,1)S(1)}, u32[]{:S(2)}, u32[]{:S(2)}) collective-permute-start(bf16[144,896]{1,0:T(8,128)(2,1)S(1)} %get-tuple-element.23), channel_id=1, source_target_pairs={{0,8},{8,0},{16,24},{24,16},{1,9},{9,1},{17,25},{25,17},{2,10},{10... | collective-permute-start | bytes 774152 | tf_op jit(solution)/shard_map/ppermute | solution.py:28
  11.8 2.6 %collective-permute-start.1 = (bf16[144,896]{1,0:T(8,128)(2,1)S(1)}, bf16[144,896]{1,0:T(8,128)(2,1)S(1)}, u32[]{:S(2)}, u32[]{:S(2)}) collective-permute-start(bf16[144,896]{1,0:T(8,128)(2,1)S(1)} %get-tuple-element.24), channel_id=1, source_target_pairs={{0,16},{8,24},{16,0},{24,8},{1,17},{9,25},{17,1},{25,9},{2,18},{10... | collective-permute-start | bytes 774152 | tf_op jit(solution)/shard_map/ppermute | solution.py:28
  14.4 1.8 %collective-permute-done.6.rest_1_.refs_1_ = bf16[32,4736]{1,0:T(8,128)(2,1)S(1)} collective-permute-done((bf16[32,4736]{1,0:T(8,128)(2,1)S(1)}, bf16[32,4736]{1,0:T(8,128)(2,1)S(1)}, u32[]{:S(2)}, u32[]{:S(2)}) %collective-permute-start.6) | collective-permute-done | bytes 303136 | tf_op jit(solution)/shard_map/ppermute | solution.py:28
  16.3 4.2 %collective-permute-start.2 = (bf16[144,896]{1,0:T(8,128)(2,1)S(1)}, bf16[144,896]{1,0:T(8,128)(2,1)S(1)}, u32[]{:S(2)}, u32[]{:S(2)}) collective-permute-start(bf16[144,896]{1,0:T(8,128)(2,1)S(1)} %get-tuple-element.25), channel_id=1, source_target_pairs={{0,24},{8,16},{16,8},{24,0},{1,25},{9,17},{17,9},{25,1},{2,26},{10... | collective-permute-start | bytes 774152 | tf_op jit(solution)/shard_map/ppermute | solution.py:28
  20.4 3.1 %copy-done = bf16[1,3584,1024]{2,1,0:T(8,128)(2,1)S(1)} copy-done((bf16[1,3584,1024]{2,1,0:T(8,128)(2,1)S(1)}, bf16[1,3584,1024]{2,1,0:T(8,128)(2,1)}, u32[]{:S(2)}) %copy-start) | copy-done | bytes 7340056
  23.5 0.0 collective-permute-done.7.rest_2_.refs_1_
  23.5 0.1 collective-permute-start.9
  23.6 0.0 collective-permute-done.8.rest_3_.refs_1_
  23.6 1.6 %collective-permute-start.11 = (bf16[32,4736]{1,0:T(8,128)(2,1)S(1)}, bf16[32,4736]{1,0:T(8,128)(2,1)S(1)}, u32[]{:S(2)}, u32[]{:S(2)}) collective-permute-start(bf16[32,4736]{1,0:T(8,128)(2,1)S(1)} %hold.6), channel_id=1, source_target_pairs={{0,5},{1,4},{2,7},{3,6},{4,1},{5,0},{6,3},{7,2},{8,13},{9,12},{10,... | collective-permute-start | bytes 909320 | tf_op jit(solution)/shard_map/ppermute | solution.py:28
  25.3 1.1 %collective-permute-start.12 = (bf16[32,4736]{1,0:T(8,128)(2,1)S(1)}, bf16[32,4736]{1,0:T(8,128)(2,1)S(1)}, u32[]{:S(2)}, u32[]{:S(2)}) collective-permute-start(bf16[32,4736]{1,0:T(8,128)(2,1)S(1)} %hold.7), channel_id=1, source_target_pairs={{0,7},{1,6},{2,5},{3,4},{4,3},{5,2},{6,1},{7,0},{8,15},{9,14},{10,... | collective-permute-start | bytes 909320 | tf_op jit(solution)/shard_map/ppermute | solution.py:28
  26.4 6.0 %collective-permute-done.1.rest_6_.refs_1_ = bf16[144,896]{1,0:T(8,128)(2,1)S(1)} collective-permute-done((bf16[144,896]{1,0:T(8,128)(2,1)S(1)}, bf16[144,896]{1,0:T(8,128)(2,1)S(1)}, u32[]{:S(2)}, u32[]{:S(2)}) %collective-permute-start.1) | collective-permute-done | bytes 258080 | tf_op jit(solution)/shard_map/ppermute | solution.py:28
  32.4 0.0 collective-permute-start.10
  32.4 1.6 %collective-permute-start.3 = (bf16[144,896]{1,0:T(8,128)(2,1)S(1)}, bf16[144,896]{1,0:T(8,128)(2,1)S(1)}, u32[]{:S(2)}, u32[]{:S(2)}) collective-permute-start(bf16[144,896]{1,0:T(8,128)(2,1)S(1)} %collective-permute-done.rest_4_.rest_5_.refs_0_), channel_id=1, source_target_pairs={{0,1},{1,0},{2,3},{3,2},{4,5},{5,4},{6,7},{7,6},{8,9},{9,8},{10,11... | collective-permute-start | bytes 774152 | tf_op jit(solution)/shard_map/ppermute | solution.py:28
  34.0 1.3 %forward.2 = (bf16[128,1024]{1,0:T(8,128)(2,1)S(1)}, bf16[128,1024]{1,0:T(8,128)(2,1)S(1)}, bf16[128,896]{1,0:T(8,128)(2,1)S(1)}) custom-call(bf16[1,3584,1024]{2,1,0:T(8,128)(2,1)S(1)} %copy-done.1, bf16[32,4736]{1,0:T(8,128)(2,1)S(1)} %get-tuple-element.26.rest_0_.tie, bf16[32,4736]{1,0:T(8,128)(2,1)S(1)} %collective-permute-done.6.rest_1_.refs_1_, ...), custom_call_target="tpu_custom_call" | custom-call | tf_op jit(solution)/shard_map/forward/pallas_call | solution.py:271
  35.4 0.0 copy-start.4
  35.4 3.1 %collective-permute-start.18 = (bf16[128,1024]{1,0:T(8,128)(2,1)S(1)}, bf16[128,1024]{1,0:T(8,128)(2,1)S(1)}, u32[]{:S(2)}, u32[]{:S(2)}) collective-permute-start(bf16[128,1024]{1,0:T(8,128)(2,1)S(1)} %get-tuple-element.35.rest_4_), channel_id=1, source_target_pairs={{0,24},{8,16},{16,8},{24,0},{1,25},{9,17},{17,9},{25,1},{2,26},{10... | collective-permute-start | bytes 786440 | tf_op jit(solution)/shard_map/ppermute | solution.py:28
  38.5 0.7 collective-permute-done.11.rest_2_
  39.1 2.7 %collective-permute-done.10.rest_1_ = bf16[32,4736]{1,0:T(8,128)(2,1)S(1)} collective-permute-done((bf16[32,4736]{1,0:T(8,128)(2,1)S(1)}, bf16[32,4736]{1,0:T(8,128)(2,1)S(1)}, u32[]{:S(2)}, u32[]{:S(2)}) %collective-permute-start.10) | collective-permute-done | bytes 303136 | tf_op jit(solution)/shard_map/ppermute | solution.py:28
  41.9 1.4 %forward.3 = (bf16[128,1024]{1,0:T(8,128)(2,1)S(1)}, bf16[256,1024]{1,0:T(8,128)(2,1)S(1)}, bf16[128,896]{1,0:T(8,128)(2,1)S(1)}) custom-call(bf16[1,3584,1024]{2,1,0:T(8,128)(2,1)S(1)} %copy-done.1, bf16[32,4736]{1,0:T(8,128)(2,1)S(1)} %collective-permute-done.9.rest_0_, bf16[32,4736]{1,0:T(8,128)(2,1)S(1)} %collective-permute-done.10.rest_1_, ...), custom_call_target="tpu_custom_call" | custom-call | tf_op jit(solution)/shard_map/forward/pallas_call | solution.py:271
  43.2 0.7 copy-done.6
  43.9 0.7 slice.3
  44.6 3.0 %collective-permute-start.19 = (bf16[128,1024]{1,0:T(8,128)(2,1)}, bf16[128,1024]{1,0:T(8,128)(2,1)S(1)}, u32[]{:S(2)}, u32[]{:S(2)}) collective-permute-start(bf16[128,1024]{1,0:T(8,128)(2,1)} %slice.3), channel_id=1, source_target_pairs={{0,24},{8,16},{16,8},{24,0},{1,25},{9,17},{17,9},{25,1},{2,26},{10... | collective-permute-start | bytes 786440 | tf_op jit(solution)/shard_map/ppermute | solution.py:28
  47.6 0.5 collective-permute-start.5
  48.1 1.0 %collective-permute-done.4.refs_4_ = bf16[144,896]{1,0:T(8,128)(2,1)S(1)} collective-permute-done((bf16[144,896]{1,0:T(8,128)(2,1)S(1)}, bf16[144,896]{1,0:T(8,128)(2,1)S(1)}, u32[]{:S(2)}, u32[]{:S(2)}) %collective-permute-start.4) | collective-permute-done | bytes 258080 | tf_op jit(solution)/shard_map/ppermute | solution.py:28
  49.1 0.4 collective-permute-done.5.refs_5_
  49.5 1.3 %place_shares.1 = (bf16[64,3712]{1,0:T(8,128)(2,1)S(1)}, bf16[64,3712]{1,0:T(8,128)(2,1)S(1)}, bf16[64,3712]{1,0:T(8,128)(2,1)S(1)}, bf16[64,3712]{1,0:T(8,128)(2,1)S(1)}) custom-call(bf16[144,896]{1,0:T(8,128)(2,1)S(1)} %collective-permute-done.rest_4_.rest_5_.refs_0_, bf16[144,896]{1,0:T(8,128)(2,1)S(1)} %collective-permute-done.1.rest_6_.refs_1_, ...), custom_call_target="tpu_custom_call" | custom-call | tf_op jit(solution)/shard_map/place_shares/pallas_call | solution.py:298
  50.8 0.7 collective-permute-start.13
  51.5 1.5 %collective-permute-start.14 = (bf16[64,3712]{1,0:T(8,128)(2,1)S(1)}, bf16[64,3712]{1,0:T(8,128)(2,1)S(1)}, u32[]{:S(2)}, u32[]{:S(2)}) collective-permute-start(bf16[64,3712]{1,0:T(8,128)(2,1)S(1)} %get-tuple-element.39), channel_id=1, source_target_pairs={{0,4},{1,5},{2,6},{3,7},{4,0},{5,1},{6,2},{7,3},{8,12},{9,13},{10,... | collective-permute-start | bytes 1425416 | tf_op jit(solution)/shard_map/ppermute | solution.py:28
  53.0 1.3 %collective-permute-start.15 = (bf16[64,3712]{1,0:T(8,128)(2,1)S(1)}, bf16[64,3712]{1,0:T(8,128)(2,1)S(1)}, u32[]{:S(2)}, u32[]{:S(2)}) collective-permute-start(bf16[64,3712]{1,0:T(8,128)(2,1)S(1)} %get-tuple-element.40), channel_id=1, source_target_pairs={{0,6},{1,7},{2,4},{3,5},{4,2},{5,3},{6,0},{7,1},{8,14},{9,15},{10,... | collective-permute-start | bytes 1425416 | tf_op jit(solution)/shard_map/ppermute | solution.py:28
  54.4 1.5 %collective-permute-done.19.refs_3_ = bf16[128,1024]{1,0:T(8,128)(2,1)S(1)} collective-permute-done((bf16[128,1024]{1,0:T(8,128)(2,1)}, bf16[128,1024]{1,0:T(8,128)(2,1)S(1)}, u32[]{:S(2)}, u32[]{:S(2)}) %collective-permute-start.19) | collective-permute-done | bytes 262176 | tf_op jit(solution)/shard_map/ppermute | solution.py:28
  55.9 0.2 maximum_select_fusion
  56.1 8.7 %collective-permute-start.20 = (bf16[256,1024]{1,0:T(8,128)(2,1)S(1)}, bf16[256,1024]{1,0:T(8,128)(2,1)S(1)}, u32[]{:S(2)}, u32[]{:S(2)}) collective-permute-start(bf16[256,1024]{1,0:T(8,128)(2,1)S(1)} %maximum_select_fusion), channel_id=1, source_target_pairs={{0,16},{8,0},{16,24},{24,8},{1,17},{9,1},{17,25},{25,9},{2,18},{10... | collective-permute-start | bytes 1572872 | tf_op jit(solution)/shard_map/ppermute | solution.py:296
  64.8 8.7 %collective-permute-done.14.refs_2_.refs_4_ = bf16[64,3712]{1,0:T(8,128)(2,1)S(1)} collective-permute-done((bf16[64,3712]{1,0:T(8,128)(2,1)S(1)}, bf16[64,3712]{1,0:T(8,128)(2,1)S(1)}, u32[]{:S(2)}, u32[]{:S(2)}) %collective-permute-start.14) | collective-permute-done | bytes 475168 | tf_op jit(solution)/shard_map/ppermute | solution.py:28
  73.4 1.5 %collective-permute-done.15.refs_3_.refs_5_ = bf16[64,3712]{1,0:T(8,128)(2,1)S(1)} collective-permute-done((bf16[64,3712]{1,0:T(8,128)(2,1)S(1)}, bf16[64,3712]{1,0:T(8,128)(2,1)S(1)}, u32[]{:S(2)}, u32[]{:S(2)}) %collective-permute-start.15) | collective-permute-done | bytes 475168 | tf_op jit(solution)/shard_map/ppermute | solution.py:28
  75.0 0.1 collective-permute-start.16
  75.1 0.6 turn.1.left_ref
  75.7 0.0 copy-start.9
  75.7 1.6 %sum.1.before_ref = f32[896,1024]{1,0:T(8,128)S(1)} custom-call(bf16[896,1024]{1,0:T(8,128)(2,1)S(1)} %turn.1.left_ref, bf16[256,1024]{1,0:T(8,128)(2,1)S(1)} %get-tuple-element.43.refs_0_, bf16[256,1024]{1,0:T(8,128)(2,1)S(1)} %collective-permute-done.17.refs_1_, bf16[128,1024]{1,0:T(8,128)(2,1)S(1)} %collective-permute-done.18.refs_2_, ...), custom_call_target="tpu_custom_call" | custom-call | tf_op jit(solution)/shard_map/sum/pallas_call | solution.py:334
  77.3 1.2 %unplace.1 = bf16[128,1024]{1,0:T(8,128)(2,1)} custom-call(s32[1,128]{1,0:T(1,128)S(1)} %bitcast.4, bf16[128,1024]{1,0:T(8,128)(2,1)S(1)} %collective-permute-done.16.theirs_ref, bf16[64,3712]{1,0:T(8,128)(2,1)S(1)} %get-tuple-element.37.refs_0_.refs_2_, bf16[64,3712]{1,0:T(8,128)(2,1)S(1)} %collective-permute-done.13.refs_1_.refs_3_, ...), custom_call_target="tpu_custom_call" | custom-call | tf_op jit(solution)/shard_map/unplace/pallas_call | solution.py:315
  78.5 2.3 %grad.1 = f32[896,1024]{1,0:T(8,128)} custom-call(bf16[896,1024]{1,0:T(8,128)(2,1)S(1)} %turn.1.left_ref, f32[896,1024]{1,0:T(8,128)S(1)} %sum.1.before_ref, bf16[256,1024]{1,0:T(8,128)(2,1)S(1)} %collective-permute-done.20.refs_0_), custom_call_target="tpu_custom_call" | custom-call | tf_op jit(solution)/shard_map/grad/pallas_call | solution.py:344
  (32 shorter events, 0.1 us)
Async XLA Ops:
  0.6 1.2 %copy-start.2 = (bf16[128,3584]{1,0:T(8,128)(2,1)S(1)}, bf16[128,3584]{1,0:T(8,128)(2,1)}, u32[]{:S(2)}) copy-start(bf16[128,3584]{1,0:T(8,128)(2,1)} %refs_3_.1) | copy-start | bytes 2752516
  1.8 0.9 %copy-start.3 = (bf16[128,1024]{1,0:T(8,128)(2,1)S(1)}, bf16[128,1024]{1,0:T(8,128)(2,1)}, u32[]{:S(2)}) copy-start(bf16[128,1024]{1,0:T(8,128)(2,1)} %refs_2_.1) | copy-start | bytes 786436
  2.8 0.7 copy-start.8
  3.4 0.7 copy-start.10
  5.3 11.0 %collective-permute-start.6 = (bf16[32,4736]{1,0:T(8,128)(2,1)S(1)}, bf16[32,4736]{1,0:T(8,128)(2,1)S(1)}, u32[]{:S(2)}, u32[]{:S(2)}) collective-permute-start(bf16[32,4736]{1,0:T(8,128)(2,1)S(1)} %get-tuple-element.27), channel_id=1, source_target_pairs={{0,2},{1,3},{2,0},{3,1},{4,6},{5,7},{6,4},{7,5},{8,10},{9,11},{10,... | collective-permute-start | bytes 909320 | tf_op jit(solution)/shard_map/ppermute | solution.py:28
  8.3 15.3 %collective-permute-start.7 = (bf16[32,4736]{1,0:T(8,128)(2,1)S(1)}, bf16[32,4736]{1,0:T(8,128)(2,1)S(1)}, u32[]{:S(2)}, u32[]{:S(2)}) collective-permute-start(bf16[32,4736]{1,0:T(8,128)(2,1)S(1)} %get-tuple-element.28), channel_id=1, source_target_pairs={{0,4},{1,5},{2,6},{3,7},{4,0},{5,1},{6,2},{7,3},{8,12},{9,13},{10,... | collective-permute-start | bytes 909320 | tf_op jit(solution)/shard_map/ppermute | solution.py:28
  9.8 13.8 %collective-permute-start.8 = (bf16[32,4736]{1,0:T(8,128)(2,1)S(1)}, bf16[32,4736]{1,0:T(8,128)(2,1)S(1)}, u32[]{:S(2)}, u32[]{:S(2)}) collective-permute-start(bf16[32,4736]{1,0:T(8,128)(2,1)S(1)} %get-tuple-element.29), channel_id=1, source_target_pairs={{0,6},{1,7},{2,4},{3,5},{4,2},{5,3},{6,0},{7,1},{8,14},{9,15},{10,... | collective-permute-start | bytes 909320 | tf_op jit(solution)/shard_map/ppermute | solution.py:28
  9.8 15.5 %collective-permute-start = (bf16[144,896]{1,0:T(8,128)(2,1)S(1)}, bf16[144,896]{1,0:T(8,128)(2,1)S(1)}, u32[]{:S(2)}, u32[]{:S(2)}) collective-permute-start(bf16[144,896]{1,0:T(8,128)(2,1)S(1)} %get-tuple-element.23), channel_id=1, source_target_pairs={{0,8},{8,0},{16,24},{24,16},{1,9},{9,1},{17,25},{25,17},{2,10},{10... | collective-permute-start | bytes 774152 | tf_op jit(solution)/shard_map/ppermute | solution.py:28
  11.8 20.6 %collective-permute-start.1 = (bf16[144,896]{1,0:T(8,128)(2,1)S(1)}, bf16[144,896]{1,0:T(8,128)(2,1)S(1)}, u32[]{:S(2)}, u32[]{:S(2)}) collective-permute-start(bf16[144,896]{1,0:T(8,128)(2,1)S(1)} %get-tuple-element.24), channel_id=1, source_target_pairs={{0,16},{8,24},{16,0},{24,8},{1,17},{9,25},{17,1},{25,9},{2,18},{10... | collective-permute-start | bytes 774152 | tf_op jit(solution)/shard_map/ppermute | solution.py:28
  16.3 16.1 %collective-permute-start.2 = (bf16[144,896]{1,0:T(8,128)(2,1)S(1)}, bf16[144,896]{1,0:T(8,128)(2,1)S(1)}, u32[]{:S(2)}, u32[]{:S(2)}) collective-permute-start(bf16[144,896]{1,0:T(8,128)(2,1)S(1)} %get-tuple-element.25), channel_id=1, source_target_pairs={{0,24},{8,16},{16,8},{24,0},{1,25},{9,17},{17,9},{25,1},{2,26},{10... | collective-permute-start | bytes 774152 | tf_op jit(solution)/shard_map/ppermute | solution.py:28
  20.4 3.1 %copy-start = (bf16[1,3584,1024]{2,1,0:T(8,128)(2,1)S(1)}, bf16[1,3584,1024]{2,1,0:T(8,128)(2,1)}, u32[]{:S(2)}) copy-start(bf16[1,3584,1024]{2,1,0:T(8,128)(2,1)} %weight_ref.5) | copy-start | bytes 22020100
  23.5 10.5 %copy-start.1 = (bf16[1,3584,1024]{2,1,0:T(8,128)(2,1)S(1)}, bf16[1,3584,1024]{2,1,0:T(8,128)(2,1)}, u32[]{:S(2)}) copy-start(bf16[1,3584,1024]{2,1,0:T(8,128)(2,1)} %weight_ref.5) | copy-start | bytes 22020100
  23.5 14.9 %collective-permute-start.9 = (bf16[32,4736]{1,0:T(8,128)(2,1)S(1)}, bf16[32,4736]{1,0:T(8,128)(2,1)S(1)}, u32[]{:S(2)}, u32[]{:S(2)}) collective-permute-start(bf16[32,4736]{1,0:T(8,128)(2,1)S(1)} %hold.4), channel_id=1, source_target_pairs={{0,1},{1,0},{2,3},{3,2},{4,5},{5,4},{6,7},{7,6},{8,9},{9,8},{10,11... | collective-permute-start | bytes 909320 | tf_op jit(solution)/shard_map/ppermute | solution.py:28
  23.6 15.5 %collective-permute-start.11 = (bf16[32,4736]{1,0:T(8,128)(2,1)S(1)}, bf16[32,4736]{1,0:T(8,128)(2,1)S(1)}, u32[]{:S(2)}, u32[]{:S(2)}) collective-permute-start(bf16[32,4736]{1,0:T(8,128)(2,1)S(1)} %hold.6), channel_id=1, source_target_pairs={{0,5},{1,4},{2,7},{3,6},{4,1},{5,0},{6,3},{7,2},{8,13},{9,12},{10,... | collective-permute-start | bytes 909320 | tf_op jit(solution)/shard_map/ppermute | solution.py:28
  25.3 13.9 %collective-permute-start.12 = (bf16[32,4736]{1,0:T(8,128)(2,1)S(1)}, bf16[32,4736]{1,0:T(8,128)(2,1)S(1)}, u32[]{:S(2)}, u32[]{:S(2)}) collective-permute-start(bf16[32,4736]{1,0:T(8,128)(2,1)S(1)} %hold.7), channel_id=1, source_target_pairs={{0,7},{1,6},{2,5},{3,4},{4,3},{5,2},{6,1},{7,0},{8,15},{9,14},{10,... | collective-permute-start | bytes 909320 | tf_op jit(solution)/shard_map/ppermute | solution.py:28
  32.4 9.4 %collective-permute-start.10 = (bf16[32,4736]{1,0:T(8,128)(2,1)S(1)}, bf16[32,4736]{1,0:T(8,128)(2,1)S(1)}, u32[]{:S(2)}, u32[]{:S(2)}) collective-permute-start(bf16[32,4736]{1,0:T(8,128)(2,1)S(1)} %hold.5), channel_id=1, source_target_pairs={{0,3},{1,2},{2,1},{3,0},{4,7},{5,6},{6,5},{7,4},{8,11},{9,10},{10,... | collective-permute-start | bytes 909320 | tf_op jit(solution)/shard_map/ppermute | solution.py:28
  32.4 3.0 %collective-permute-start.3 = (bf16[144,896]{1,0:T(8,128)(2,1)S(1)}, bf16[144,896]{1,0:T(8,128)(2,1)S(1)}, u32[]{:S(2)}, u32[]{:S(2)}) collective-permute-start(bf16[144,896]{1,0:T(8,128)(2,1)S(1)} %collective-permute-done.rest_4_.rest_5_.refs_0_), channel_id=1, source_target_pairs={{0,1},{1,0},{2,3},{3,2},{4,5},{5,4},{6,7},{7,6},{8,9},{9,8},{10,11... | collective-permute-start | bytes 774152 | tf_op jit(solution)/shard_map/ppermute | solution.py:28
  35.4 7.8 %copy-start.4 = (bf16[128,896]{1,0:T(8,128)(2,1)}, bf16[128,896]{1,0:T(8,128)(2,1)S(1)}, u32[]{:S(2)}) copy-start(bf16[128,896]{1,0:T(8,128)(2,1)S(1)} %get-tuple-element.41.refs_0_) | copy-start | bytes 688132
  35.4 17.6 %collective-permute-start.18 = (bf16[128,1024]{1,0:T(8,128)(2,1)S(1)}, bf16[128,1024]{1,0:T(8,128)(2,1)S(1)}, u32[]{:S(2)}, u32[]{:S(2)}) collective-permute-start(bf16[128,1024]{1,0:T(8,128)(2,1)S(1)} %get-tuple-element.35.rest_4_), channel_id=1, source_target_pairs={{0,24},{8,16},{16,8},{24,0},{1,25},{9,17},{17,9},{25,1},{2,26},{10... | collective-permute-start | bytes 786440 | tf_op jit(solution)/shard_map/ppermute | solution.py:28
  43.2 0.7 copy-start.6
  44.6 11.2 %collective-permute-start.19 = (bf16[128,1024]{1,0:T(8,128)(2,1)}, bf16[128,1024]{1,0:T(8,128)(2,1)S(1)}, u32[]{:S(2)}, u32[]{:S(2)}) collective-permute-start(bf16[128,1024]{1,0:T(8,128)(2,1)} %slice.3), channel_id=1, source_target_pairs={{0,24},{8,16},{16,8},{24,0},{1,25},{9,17},{17,9},{25,1},{2,26},{10... | collective-permute-start | bytes 786440 | tf_op jit(solution)/shard_map/ppermute | solution.py:28
  47.6 1.5 %collective-permute-start.4 = (bf16[144,896]{1,0:T(8,128)(2,1)S(1)}, bf16[144,896]{1,0:T(8,128)(2,1)S(1)}, u32[]{:S(2)}, u32[]{:S(2)}) collective-permute-start(bf16[144,896]{1,0:T(8,128)(2,1)S(1)} %collective-permute-done.1.rest_6_.refs_1_), channel_id=1, source_target_pairs={{0,1},{1,0},{2,3},{3,2},{4,5},{5,4},{6,7},{7,6},{8,9},{9,8},{10,11... | collective-permute-start | bytes 774152 | tf_op jit(solution)/shard_map/ppermute | solution.py:28
  47.6 1.9 %collective-permute-start.5 = (bf16[144,896]{1,0:T(8,128)(2,1)S(1)}, bf16[144,896]{1,0:T(8,128)(2,1)S(1)}, u32[]{:S(2)}, u32[]{:S(2)}) collective-permute-start(bf16[144,896]{1,0:T(8,128)(2,1)S(1)} %collective-permute-done.2.rest_7_.refs_2_), channel_id=1, source_target_pairs={{0,1},{1,0},{2,3},{3,2},{4,5},{5,4},{6,7},{7,6},{8,9},{9,8},{10,11... | collective-permute-start | bytes 774152 | tf_op jit(solution)/shard_map/ppermute | solution.py:28
  48.1 26.9 %copy-start.5 = (bf16[128,896]{1,0:T(8,128)(2,1)S(1)}, bf16[128,896]{1,0:T(8,128)(2,1)}, u32[]{:S(2)}) copy-start(bf16[128,896]{1,0:T(8,128)(2,1)} %copy-done.4) | copy-start | bytes 688132
  48.1 26.9 %copy-start.7 = (bf16[128,896]{1,0:T(8,128)(2,1)S(1)}, bf16[128,896]{1,0:T(8,128)(2,1)}, u32[]{:S(2)}) copy-start(bf16[128,896]{1,0:T(8,128)(2,1)} %copy-done.6) | copy-start | bytes 688132
  48.1 27.6 %collective-permute-start.17 = (bf16[256,1024]{1,0:T(8,128)(2,1)S(1)}, bf16[256,1024]{1,0:T(8,128)(2,1)S(1)}, u32[]{:S(2)}, u32[]{:S(2)}) collective-permute-start(bf16[256,1024]{1,0:T(8,128)(2,1)S(1)} %get-tuple-element.43.refs_0_), channel_id=1, source_target_pairs={{0,8},{8,0},{16,24},{24,16},{1,9},{9,1},{17,25},{25,17},{2,10},{10... | collective-permute-start | bytes 1572872 | tf_op jit(solution)/shard_map/ppermute | solution.py:28
  50.8 13.9 %collective-permute-start.13 = (bf16[64,3712]{1,0:T(8,128)(2,1)S(1)}, bf16[64,3712]{1,0:T(8,128)(2,1)S(1)}, u32[]{:S(2)}, u32[]{:S(2)}) collective-permute-start(bf16[64,3712]{1,0:T(8,128)(2,1)S(1)} %get-tuple-element.38), channel_id=1, source_target_pairs={{0,2},{1,3},{2,0},{3,1},{4,6},{5,7},{6,4},{7,5},{8,10},{9,11},{10,... | collective-permute-start | bytes 1425416 | tf_op jit(solution)/shard_map/ppermute | solution.py:28
  51.5 21.9 %collective-permute-start.14 = (bf16[64,3712]{1,0:T(8,128)(2,1)S(1)}, bf16[64,3712]{1,0:T(8,128)(2,1)S(1)}, u32[]{:S(2)}, u32[]{:S(2)}) collective-permute-start(bf16[64,3712]{1,0:T(8,128)(2,1)S(1)} %get-tuple-element.39), channel_id=1, source_target_pairs={{0,4},{1,5},{2,6},{3,7},{4,0},{5,1},{6,2},{7,3},{8,12},{9,13},{10,... | collective-permute-start | bytes 1425416 | tf_op jit(solution)/shard_map/ppermute | solution.py:28
  53.0 21.9 %collective-permute-start.15 = (bf16[64,3712]{1,0:T(8,128)(2,1)S(1)}, bf16[64,3712]{1,0:T(8,128)(2,1)S(1)}, u32[]{:S(2)}, u32[]{:S(2)}) collective-permute-start(bf16[64,3712]{1,0:T(8,128)(2,1)S(1)} %get-tuple-element.40), channel_id=1, source_target_pairs={{0,6},{1,7},{2,4},{3,5},{4,2},{5,3},{6,0},{7,1},{8,14},{9,15},{10,... | collective-permute-start | bytes 1425416 | tf_op jit(solution)/shard_map/ppermute | solution.py:28
  56.1 22.4 %collective-permute-start.20 = (bf16[256,1024]{1,0:T(8,128)(2,1)S(1)}, bf16[256,1024]{1,0:T(8,128)(2,1)S(1)}, u32[]{:S(2)}, u32[]{:S(2)}) collective-permute-start(bf16[256,1024]{1,0:T(8,128)(2,1)S(1)} %maximum_select_fusion), channel_id=1, source_target_pairs={{0,16},{8,0},{16,24},{24,8},{1,17},{9,1},{17,25},{25,9},{2,18},{10... | collective-permute-start | bytes 1572872 | tf_op jit(solution)/shard_map/ppermute | solution.py:296
  75.0 2.3 %collective-permute-start.16 = (bf16[128,1024]{1,0:T(8,128)(2,1)S(1)}, bf16[128,1024]{1,0:T(8,128)(2,1)S(1)}, u32[]{:S(2)}, u32[]{:S(2)}) collective-permute-start(bf16[128,1024]{1,0:T(8,128)(2,1)S(1)} %split.1), channel_id=1, source_target_pairs={{0,1},{1,0},{2,3},{3,2},{4,5},{5,4},{6,7},{7,6},{8,9},{9,8},{10,11... | collective-permute-start | bytes 786440 | tf_op jit(solution)/shard_map/ppermute | solution.py:28
  75.7 1.6 %copy-start.9 = (s32[128,1]{0,1:T(1,128)S(1)}, s32[128,1]{0,1:T(1,128)}, u32[]{:S(2)}) copy-start(s32[128,1]{0,1:T(1,128)} %param.6) | copy-start | bytes 1540
